TPU v7x, 128 devices: a whole 4x4x4 slice. The times are simulated.
128 devices in a mesh: gx: 2 (over y_hi), gy: 16 (over y_lo, x, core), gz: 4 (over z).
Axes of the slice: x: 4, y: 4 (y_hi: 2, y_lo: 2; y = y_hi * 2 + y_lo), z: 4, core: 2. Of those that a mesh axis runs over, the one named last changes fastest.
Arguments:
- magnetic: float32 [8, 3, 16, 256, 512], P(None, None, 'gx', 'gy', 'gz'), may hold values from -6 to 6
- velocity: float32 [3, 16, 256, 512], P(None, 'gx', 'gy', 'gz'), may hold values from -6 to 6
- shear_shift: int32 [2], replicated, may hold values from 0 to 255
- freq_index: int32 [2], replicated, may hold values from 1 to 5
Outputs:
- section_rate: float32 [8, 3, 16, 256, 512], P(None, None, 'gx', 'gy', 'gz')
- advanced: float32 [8, 3, 16, 256, 512], P(None, None, 'gx', 'gy', 'gz')
Inputs may be any that keep to these rules, and one draw needn't show every extreme that they name: `shear_shift`: element 0 is the azimuthal offset of the left radial boundary, element 1 that of the right one. `freq_index`: wavenumbers in units of 2 pi / 512.
All inputs are finite; a program needn't handle non-finite values.
Results may differ from a plain program's by a relative error of at most 0.00007.
Values sent between devices are 32-bit elements; how exact they have to be, the bound alone decides.
No kernel may reach another device: no remote copies, remote signals or barrier semaphores. Data moves between devices by JAX's collectives and lax.ppermute only.
A program may use at most 128 MiB of HBM per device.

v0:
```python
import math

import jax
import jax.numpy as jnp
from jax import lax
from jax.sharding import PartitionSpec as P

SHEAR_RATE = 1.5
TIME_STEP = 0.2
DIFFUSIVITY = 0.1
SECTION_WEIGHT = 1.0 / 3.0


def from_behind(value, axis, steps):
    count = lax.axis_size(axis)
    pairs = [(source, (source + steps) % count) for source in range(count)]
    return lax.ppermute(value, axis, pairs)


def from_partner(block, axis, stride):
    count = lax.axis_size(axis)
    route = []
    for low in range(count):
        high = low | 1 << stride
        if high != low and high < count:
            route += [(low, high), (high, low)]
    return lax.ppermute(block, axis, route)


def padded_2(value, sides, width):
    for axis, dim in sides:
        size, length = (lax.axis_size(axis), value.shape[dim])
        up = [(i, (i + 1) % size) for i in range(size)]
        down = [(j, i) for i, j in up]
        last = lax.slice_in_dim(value, length - width, length, axis=dim)
        leading = lax.slice_in_dim(value, 0, width, axis=dim)
        before = lax.ppermute(last, axis, up)
        after = lax.ppermute(leading, axis, down)
        value = jnp.concatenate([before, value, after], axis=dim)
    return value


def test_fields(freq_index, positions, total_z):
    phase = 2.0 * math.pi * freq_index.astype(jnp.float32)[:, None] * positions[None, :] / total_z
    cosine = jnp.cos(phase)
    sine = jnp.sin(phase)
    zeros = jnp.zeros_like(cosine)
    table = jnp.stack(
        [
            jnp.stack([cosine, zeros, zeros], 1),
            jnp.stack([sine, zeros, zeros], 1),
            jnp.stack([zeros, cosine, zeros], 1),
            jnp.stack([zeros, sine, zeros], 1),
        ],
        1,
    )
    return table.reshape(4 * freq_index.shape[0], 3, positions.shape[0])


def motive_force(velocity, magnetic, waves):
    combined = magnetic + waves[:, :, None, None, :]
    flow_x, flow_y, flow_z = (velocity[0], velocity[1], velocity[2])
    full_x, full_y, full_z = (combined[:, 0], combined[:, 1], combined[:, 2])
    return jnp.stack(
        [
            flow_y * full_z - flow_z * full_y,
            flow_z * full_x - flow_x * full_z,
            flow_x * full_y - flow_y * full_x,
        ],
        1,
    )


def first_diff(padded, along, length):

    def window(offset_cells):
        return lax.slice_in_dim(padded, 3 + offset_cells, 3 + offset_cells + length, axis=along)

    return (
        45.0 * (window(1) - window(-1)) - 9.0 * (window(2) - window(-2)) + (window(3) - window(-3))
    ) / 60.0


def second_diff(padded, along, length):

    def window(offset_cells):
        return lax.slice_in_dim(padded, 3 + offset_cells, 3 + offset_cells + length, axis=along)

    return (
        2.0 * (window(3) + window(-3))
        - 27.0 * (window(2) + window(-2))
        + 270.0 * (window(1) + window(-1))
        - 490.0 * window(0)
    ) / 180.0


def section_rate_of(grad_x, grad_y, grad_z, laplace, magnetic, waves):
    curl_x = grad_y[:, 2] - grad_z[:, 1]
    curl_y = grad_z[:, 0] - grad_x[:, 2]
    curl_z = grad_x[:, 1] - grad_y[:, 0]
    stretch = -SHEAR_RATE * (magnetic[:, 0] + waves[:, 0, None, None, :])
    return TIME_STEP * jnp.stack(
        [
            curl_x + DIFFUSIVITY * laplace[:, 0],
            curl_y + DIFFUSIVITY * laplace[:, 1] + stretch,
            curl_z + DIFFUSIVITY * laplace[:, 2],
        ],
        1,
    )


def offset_rows(planes, amount):
    cells_y = planes.shape[3]
    owner_step = amount // cells_y
    offset = amount % cells_y
    current = planes
    for level in range(lax.axis_size("gy").bit_length() - 1):
        moved_rows = from_behind(current, "gy", -(1 << level))
        current = jnp.where(owner_step // (1 << level) % 2 == 1, moved_rows, current)
    following = from_behind(current, "gy", -1)
    joined = jnp.concatenate([current, following], axis=3)
    return lax.dynamic_slice_in_dim(joined, offset, cells_y, axis=3)


def shear_extend(stacked, shear_shift, total_y):
    cells_x = stacked.shape[2]
    on_left = lax.axis_index("gx") == 0
    low_planes = stacked[:, :, :3]
    high_planes = stacked[:, :, cells_x - 3 :]
    facing = jnp.where(on_left, high_planes, low_planes)
    outer_planes = jnp.where(on_left, low_planes, high_planes)
    amount = jnp.where(on_left, (total_y - shear_shift[1]) % total_y, shear_shift[0])
    moved_rows = offset_rows(outer_planes, amount)
    received = from_partner(jnp.concatenate([facing, moved_rows], 2), "gx", 0)
    from_facing = received[:, :, :3]
    from_moved = received[:, :, 3:]
    left_ghost = jnp.where(on_left, from_moved, from_facing)
    right_ghost = jnp.where(on_left, from_facing, from_moved)
    return jnp.concatenate([left_ghost, stacked, right_ghost], 2)


def periodic_faces(stacked):
    return padded_2(stacked, (("gy", 3), ("gz", 4)), 3)


def spectral_tables(total_y):
    modes = jnp.arange(total_y)
    products = modes[:, None] * modes[None, :] % total_y
    angles = 2.0 * math.pi / total_y * products.astype(jnp.float32)
    cos_table = jnp.cos(angles)
    sin_table = jnp.sin(angles)
    forward = jnp.concatenate([cos_table, -sin_table], 1)
    inverse = jnp.concatenate([cos_table, -sin_table], 0) / total_y
    signed_modes = jnp.where(modes <= total_y // 2, modes, modes - total_y).astype(jnp.float32)
    return (forward, inverse, signed_modes)


def spectral_shift(pencil, sigma_rows, tables, total_y):
    forward, inverse, signed_modes = tables
    angles = 2.0 * math.pi / total_y * sigma_rows[:, None] * signed_modes[None, :]
    cos_phase = jnp.cos(angles)[:, :, None]
    sin_phase = jnp.sin(angles)[:, :, None]
    spectrum = jnp.einsum("ryz,yk->rkz", pencil, forward, precision=lax.Precision.HIGHEST)
    real_part = spectrum[:, :total_y]
    imag_part = spectrum[:, total_y:]
    rotated = jnp.concatenate(
        [
            real_part * cos_phase + imag_part * sin_phase,
            imag_part * cos_phase - real_part * sin_phase,
        ],
        1,
    )
    return jnp.einsum("rkz,ky->ryz", rotated, inverse, precision=lax.Precision.HIGHEST)


def on_device(magnetic, velocity, shear_shift, freq_index):
    problems, comps, cells_x, cells_y, cells_z = magnetic.shape
    total_x = cells_x * lax.axis_size("gx")
    total_y = cells_y * lax.axis_size("gy")
    total_z = cells_z * lax.axis_size("gz")
    z_start = lax.axis_index("gz") * cells_z
    test_waves = test_fields(
        freq_index, (z_start + jnp.arange(cells_z)).astype(jnp.float32), total_z
    )
    forcing = motive_force(velocity, magnetic, test_waves)
    stacked = jnp.concatenate([forcing, magnetic], 0)
    radial = shear_extend(stacked, shear_shift, total_y)
    face_ext = periodic_faces(stacked)
    emf_radial = radial[:problems]
    emf_faces = face_ext[:problems]
    field_radial = radial[problems:]
    field_faces = face_ext[problems:]
    grad_x = first_diff(emf_radial, 2, cells_x)
    grad_y = first_diff(emf_faces[:, :, :, :, 3 : 3 + cells_z], 3, cells_y)
    grad_z = first_diff(emf_faces[:, :, :, 3 : 3 + cells_y, :], 4, cells_z)
    laplace = (
        second_diff(field_radial, 2, cells_x)
        + second_diff(field_faces[:, :, :, :, 3 : 3 + cells_z], 3, cells_y)
        + second_diff(field_faces[:, :, :, 3 : 3 + cells_y, :], 4, cells_z)
    )
    section_rates = section_rate_of(grad_x, grad_y, grad_z, laplace, magnetic, test_waves)
    sectioned = magnetic + SECTION_WEIGHT * section_rates
    row_block = sectioned.reshape(problems * comps * cells_x, cells_y, cells_z)
    tables = spectral_tables(total_y)
    pencil = lax.all_to_all(row_block, "gy", split_axis=2, concat_axis=1, tiled=True)
    x_global = lax.axis_index("gx") * cells_x + jnp.arange(row_block.shape[0]) % cells_x
    turned = spectral_shift(
        pencil,
        -SHEAR_RATE
        * SECTION_WEIGHT
        * TIME_STEP
        * (x_global.astype(jnp.float32) + 0.5 - total_x / 2.0),
        tables,
        total_y,
    )
    returned = lax.all_to_all(turned, "gy", split_axis=1, concat_axis=2, tiled=True)
    advanced = returned.reshape(magnetic.shape)
    return (section_rates, advanced)


def solution(mesh):
    return jax.shard_map(
        on_device,
        mesh=mesh,
        in_specs=(P(None, None, "gx", "gy", "gz"), P(None, "gx", "gy", "gz"), P(), P()),
        out_specs=(P(None, None, "gx", "gy", "gz"), P(None, None, "gx", "gy", "gz")),
        check_vma=False,
    )
```

profile of v0, /device:TPU:1, one launch (start us, length us, event | category | flops | bytes accessed | tf_op | source)
XLA Modules:
  0.0 342.9 jit_solution(2709438559624552644)
XLA Ops:
  2.4 2.7 broadcast_add_fusion
  13.0 13.4 %collective-permute-done.4 = f32[16,3,3,16,128]{4,3,2,1,0:T(8,128)} collective-permute-done((f32[16,3,3,16,128]{4,3,2,1,0:T(8,128)}, f32[16,3,3,16,128]{4,3,2,1,0:T(8,128)}, u32[]{:S(2)}, u32[]{:S(2)}) %collective-permute-start.4) | collective-permute-done | bytes 1179680 | tf_op jit(solution)/shard_map/ppermute | solution.py:17
  26.4 2.4 broadcast_select_fusion
  28.8 5.6 %collective-permute-start.5 = (f32[16,3,3,16,128]{4,3,2,1,0:T(8,128)}, f32[16,3,3,16,128]{4,3,2,1,0:T(8,128)}, u32[]{:S(2)}, u32[]{:S(2)}) collective-permute-start(f32[16,3,3,16,128]{4,3,2,1,0:T(8,128)} %broadcast_select_fusion), channel_id=1, source_target_pairs={{0,56},{4,60},{8,0},{12,4},{16,8},{20,12},{24,16},{28,20},{32,24},... | collective-permute-start | bytes 3538952 | tf_op jit(solution)/shard_map/ppermute | solution.py:17
  34.4 23.5 %collective-permute-done.5 = f32[16,3,3,16,128]{4,3,2,1,0:T(8,128)} collective-permute-done((f32[16,3,3,16,128]{4,3,2,1,0:T(8,128)}, f32[16,3,3,16,128]{4,3,2,1,0:T(8,128)}, u32[]{:S(2)}, u32[]{:S(2)}) %collective-permute-start.5) | collective-permute-done | bytes 1179680 | tf_op jit(solution)/shard_map/ppermute | solution.py:17
  57.9 2.4 broadcast_select_fusion.1
  62.2 27.8 %collective-permute-done.6 = f32[16,3,3,16,128]{4,3,2,1,0:T(8,128)} collective-permute-done((f32[16,3,3,16,128]{4,3,2,1,0:T(8,128)}, f32[16,3,3,16,128]{4,3,2,1,0:T(8,128)}, u32[]{:S(2)}, u32[]{:S(2)}) %collective-permute-start.6) | collective-permute-done | bytes 1179680 | tf_op jit(solution)/shard_map/ppermute | solution.py:17
  90.0 2.4 broadcast_select_fusion.2
  96.5 29.7 %collective-permute-done.7 = f32[16,3,3,16,128]{4,3,2,1,0:T(8,128)} collective-permute-done((f32[16,3,3,16,128]{4,3,2,1,0:T(8,128)}, f32[16,3,3,16,128]{4,3,2,1,0:T(8,128)}, u32[]{:S(2)}, u32[]{:S(2)}) %collective-permute-start.7) | collective-permute-done | bytes 1179680 | tf_op jit(solution)/shard_map/ppermute | solution.py:17
  126.2 2.4 broadcast_select_fusion.3
  134.0 5.3 %fusion.78 = (f32[16,3,8,22,3]{4,3,2,1,0:T(8,128)}, f32[16,3,8,22,3]{4,3,2,1,0:T(8,128)}) fusion(f32[16,3,8,22,128]{4,3,2,1,0:T(8,128)S(1)} %pad_maximum_fusion.2), kind=kLoop, calls=%fused_computation.146 | loop fusion | bytes 405504 | tf_op jit(solution)/shard_map/slice | solution.py:36
  139.3 4.8 %copy.62 = f32[16,3,8,22,3]{3,2,4,1,0:T(8,128)} copy(f32[16,3,8,22,3]{4,3,2,1,0:T(8,128)} %get-tuple-element.12) | data formatting | bytes 202752 | tf_op jit(solution)/shard_map/slice | solution.py:36
  144.1 3.8 %collective-permute-start.2 = (f32[16,3,8,22,3]{3,2,4,1,0:T(8,128)}, f32[16,3,8,22,3]{3,2,4,1,0:T(8,128)}, u32[]{:S(2)}, u32[]{:S(2)}) collective-permute-start(f32[16,3,8,22,3]{3,2,4,1,0:T(8,128)} %copy.62), channel_id=1, source_target_pairs={{1,0},{2,1},{3,2},{0,3},{5,4},{6,5},{7,6},{4,7},{9,8},{10,9},{11,1... | collective-permute-start | bytes 304136 | tf_op jit(solution)/shard_map/ppermute | solution.py:38
  147.9 4.9 %copy.64 = f32[16,3,8,22,3]{3,2,4,1,0:T(8,128)} copy(f32[16,3,8,22,3]{4,3,2,1,0:T(8,128)} %get-tuple-element.13) | data formatting | bytes 202752 | tf_op jit(solution)/shard_map/slice | solution.py:35
  156.4 2.4 collective-permute-start.9
  158.8 4.4 %pad_maximum_fusion.1 = (f32[16,3,8,19,128]{4,3,2,1,0:T(8,128)}, f32[16,3,8,19,128]{4,3,2,1,0:T(8,128)}) fusion(f32[16,3,8,3,128]{4,3,2,1,0:T(4,128)S(1)} %copy-done.4, f32[8,3,8,16,128]{4,3,2,1,0:T(8,128)S(1)} %copy-done, f32[8,1,8,16,128]{4,3,2,1,0:T(8,128)S(1)} %get-tuple-element.31, f32[8,1,8,16,128]{4,3,2,1,0:T(8,128)S(1)} %get-tuple-element.30, ...), kind=kLoop, calls=%fused_computation.2 | loop fusion | flops 7471104 | bytes 11796480 | tf_op jit(solution)/shard_map/concatenate | solution.py:39
  163.2 4.8 %copy.63 = f32[16,3,8,22,3]{4,3,2,1,0:T(8,128)} copy(f32[16,3,8,22,3]{3,2,4,1,0:T(8,128)} %collective-permute-done.2) | data formatting | bytes 202752 | tf_op jit(solution)/shard_map/ppermute | solution.py:38
  168.0 4.9 %copy.65 = f32[16,3,8,22,3]{4,3,2,1,0:T(8,128)} copy(f32[16,3,8,22,3]{3,2,4,1,0:T(8,128)} %collective-permute-done.3) | data formatting | bytes 202752 | tf_op jit(solution)/shard_map/ppermute | solution.py:37
  172.9 14.4 %pad_maximum_fusion = (f32[16,3,8,22,131]{4,3,2,1,0:T(8,128)}, f32[16,3,8,22,131]{4,3,2,1,0:T(8,128)}) fusion(f32[16,3,8,22,3]{4,3,2,1,0:T(8,128)} %copy.63, f32[16,3,8,3,128]{4,3,2,1,0:T(4,128)} %copy-done.3, f32[8,3,8,16,128]{4,3,2,1,0:T(8,128)S(1)} %copy-done, f32[8,1,8,16,128]{4,3,2,1,0:T(8,128)S(1)} %get-tuple-element.31, ...), kind=kLoop, calls=%fused_computation | loop fusion | flops 13280256 | bytes 13381632 | tf_op jit(solution)/shard_map/concatenate | solution.py:39
  187.3 11.9 %fusion.36 = f32[8,3,8,16,128]{4,3,2,1,0:T(8,128)} fusion(f32[16,3,8,22,131]{4,3,2,1,0:T(8,128)} %get-tuple-element.11, f32[16,3,8,22,131]{4,3,2,1,0:T(8,128)} %get-tuple-element.10), kind=kLoop, calls=%fused_computation.58 | loop fusion | flops 3145728 | bytes 11010048 | tf_op jit(solution)/shard_map/div | solution.py:79
  199.2 9.1 %collective-permute-done.9 = f32[16,3,6,16,128]{4,3,2,1,0:T(8,128)} collective-permute-done((f32[16,3,6,16,128]{4,3,2,1,0:T(8,128)}, f32[16,3,6,16,128]{4,3,2,1,0:T(8,128)}, u32[]{:S(2)}, u32[]{:S(2)}) %collective-permute-start.9) | collective-permute-done | bytes 2359328 | tf_op jit(solution)/shard_map/ppermute | solution.py:27
  210.1 3.8 %pad_maximum_fusion.3 = (f32[16,3,11,16,128]{4,3,2,1,0:T(8,128)}, f32[16,3,11,16,128]{4,3,2,1,0:T(8,128)}) fusion(f32[16,3,3,16,128]{4,3,2,1,0:T(8,128)S(1)} %get-tuple-element.27, f32[8,3,8,16,128]{4,3,2,1,0:T(8,128)S(1)} %copy-done, f32[8,1,8,16,128]{4,3,2,1,0:T(8,128)S(1)} %get-tuple-element.31, f32[8,1,8,16,128]{4,3,2,1,0:T(8,128)S(1)} %get-tuple-element.30, ...), kind=kLoop, calls=%fused_computation.5 | loop fusion | flops 8650752 | bytes 14155776 | tf_op jit(solution)/shard_map/concatenate | solution.py:139
  213.9 18.7 %fusion.18 = f32[8,3,8,16,128]{4,3,2,1,0:T(8,128)S(1)} fusion(f32[16,3,8,22,131]{4,3,2,1,0:T(8,128)} %get-tuple-element.11, f32[16,3,8,22,131]{4,3,2,1,0:T(8,128)} %get-tuple-element.10, f32[16,3,8,19,128]{4,3,2,1,0:T(8,128)} %get-tuple-element.24, f32[16,3,8,19,128]{4,3,2,1,0:T(8,128)} %get-tuple-element.23, f32[16,3,11,16,128]{4,3,2,1,0:T(8,128)} %get-tuple-element.20, ...), kind=kLoop, calls=%fused_computation.31 | loop fusion | flops 12189696 | bytes 31457280 | tf_op jit(solution)/shard_map/add | solution.py:197
  232.6 10.0 %fusion.10 = (f32[8,3,8,16,128]{4,3,2,1,0:T(8,128)S(1)}, f32[8,3,8,16,128]{4,3,2,1,0:T(8,128)S(1)}) fusion(f32[16,3,11,16,128]{4,3,2,1,0:T(8,128)} %get-tuple-element.20, f32[16,3,11,16,128]{4,3,2,1,0:T(8,128)} %get-tuple-element.19, f32[16,3,8,19,128]{4,3,2,1,0:T(8,128)} %get-tuple-element.24, f32[16,3,8,19,128]{4,3,2,1,0:T(8,128)} %get-tuple-element.23), kind=kLoop, calls=%fused_computation.20 | loop fusion | flops 6291456 | bytes 22020096 | tf_op jit(solution)/shard_map/div | solution.py:79
  246.5 7.8 %all-to-all-start = ((f32[192,16,128]{0,1,2:T(8,128)}), f32[192,16,128]{0,1,2:T(8,128)}, u32[]{:S(2)}, u32[]{:S(2)}) async-start(f32[192,16,128]{0,1,2:T(8,128)} %copy.66), calls=%async_computation | async-start | bytes 4194304 | tf_op jit(solution)/shard_map/all_to_all | solution.py:205
  256.2 25.5 %all-to-all-done = f32[192,16,128]{0,1,2:T(8,128)} async-done(((f32[192,16,128]{0,1,2:T(8,128)}), f32[192,16,128]{0,1,2:T(8,128)}, u32[]{:S(2)}, u32[]{:S(2)}) %all-to-all-start) | async-done | bytes 1572896 | tf_op jit(solution)/shard_map/all_to_all | solution.py:205
  281.7 3.2 copy.68
  284.9 4.0 %fusion.6 = f32[192,512,8]{1,0,2:T(8,128)S(1)} fusion(f32[192,256,8]{0,2,1:T(8,128)S(1)} %bitcast.42, f32[256,256]{1,0:T(8,128)S(1)} %get-tuple-element.49, f32[256,256]{1,0:T(8,128)S(1)} %get-tuple-element.50), kind=kOutput, calls=%fused_computation.17 | convolution fusion | flops 2416050176 | bytes 5242880 | tf_op jit(solution)/shard_map/ryz,yk->rkz/dot_general | solution.py:163
  289.3 2.7 fusion.45
  294.0 32.3 %all_to_all.33 = f32[192,256,8]{0,2,1:T(8,128)} all-to-all(f32[192,256,8]{0,2,1:T(8,128)} %copy.70), channel_id=1, replica_groups=mesh['gx'=2,'gy'=16,'gz'=4] {'gy'}, dimensions={1} | all-to-all | bytes 3145728 | tf_op jit(solution)/shard_map/all_to_all | solution.py:216
  326.3 8.2 %copy.71 = f32[192,16,16,8]{1,3,2,0:T(8,128)} copy(f32[192,16,16,8]{0,3,1,2:T(8,128)} %bitcast.41) | data formatting | bytes 3145728 | tf_op jit(solution)/shard_map/all_to_all | solution.py:216
  334.5 8.4 %copy.72 = f32[8,3,8,16,128]{4,3,2,1,0:T(8,128)} copy(f32[8,3,8,16,128]{3,4,2,1,0:T(8,128)} %bitcast.40) | data formatting | bytes 3145728
  (63 shorter events, 33.0 us)
Async XLA Ops:
  5.1 1.9 copy-start
  7.2 2.4 copy-start.1
  7.2 3.8 %copy-start.9 = (s32[2]{0:T(128)S(1)}, s32[2]{0:T(128)}, u32[]{:S(2)}) copy-start(s32[2]{0:T(128)} %param.6) | copy-start | bytes 28
  9.6 16.8 %collective-permute-start.4 = (f32[16,3,3,16,128]{4,3,2,1,0:T(8,128)}, f32[16,3,3,16,128]{4,3,2,1,0:T(8,128)}, u32[]{:S(2)}, u32[]{:S(2)}) collective-permute-start(f32[16,3,3,16,128]{4,3,2,1,0:T(8,128)} %get-tuple-element.22), channel_id=1, source_target_pairs={{0,60},{4,0},{8,4},{12,8},{16,12},{20,16},{24,20},{28,24},{32,28},... | collective-permute-start | bytes 3538952 | tf_op jit(solution)/shard_map/ppermute | solution.py:17
  28.8 29.1 %collective-permute-start.5 = (f32[16,3,3,16,128]{4,3,2,1,0:T(8,128)}, f32[16,3,3,16,128]{4,3,2,1,0:T(8,128)}, u32[]{:S(2)}, u32[]{:S(2)}) collective-permute-start(f32[16,3,3,16,128]{4,3,2,1,0:T(8,128)} %broadcast_select_fusion), channel_id=1, source_target_pairs={{0,56},{4,60},{8,0},{12,4},{16,8},{20,12},{24,16},{28,20},{32,24},... | collective-permute-start | bytes 3538952 | tf_op jit(solution)/shard_map/ppermute | solution.py:17
  60.3 29.7 %collective-permute-start.6 = (f32[16,3,3,16,128]{4,3,2,1,0:T(8,128)}, f32[16,3,3,16,128]{4,3,2,1,0:T(8,128)}, u32[]{:S(2)}, u32[]{:S(2)}) collective-permute-start(f32[16,3,3,16,128]{4,3,2,1,0:T(8,128)} %broadcast_select_fusion.1), channel_id=1, source_target_pairs={{0,48},{4,52},{8,56},{12,60},{16,0},{20,4},{24,8},{28,12},{32,16},... | collective-permute-start | bytes 3538952 | tf_op jit(solution)/shard_map/ppermute | solution.py:17
  62.2 30.2 %copy-start.2 = (f32[16,3,8,16,128]{4,3,2,1,0:T(8,128)S(1)}, f32[16,3,8,16,128]{4,3,2,1,0:T(8,128)}, u32[]{:S(2)}) copy-start(f32[16,3,8,16,128]{4,3,2,1,0:T(8,128)} %copy-done.1) | copy-start | bytes 9437188
  92.5 33.7 %collective-permute-start.7 = (f32[16,3,3,16,128]{4,3,2,1,0:T(8,128)}, f32[16,3,3,16,128]{4,3,2,1,0:T(8,128)}, u32[]{:S(2)}, u32[]{:S(2)}) collective-permute-start(f32[16,3,3,16,128]{4,3,2,1,0:T(8,128)} %broadcast_select_fusion.2), channel_id=1, source_target_pairs={{0,32},{4,36},{8,40},{12,44},{16,48},{20,52},{24,56},{28,60},{32,0... | collective-permute-start | bytes 3538952 | tf_op jit(solution)/shard_map/ppermute | solution.py:17
  93.8 36.1 %collective-permute-start = (f32[16,3,8,3,128]{4,2,3,1,0:T(8,128)}, f32[16,3,8,3,128]{4,2,3,1,0:T(8,128)}, u32[]{:S(2)}, u32[]{:S(2)}) collective-permute-start(f32[16,3,8,3,128]{4,2,3,1,0:T(8,128)} %copy.56), channel_id=1, source_target_pairs={{4,0},{8,4},{12,8},{16,12},{20,16},{24,20},{28,24},{32,28},{36,32}... | collective-permute-start | bytes 1769480 | tf_op jit(solution)/shard_map/ppermute | solution.py:38
  95.6 35.6 %collective-permute-start.1 = (f32[16,3,8,3,128]{4,2,3,1,0:T(8,128)}, f32[16,3,8,3,128]{4,2,3,1,0:T(8,128)}, u32[]{:S(2)}, u32[]{:S(2)}) collective-permute-start(f32[16,3,8,3,128]{4,2,3,1,0:T(8,128)} %copy.58), channel_id=1, source_target_pairs={{0,4},{4,8},{8,12},{12,16},{16,20},{20,24},{24,28},{28,32},{32,36}... | collective-permute-start | bytes 1769480 | tf_op jit(solution)/shard_map/ppermute | solution.py:37
  128.6 24.1 %collective-permute-start.8 = (f32[16,3,3,16,128]{4,3,2,1,0:T(8,128)}, f32[16,3,3,16,128]{4,3,2,1,0:T(8,128)}, u32[]{:S(2)}, u32[]{:S(2)}) collective-permute-start(f32[16,3,3,16,128]{4,3,2,1,0:T(8,128)} %broadcast_select_fusion.3), channel_id=1, source_target_pairs={{0,60},{4,0},{8,4},{12,8},{16,12},{20,16},{24,20},{28,24},{32,28},... | collective-permute-start | bytes 3538952 | tf_op jit(solution)/shard_map/ppermute | solution.py:17
  131.2 2.7 copy-start.3
  132.8 1.1 copy-start.5
  144.1 19.1 %collective-permute-start.2 = (f32[16,3,8,22,3]{3,2,4,1,0:T(8,128)}, f32[16,3,8,22,3]{3,2,4,1,0:T(8,128)}, u32[]{:S(2)}, u32[]{:S(2)}) collective-permute-start(f32[16,3,8,22,3]{3,2,4,1,0:T(8,128)} %copy.62), channel_id=1, source_target_pairs={{1,0},{2,1},{3,2},{0,3},{5,4},{6,5},{7,6},{4,7},{9,8},{10,9},{11,1... | collective-permute-start | bytes 304136 | tf_op jit(solution)/shard_map/ppermute | solution.py:38
  152.7 1.9 copy-start.7
  152.7 15.3 %collective-permute-start.3 = (f32[16,3,8,22,3]{3,2,4,1,0:T(8,128)}, f32[16,3,8,22,3]{3,2,4,1,0:T(8,128)}, u32[]{:S(2)}, u32[]{:S(2)}) collective-permute-start(f32[16,3,8,22,3]{3,2,4,1,0:T(8,128)} %copy.64), channel_id=1, source_target_pairs={{0,1},{1,2},{2,3},{3,0},{4,5},{5,6},{6,7},{7,4},{8,9},{9,10},{10,1... | collective-permute-start | bytes 304136 | tf_op jit(solution)/shard_map/ppermute | solution.py:37
  154.6 4.2 %copy-start.4 = (f32[16,3,8,3,128]{4,3,2,1,0:T(4,128)S(1)}, f32[16,3,8,3,128]{4,3,2,1,0:T(4,128)}, u32[]{:S(2)}) copy-start(f32[16,3,8,3,128]{4,3,2,1,0:T(4,128)} %copy-done.3) | copy-start | bytes 1769476
  154.6 4.2 %copy-start.6 = (f32[16,3,8,3,128]{4,3,2,1,0:T(4,128)S(1)}, f32[16,3,8,3,128]{4,3,2,1,0:T(4,128)}, u32[]{:S(2)}) copy-start(f32[16,3,8,3,128]{4,3,2,1,0:T(4,128)} %copy-done.5) | copy-start | bytes 1769476
  156.4 51.8 %collective-permute-start.9 = (f32[16,3,6,16,128]{4,3,2,1,0:T(8,128)}, f32[16,3,6,16,128]{4,3,2,1,0:T(8,128)}, u32[]{:S(2)}, u32[]{:S(2)}) collective-permute-start(f32[16,3,6,16,128]{4,3,2,1,0:T(8,128)} %pad_maximum_fusion.5), channel_id=1, source_target_pairs={{0,64},{64,0},{1,65},{65,1},{2,66},{66,2},{3,67},{67,3},{4,68},{68... | collective-permute-start | bytes 7077896 | tf_op jit(solution)/shard_map/ppermute | solution.py:27
  232.5 10.0 %copy-start.8 = (f32[8,3,8,16,128]{4,3,2,1,0:T(8,128)S(1)}, f32[8,3,8,16,128]{4,3,2,1,0:T(8,128)}, u32[]{:S(2)}) copy-start(f32[8,3,8,16,128]{4,3,2,1,0:T(8,128)} %fusion.36) | copy-start | bytes 4718596
  246.5 35.1 %all-to-all-start = ((f32[192,16,128]{0,1,2:T(8,128)}), f32[192,16,128]{0,1,2:T(8,128)}, u32[]{:S(2)}, u32[]{:S(2)}) async-start(f32[192,16,128]{0,1,2:T(8,128)} %copy.66), calls=%async_computation | async-start | bytes 4194304 | tf_op jit(solution)/shard_map/all_to_all | solution.py:205
where the time goes:
time: 344 us; the launch traced here: 343 us
  waiting for transfers between devices  129 us (38%)
  other arithmetic  90.7 us (26%)
  local copies, waits for them, and re-layouts  56 us (16%)
  blocking collectives  32.3 us (9%)
  starting transfers between devices  25.9 us (8%)
  matrix products  6.7 us (2%)
    ppermute x5, waiting for transfers between devices, from_behind(): return lax.ppermute(value, axis, pairs)  94.4 us
    all_to_all x1, blocking collectives, on_device(): lax.all_to_all(turned, 'gy', split_axis=1, concat_axis=2, tiled=True)  32.3 us
    all_to_all x1, waiting for transfers between devices, on_device(): lax.all_to_all(row_block, 'gy', split_axis=2, concat_axis=1, tiled=True)  25.5 us
    div x2, other arithmetic, first_diff(): (45.0 * (window(1) - window(-1)) - 9.0 * (window(2) - window(-2)) + (wind...  21.9 us
    concatenate x3, other arithmetic, padded_2(): value = jnp.concatenate([before, value, after], axis=dim)  19.8 us
    add x1, other arithmetic, on_device(): second_diff(field_radial, 2, cells_x)  18.7 us
    slice x3, local copies, waits for them, and re-layouts, padded_2(): leading = lax.slice_in_dim(value, 0, width, axis=dim)  11.1 us
    ppermute x5, starting transfers between devices, from_behind(): return lax.ppermute(value, axis, pairs)  10.2 us
  transfers between devices with their start and end apart: 11, of which 6 were waited for; matrix products, arithmetic and copies ran while one was open for 20% of the time, Pallas kernels for 0%

commit v1 on v0

v1 whole, which is shorter than its diff:
```python
import functools
import math

import jax
import jax.numpy as jnp
import ml_dtypes
import numpy as np
from jax import lax
from jax.experimental import pallas as pl
from jax.experimental.pallas import tpu as pltpu
from jax.sharding import PartitionSpec as P

SHEAR_RATE = 1.5
TIME_STEP = 0.2
DIFFUSIVITY = 0.1
SECTION_WEIGHT = 1.0 / 3.0

D1 = [TIME_STEP * w / 60.0 for w in (45.0, -9.0, 1.0)]
D2 = [TIME_STEP * DIFFUSIVITY * w / 180.0 for w in (270.0, -27.0, 2.0)]
D2_CENTRE = -TIME_STEP * DIFFUSIVITY * 490.0 / 180.0
STRETCH = -TIME_STEP * SHEAR_RATE

BF16 = jnp.bfloat16
F32 = jnp.float32


def np_split(value):
    value = np.asarray(value, np.float64)
    high = value.astype(np.float32).astype(ml_dtypes.bfloat16)
    low = (value - high.astype(np.float64)).astype(np.float32).astype(ml_dtypes.bfloat16)
    return high, low


def stencil_1d(first_out, outs, size, centre):
    one = np.zeros((outs, size))
    two = np.zeros((outs, size))
    for row in range(outs):
        at = first_out + row
        for d in (1, 2, 3):
            if 0 <= at + d < size:
                one[row, at + d] += D1[d - 1]
                two[row, at + d] += D2[d - 1]
            if 0 <= at - d < size:
                one[row, at - d] -= D1[d - 1]
                two[row, at - d] += D2[d - 1]
        if 0 <= at < size:
            two[row, at] += centre
    return one, two


def left_weights(cx, cy):
    eye_x, eye_y = np.eye(cx), np.eye(cy)
    x1, x2 = stencil_1d(0, cx, cx, D2_CENTRE)
    y1, y2 = stencil_1d(0, cy, cy, D2_CENTRE)
    xl1, xl2 = stencil_1d(-3, 3, cx, 0.0)
    xh1, xh2 = stencil_1d(cx, 3, cx, 0.0)
    yl1, yl2 = stencil_1d(-3, 3, cy, 0.0)
    yh1, yh2 = stencil_1d(cy, 3, cy, 0.0)

    def face_y(rows):
        return np.einsum("iy,xz->ixzy", rows, eye_x).reshape(3 * cx, cx * cy)

    none_x = np.zeros((3 * cy, cx * cy))
    none_y = np.zeros((3 * cx, cx * cy))
    dx = np.concatenate([np.kron(x1, eye_y), np.kron(xl1, eye_y), np.kron(xh1, eye_y), none_y, none_y])
    dy = np.concatenate([np.kron(eye_x, y1), none_x, none_x, face_y(yl1), face_y(yh1)])
    lap = np.concatenate([
        np.kron(x2, eye_y) + np.kron(eye_x, y2),
        np.kron(xl2, eye_y), np.kron(xh2, eye_y), face_y(yl2), face_y(yh2),
    ])
    out_x = np.concatenate([dy, lap], 1)
    out_y = np.concatenate([-dx, lap], 1)
    out_z = np.concatenate([dx, -dy, lap], 1)
    result = []
    for value in (out_x, out_y, out_z):
        high, low = np_split(value)
        result.append(np.concatenate([high, high, low], 1))
    return result


def right_weights(cz):
    one, two = stencil_1d(0, cz, cz, D2_CENTRE)
    lo1, lo2 = stencil_1d(-3, 3, cz, 0.0)
    hi1, hi2 = stencil_1d(cz, 3, cz, 0.0)
    pad = np.zeros((2, cz))
    face1 = np.concatenate([lo1, hi1, pad])
    face2 = np.concatenate([lo2, hi2, pad])
    mains, faces = [], []
    for main, face in (
        (np.concatenate([-one.T, two.T]), np.concatenate([-face1, face2], 1)),
        (np.concatenate([one.T, two.T]), np.concatenate([face1, face2], 1)),
        (two.T, face2),
    ):
        high, low = np_split(main)
        mains.append(np.concatenate([high, high, low], 0))
        high, low = np_split(face)
        faces.append(np.concatenate([high, high, low], 1))
    return mains, faces


def shift_matrices(total_x, total_y):
    modes = np.arange(total_y // 2 + 1)
    sigma = -SHEAR_RATE * SECTION_WEIGHT * TIME_STEP * (np.arange(total_x) + 0.5 - total_x / 2.0)
    weight = np.full(modes.shape, 2.0)
    weight[0] = 1.0
    away = np.arange(total_y)
    rows = []
    for s in sigma:
        terms = weight[:-1, None] * np.cos(2.0 * np.pi / total_y * modes[:-1, None] * (away[None, :] - s))
        nyquist = np.cos(np.pi * s) * np.cos(np.pi * away)
        rows.append((terms.sum(0) + nyquist) / total_y)
    index = (away[:, None] - away[None, :]) % total_y
    full = np.stack(rows)[:, index]
    high, low = np_split(full)
    return np.concatenate([high, low], 2)


def split(value):
    high = value.astype(BF16)
    low = (value - high.astype(F32)).astype(BF16)
    return high, low


def rates_kernel(m_ref, v_ref, w_ref, lx_ref, ly_ref, lz_ref, rx_ref, ry_ref, rz_ref, fx_ref, fy_ref, fz_ref,
                 rate_ref, x0_ref, x1_ref, y0_ref, y1_ref, z_ref):
    problems, comps, cx, cy, cz = m_ref.shape
    cells = cx * cy
    planes = problems * comps * 3

    @pl.loop(0, problems)
    def _(p):
        m = [m_ref[p, c].reshape(cells, cz) for c in range(3)]
        v = [v_ref[c].reshape(cells, cz) for c in range(3)]
        wave = w_ref[p]
        tx = m[0] + wave[0:1]
        ty = m[1] + wave[1:2]
        tz = m[2]
        f = [
            v[1] * tz - v[2] * ty,
            v[2] * tx - v[0] * tz,
            v[0] * ty - v[1] * tx,
        ]
        fh, fl = zip(*[split(a) for a in f])
        mh, ml = zip(*[split(a) for a in m])
        lefts = (
            (lx_ref, [fh[2], mh[0], fl[2], ml[0], fh[2], mh[0]]),
            (ly_ref, [fh[2], mh[1], fl[2], ml[1], fh[2], mh[1]]),
            (lz_ref, [fh[1], fh[0], mh[2], fl[1], fl[0], ml[2], fh[1], fh[0], mh[2]]),
        )
        rights = (
            (rx_ref, fx_ref, [fh[1], mh[0], fl[1], ml[0], fh[1], mh[0]]),
            (ry_ref, fy_ref, [fh[0], mh[1], fl[0], ml[1], fh[0], mh[1]]),
            (rz_ref, fz_ref, [mh[2], ml[2], mh[2]]),
        )
        for c in range(3):
            weights, data = lefts[c]
            left = jnp.dot(weights[...], jnp.concatenate(data, 0), preferred_element_type=F32)
            main, face, data = rights[c]
            data = jnp.concatenate(data, 1)
            rate = left[:cells] + jnp.dot(data, main[...], preferred_element_type=F32)
            if c == 1:
                rate = rate + STRETCH * tx
            rate_ref[p, c] = rate.reshape(cx, cy, cz)
            z_ref[p, c] = lax.dot_general(face[...], data, (((1,), (1,)), ((), ())), preferred_element_type=F32)
            at = cells
            for ref in (x0_ref, x1_ref):
                for i in range(3):
                    ref[pl.ds(p * comps * 3 + c * 3 + i, cy, stride=planes), :] = left[at:at + cy]
                    at += cy
            for ref in (y0_ref, y1_ref):
                ref[p, c] = left[at:at + 3 * cx].reshape(3, cx, cz)
                at += 3 * cx


def finish_kernel(offset_ref, m_ref, local_ref, x0_ref, follow_ref, x1_ref, y0_ref, y1_ref, zup_ref, zdown_ref,
                  rate_ref, section_ref, joined_ref):
    problems, comps, cx, cy, cz = m_ref.shape
    cells = cx * cy
    planes = problems * comps * 3
    half = cy * planes
    joined_ref[0:half] = x0_ref[...]
    joined_ref[half:] = follow_ref[...]
    first = offset_ref[0] * planes
    rows = lax.broadcasted_iota(jnp.int32, (8, cz), 0)
    lanes = lax.broadcasted_iota(jnp.int32, (8, cz), 1)
    place = jnp.where((rows < 3) & (lanes == cz - 3 + rows), 1.0, 0.0) + jnp.where(
        (rows >= 3) & (rows < 6) & (lanes == rows - 3), 1.0, 0.0)
    zrow = lax.broadcasted_iota(jnp.int32, (8, cells), 0)

    @pl.loop(0, problems)
    def _(p):
        for c in range(3):
            ghosts = jnp.where(zrow < 3, zup_ref[p, c], zdown_ref[p, c])
            spread = lax.dot_general(ghosts, place, (((0,), (0,)), ((), ())),
                                     preferred_element_type=F32, precision=lax.Precision.HIGHEST)
            k = p * comps * 3 + c * 3
            spread = spread.reshape(cx, cy, cz)
            for x in range(cx):
                value = local_ref[p, c, x] + spread[x]
                if x < 3:
                    value = value + x1_ref[pl.ds(k + x, cy, stride=planes), :]
                if x >= cx - 3:
                    value = value + joined_ref[pl.ds(first + k + x - (cx - 3), cy, stride=planes), :]
                low = jnp.concatenate([y1_ref[p, c, i, x:x + 1] for i in range(3)], 0)
                high = jnp.concatenate([y0_ref[p, c, i, x:x + 1] for i in range(3)], 0)
                value = value + jnp.concatenate([low, jnp.zeros((cy - 6, cz), F32), high], 0)
                rate_ref[p, c, x] = value
                section_ref[x, p * comps + c] = m_ref[p, c, x] + SECTION_WEIGHT * value


def shift_kernel(data_ref, table_ref, out_ref):
    blocks, rows, cy, cz = data_ref.shape
    total = blocks * cy
    high = table_ref[:, :total]
    low = table_ref[:, total:]
    for row in range(0, rows, 2):
        data = jnp.concatenate([data_ref[:, r].reshape(total, cz) for r in (row, row + 1)], 1)
        dh, dl = split(data)
        out = (jnp.dot(high, dh, preferred_element_type=F32) + jnp.dot(high, dl, preferred_element_type=F32)
               + jnp.dot(low, dh, preferred_element_type=F32))
        out_ref[:, row] = out[:, :cz].reshape(blocks, cy, cz)
        out_ref[:, row + 1] = out[:, cz:].reshape(blocks, cy, cz)


def reorder_kernel(in_ref, out_ref):
    cx, rows = in_ref.shape[:2]
    for x in range(cx):
        out_ref[:, x] = in_ref[x]


def struct(*shape):
    return jax.ShapeDtypeStruct(shape, F32)


VMEM = pl.BlockSpec(memory_space=pltpu.VMEM)
PARAMS = pltpu.CompilerParams(vmem_limit_bytes=48 * 1024 * 1024)


def wave_table(freq_index, positions, total_z):
    phase = 2.0 * math.pi * freq_index.astype(F32)[:, None] * positions[None, :] / total_z
    cosine, sine = jnp.cos(phase), jnp.sin(phase)
    zeros = jnp.zeros_like(cosine)
    table = jnp.stack([
        jnp.stack([cosine, zeros], 1), jnp.stack([sine, zeros], 1),
        jnp.stack([zeros, cosine], 1), jnp.stack([zeros, sine], 1),
    ], 1)
    return table.reshape(4 * freq_index.shape[0], 2, positions.shape[0])


def on_device(magnetic, velocity, shear_shift, freq_index):
    problems, comps, cx, cy, cz = magnetic.shape
    nx, ny, nz = lax.axis_size("gx"), lax.axis_size("gy"), lax.axis_size("gz")
    total_x, total_y, total_z = cx * nx, cy * ny, cz * nz
    gx, gy, gz = lax.axis_index("gx"), lax.axis_index("gy"), lax.axis_index("gz")
    positions = (gz * cz + jnp.arange(cz)).astype(F32)
    waves = wave_table(freq_index, positions, total_z)
    lefts = [jnp.asarray(w) for w in left_weights(cx, cy)]
    mains, faces = right_weights(cz)
    mains, faces = [jnp.asarray(w) for w in mains], [jnp.asarray(w) for w in faces]
    planes = problems * comps * 3
    local, x0, x1, y0, y1, z = pl.pallas_call(
        rates_kernel,
        out_shape=(
            struct(problems, comps, cx, cy, cz), struct(cy * planes, cz), struct(cy * planes, cz),
            struct(problems, comps, 3, cx, cz), struct(problems, comps, 3, cx, cz),
            struct(problems, comps, 8, cx * cy),
        ),
        in_specs=[VMEM] * 12, out_specs=(VMEM,) * 6, compiler_params=PARAMS,
    )(magnetic, velocity, waves, *lefts, *mains, *faces)

    def at(x, y):
        return (x % nx) * ny + y % ny

    down = [(j, (j - 1) % ny) for j in range(ny)]
    up = [(j, (j + 1) % ny) for j in range(ny)]
    zdown = [(j, (j - 1) % nz) for j in range(nz)]
    zup = [(j, (j + 1) % nz) for j in range(nz)]
    follow = [(at(1, j + 1), at(1, j)) for j in range(ny)]
    low_amount = (total_y - shear_shift[1]) % total_y
    high_amount = shear_shift[0]

    def towards_low(q):
        return [(at(0, j + q), at(1, j)) for j in range(ny)] + [(at(1, j), at(0, j)) for j in range(ny)]

    def towards_high(q):
        return [(at(1, j + q), at(0, j)) for j in range(ny)] + [(at(0, j), at(1, j)) for j in range(ny)]

    def routed(value, route, q):
        return lax.switch(q, [functools.partial(lax.ppermute, axis_name=("gx", "gy"), perm=route(i)) for i in range(ny)],
                          value)

    x1_next = lax.ppermute(x1, ("gx", "gy"), follow)
    y0_in = lax.ppermute(y0, "gy", down)
    y1_in = lax.ppermute(y1, "gy", up)
    z_up = lax.ppermute(z, "gz", zdown)
    z_down = lax.ppermute(z, "gz", zup)
    x0_in = routed(x0, towards_low, low_amount // cy)
    x0_next = lax.ppermute(x0_in, ("gx", "gy"), follow)
    start = jnp.where(gx == 1, high_amount % cy, 0)
    x1_rows = lax.dynamic_slice_in_dim(
        jnp.concatenate([x1.reshape(cy, planes, cz), x1_next.reshape(cy, planes, cz)], 0), start, cy, 0)
    x1_in = routed(x1_rows.reshape(cy * planes, cz), towards_high, high_amount // cy)
    offset = jnp.where(gx == 1, low_amount % cy, 0).astype(jnp.int32).reshape(1)
    rate, section = pl.pallas_call(
        finish_kernel,
        out_shape=(struct(problems, comps, cx, cy, cz), struct(cx, problems * comps, cy, cz)),
        in_specs=[pl.BlockSpec(memory_space=pltpu.SMEM)] + [VMEM] * 9, out_specs=(VMEM,) * 2,
        scratch_shapes=[pltpu.VMEM((2 * cy * planes, cz), F32)],
        compiler_params=PARAMS,
    )(offset, magnetic, local, x0_in, x0_next, x1_in, y0_in, y1_in, z_up, z_down)

    rows = cx * problems * comps
    tables = jnp.asarray(shift_matrices(total_x, total_y))
    table = lax.dynamic_index_in_dim(tables, gx * cx + gy * (rows // ny) // (problems * comps), 0, keepdims=False)
    pencil = lax.all_to_all(section.reshape(rows, cy, cz), "gy", 0, 0, tiled=True)
    turned = pl.pallas_call(
        shift_kernel, out_shape=struct(ny, rows // ny, cy, cz), in_specs=[VMEM] * 2, out_specs=VMEM,
        compiler_params=PARAMS,
    )(pencil.reshape(ny, rows // ny, cy, cz), table)
    returned = lax.all_to_all(turned.reshape(rows, cy, cz), "gy", 0, 0, tiled=True)
    advanced = pl.pallas_call(
        reorder_kernel, out_shape=struct(problems * comps, cx, cy, cz), in_specs=[VMEM], out_specs=VMEM,
        compiler_params=PARAMS,
    )(returned.reshape(cx, problems * comps, cy, cz))
    return rate, advanced.reshape(magnetic.shape)


def solution(mesh):
    return jax.shard_map(
        on_device,
        mesh=mesh,
        in_specs=(P(None, None, "gx", "gy", "gz"), P(None, "gx", "gy", "gz"), P(), P()),
        out_specs=(P(None, None, "gx", "gy", "gz"), P(None, None, "gx", "gy", "gz")),
        check_vma=False,
    )
```

time: 344 us -> 146 us (0.42)
  other arithmetic: 90.7 us -> 1.96 us
  waiting for transfers between devices: 129 us -> 48.9 us
  local copies, waits for them, and re-layouts: 56 us -> 12.5 us
  Pallas kernels: 0 us -> 17.3 us
  starting transfers between devices: 25.9 us -> 35.9 us
  blocking collectives: 32.3 us -> 24.8 us
  matrix products: 6.7 us -> 0 us
    ppermute x10 -> x8, waiting for transfers between devices: 104 us -> 28.4 us  [the longest x2 24 us: routed(): lax.switch(q, [functools.partial(lax.ppermute, axis_name=('gx', 'gy'), pe...]
    concatenate x7 -> x1, other arithmetic: 27.5 us -> 1.17 us  [on_device(): jnp.concatenate([x1.reshape(cy, planes, cz), x1_next.reshape(cy, planes,...]
    add x5 -> x0, other arithmetic: 23.8 us -> none  [the longest x1 18.7 us: on_device(): second_diff(field_radial, 2, cells_x)]
    div x2 -> x0, other arithmetic: 21.9 us -> none  [first_diff(): (45.0 * (window(1) - window(-1)) - 9.0 * (window(2) - window(-2)) + (wind...]
    pallas_call x0 -> x4, Pallas kernels: none -> 17.3 us  [the longest x1 9 us: on_device(): pl.pallas_call(rates_kernel, out_shape=(struct(problems, comps, cx, cy, c...]
    slice x7 -> x1, local copies, waits for them, and re-layouts: 17.9 us -> 0.6 us  [on_device(): high_amount = shear_shift[0]]
    select_n x6 -> x0, other arithmetic: 13.2 us -> none  [the longest x4 9.75 us: offset_rows(): jnp.where(owner_step // (1 << level) % 2 == 1, moved_rows, current)]
    ppermute x4 -> x0, local copies, waits for them, and re-layouts: 12.6 us -> none  [the longest x2 6.47 us: padded_2(): before = lax.ppermute(last, axis, up)]
  transfers between devices with their start and end apart: 11 -> 9, of which waited for: 6 -> 4; matrix products, arithmetic and copies ran while one was open for 20% -> 2% of each run, Pallas kernels for 0% -> 0%
where the time goes in v1:
time: 146 us; the launch traced here: 145 us
  waiting for transfers between devices  48.9 us (33%)
  starting transfers between devices  35.9 us (25%)
  blocking collectives  24.8 us (17%)
  Pallas kernels  17.3 us (12%)
  local copies, waits for them, and re-layouts  12.5 us (9%)
  between operations  3.6 us (2%)
  other arithmetic  1.96 us (1%)
    all_to_all x1, blocking collectives, on_device(): lax.all_to_all(turned.reshape(rows, cy, cz), 'gy', 0, 0, tiled=True)  24.8 us
    ppermute x2, waiting for transfers between devices, routed(): lax.switch(q, [functools.partial(lax.ppermute, axis_name=('gx', 'gy'), pe...  24 us
    all_to_all x1, waiting for transfers between devices, on_device(): lax.all_to_all(section.reshape(rows, cy, cz), 'gy', 0, 0, tiled=True)  20.5 us
    ppermute x2, starting transfers between devices, routed(): lax.switch(q, [functools.partial(lax.ppermute, axis_name=('gx', 'gy'), pe...  13.9 us
    unnamed x30, local copies, waits for them, and re-layouts  11 us
    all_to_all x1, starting transfers between devices, on_device(): lax.all_to_all(section.reshape(rows, cy, cz), 'gy', 0, 0, tiled=True)  9.68 us
    pallas_call x1, Pallas kernels, on_device(): pl.pallas_call(rates_kernel, out_shape=(struct(problems, comps, cx, cy, c...  9 us
    pallas_call x1, Pallas kernels, on_device(): pl.pallas_call(finish_kernel, out_shape=(struct(problems, comps, cx, cy,...  6.25 us
  transfers between devices with their start and end apart: 9, of which 4 were waited for; matrix products, arithmetic and copies ran while one was open for 2% of the time, Pallas kernels for 0%

profile of v1, /device:TPU:1, one launch (start us, length us, event | category | flops | bytes accessed | tf_op | source)
XLA Modules:
  0.0 145.1 jit_solution(6908967583220956294)
XLA Ops:
  1.5 1.1 copy-done.1
  2.5 1.0 copy-done.2
  3.5 1.0 copy-done.3
  4.6 0.9 copy-done.4
  5.5 0.9 copy-done.5
  6.4 0.9 copy-done.6
  7.3 0.9 copy-done.7
  8.2 0.7 copy-done.8
  8.9 0.7 copy-done.9
  10.3 9.0 %shard_map.149 = (f32[8,3,8,16,128]{4,3,2,1,0:T(8,128)S(1)}, f32[1152,128]{1,0:T(8,128)}, f32[1152,128]{1,0:T(8,128)}, f32[8,3,3,8,128]{4,3,2,1,0:T(8,128)S(1)},...) custom-call(f32[8,3,8,16,128]{4,3,2,1,0:T(8,128)} %m_ref.3, f32[3,8,16,128]{3,2,1,0:T(8,128)S(1)} %copy-done.4, ...), custom_call_target="tpu_custom_call" | custom-call | tf_op jit(solution)/shard_map/pallas_call | solution.py:261
  19.3 0.7 copy-done.11
  20.1 0.7 copy-done.12
  21.4 1.6 %collective-permute-start.33 = (f32[1152,128]{1,0:T(8,128)}, f32[1152,128]{1,0:T(8,128)}, u32[]{:S(2)}, u32[]{:S(2)}) collective-permute-start(f32[1152,128]{1,0:T(8,128)} %get-tuple-element.78), channel_id=1, source_target_pairs={{68,64},{72,68},{76,72},{80,76},{84,80},{88,84},{92,88},{96,92},{1... | collective-permute-start | bytes 1769480 | tf_op jit(solution)/shard_map/ppermute | solution.py:292
  24.3 19.1 %conditional.2 = (f32[1152,128]{1,0:T(8,128)}) conditional(s32[]{:T(128)} %clamp.6, f32[1152,128]{1,0:T(8,128)} %get-tuple-element.77, f32[1152,128]{1,0:T(8,128)} %get-tuple-element.77, f32[1152,128]{1,0:T(8,128)} %get-tuple-element.77, f32[1152,128]{1,0:T(8,128)} %get-tuple-element.77, ...), branch_computations={%region_0.1_spmd, %region_1.2_spmd, %region_2.3_spmd, %region_3.4_... | conditional | bytes 2359344 | solution.py:289
  24.3 7.1 %collective-permute-start.3 = (f32[1152,128]{1,0:T(8,128)}, f32[1152,128]{1,0:T(8,128)}, u32[]{:S(2)}, u32[]{:S(2)}) collective-permute-start(f32[1152,128]{1,0:T(8,128)} %param.3), channel_id=1, source_target_pairs={{12,64},{16,68},{20,72},{24,76},{28,80},{32,84},{36,88},{40,92},{4... | collective-permute-start | bytes 1769480 | tf_op jit(solution)/shard_map/cond/branch_3_fun/ppermute | solution.py:289
  31.4 12.0 %collective-permute-done.3 = f32[1152,128]{1,0:T(8,128)} collective-permute-done((f32[1152,128]{1,0:T(8,128)}, f32[1152,128]{1,0:T(8,128)}, u32[]{:S(2)}, u32[]{:S(2)}) %collective-permute-start.3) | collective-permute-done | bytes 589856 | tf_op jit(solution)/shard_map/cond/branch_3_fun/ppermute | solution.py:289
  43.4 1.5 %collective-permute-start.32 = (f32[1152,128]{1,0:T(8,128)}, f32[1152,128]{1,0:T(8,128)}, u32[]{:S(2)}, u32[]{:S(2)}) collective-permute-start(f32[1152,128]{1,0:T(8,128)} %get-tuple-element.94.x0_ref), channel_id=1, source_target_pairs={{68,64},{72,68},{76,72},{80,76},{84,80},{88,84},{92,88},{96,92},{1... | collective-permute-start | bytes 1769480 | tf_op jit(solution)/shard_map/ppermute | solution.py:298
  45.3 3.0 %collective-permute-start.35 = (f32[8,3,3,8,128]{4,3,2,1,0:T(8,128)}, f32[8,3,3,8,128]{4,3,2,1,0:T(8,128)}, u32[]{:S(2)}, u32[]{:S(2)}) collective-permute-start(f32[8,3,3,8,128]{4,3,2,1,0:T(8,128)} %copy-done.11), channel_id=1, source_target_pairs={{0,4},{4,8},{8,12},{12,16},{16,20},{20,24},{24,28},{28,32},{32,36}... | collective-permute-start | bytes 884744 | tf_op jit(solution)/shard_map/ppermute | solution.py:294
  48.3 3.8 %collective-permute-start.36 = (f32[8,3,8,128]{3,2,1,0:T(8,128)}, f32[8,3,8,128]{3,2,1,0:T(8,128)S(1)}, u32[]{:S(2)}, u32[]{:S(2)}) collective-permute-start(f32[8,3,8,128]{3,2,1,0:T(8,128)} %copy-done.13), channel_id=1, source_target_pairs={{0,3},{1,0},{2,1},{3,2},{4,7},{5,4},{6,5},{7,6},{8,11},{9,8},{10,9... | collective-permute-start | bytes 294920 | tf_op jit(solution)/shard_map/ppermute | solution.py:295
  54.3 1.2 fusion
  55.5 18.8 %conditional.3 = (f32[1152,128]{1,0:T(8,128)}) conditional(s32[]{:T(128)} %clamp.7, f32[1152,128]{1,0:T(8,128)S(1)} %bitcast.33, f32[1152,128]{1,0:T(8,128)S(1)} %bitcast.34, f32[1152,128]{1,0:T(8,128)S(1)} %bitcast.35, f32[1152,128]{1,0:T(8,128)S(1)} %bitcast.36, f32[1152,128]{1,0:T(8,128)S(1)} %bitcast.37, ...), branch_computations={%region_16.17_spmd, %region_17.18_spmd, %region_18.19_spmd, %regio... | conditional | bytes 2359344 | solution.py:289
  55.5 6.8 %collective-permute-start.16 = (f32[1152,128]{1,0:T(8,128)S(1)}, f32[1152,128]{1,0:T(8,128)}, u32[]{:S(2)}, u32[]{:S(2)}) collective-permute-start(f32[1152,128]{1,0:T(8,128)S(1)} %param.16), channel_id=1, source_target_pairs={{64,0},{68,4},{72,8},{76,12},{80,16},{84,20},{88,24},{92,28},{96,3... | collective-permute-start | bytes 1769480 | tf_op jit(solution)/shard_map/cond/branch_0_fun/ppermute | solution.py:289
  62.3 12.0 %collective-permute-done.16 = f32[1152,128]{1,0:T(8,128)} collective-permute-done((f32[1152,128]{1,0:T(8,128)S(1)}, f32[1152,128]{1,0:T(8,128)}, u32[]{:S(2)}, u32[]{:S(2)}) %collective-permute-start.16) | collective-permute-done | bytes 589856 | tf_op jit(solution)/shard_map/cond/branch_0_fun/ppermute | solution.py:289
  74.3 2.1 %collective-permute-start.37 = (f32[8,3,8,128]{3,2,1,0:T(8,128)}, f32[8,3,8,128]{3,2,1,0:T(8,128)}, u32[]{:S(2)}, u32[]{:S(2)}) collective-permute-start(f32[8,3,8,128]{3,2,1,0:T(8,128)} %copy-done.13), channel_id=1, source_target_pairs={{0,1},{1,2},{2,3},{3,0},{4,5},{5,6},{6,7},{7,4},{8,9},{9,10},{10,1... | collective-permute-start | bytes 294920 | tf_op jit(solution)/shard_map/ppermute | solution.py:296
  76.4 4.4 %collective-permute-done.37.zdown_ref = f32[8,3,8,128]{3,2,1,0:T(8,128)} collective-permute-done((f32[8,3,8,128]{3,2,1,0:T(8,128)}, f32[8,3,8,128]{3,2,1,0:T(8,128)}, u32[]{:S(2)}, u32[]{:S(2)}) %collective-permute-start.37) | collective-permute-done | bytes 98336 | tf_op jit(solution)/shard_map/ppermute | solution.py:296
  80.8 6.2 %shard_map.150 = (f32[8,3,8,16,128]{4,3,2,1,0:T(8,128)}, f32[8,24,16,128]{3,2,1,0:T(8,128)}) custom-call(s32[1]{0:T(128)} %bitcast.1.offset_ref, f32[8,3,8,16,128]{4,3,2,1,0:T(8,128)S(1)} %copy-done, f32[8,3,8,16,128]{4,3,2,1,0:T(8,128)S(1)} %get-tuple-element.76.local_ref, f32[1152,128]{1,0:T(8,128)} %get-tuple-element.94.x0_ref, ...), custom_call_target="tpu_custom_call" | custom-call | tf_op jit(solution)/shard_map/pallas_call | solution.py:304
  87.1 9.7 %all-to-all-start = ((f32[192,16,128]{2,1,0:T(8,128)}), f32[192,16,128]{2,1,0:T(8,128)S(1)}, u32[]{:S(2)}, u32[]{:S(2)}) async-start(f32[192,16,128]{2,1,0:T(8,128)} %bitcast.14), calls=%async_computation | async-start | bytes 3145728 | tf_op jit(solution)/shard_map/all_to_all | solution.py:315
  96.8 1.0 dynamic-slice_bitcast_fusion.table_ref
  97.7 20.5 %all-to-all-done = f32[192,16,128]{2,1,0:T(8,128)S(1)} async-done(((f32[192,16,128]{2,1,0:T(8,128)}), f32[192,16,128]{2,1,0:T(8,128)S(1)}, u32[]{:S(2)}, u32[]{:S(2)}) %all-to-all-start) | async-done | bytes 1572896 | tf_op jit(solution)/shard_map/all_to_all | solution.py:315
  118.2 0.8 shard_map.151
  119.0 24.8 %all_to_all.10 = f32[192,16,128]{2,1,0:T(8,128)S(1)} all-to-all(f32[192,16,128]{2,1,0:T(8,128)S(1)} %bitcast.30), channel_id=1, replica_groups=mesh['gx'=2,'gy'=16,'gz'=4] {'gy'}, dimensions={0} | all-to-all | bytes 3145728 | tf_op jit(solution)/shard_map/all_to_all | solution.py:320
  143.9 1.2 shard_map.152
  (31 shorter events, 3.2 us)
Async XLA Ops:
  1.5 1.1 copy-start.1
  2.5 1.0 copy-start.2
  3.5 1.0 copy-start.3
  4.6 0.9 copy-start.4
  5.5 0.9 copy-start.5
  6.4 0.9 copy-start.6
  7.3 0.9 copy-start.7
  8.2 0.7 copy-start.8
  8.9 0.7 copy-start.9
  9.6 0.7 copy-start.10
  10.3 12.7 %copy-start.14 = (s32[2]{0:T(128)S(1)}, s32[2]{0:T(128)}, u32[]{:S(2)}) copy-start(s32[2]{0:T(128)} %param.48) | copy-start | bytes 28
  19.3 0.7 copy-start.11
  20.1 0.7 copy-start.12
  20.8 0.6 copy-start.13
  21.4 59.4 %copy-start = (f32[8,3,8,16,128]{4,3,2,1,0:T(8,128)S(1)}, f32[8,3,8,16,128]{4,3,2,1,0:T(8,128)}, u32[]{:S(2)}) copy-start(f32[8,3,8,16,128]{4,3,2,1,0:T(8,128)} %m_ref.3) | copy-start | bytes 4718596
  21.4 32.9 %collective-permute-start.33 = (f32[1152,128]{1,0:T(8,128)}, f32[1152,128]{1,0:T(8,128)}, u32[]{:S(2)}, u32[]{:S(2)}) collective-permute-start(f32[1152,128]{1,0:T(8,128)} %get-tuple-element.78), channel_id=1, source_target_pairs={{68,64},{72,68},{76,72},{80,76},{84,80},{88,84},{92,88},{96,92},{1... | collective-permute-start | bytes 1769480 | tf_op jit(solution)/shard_map/ppermute | solution.py:292
  24.3 19.1 %collective-permute-start.3 = (f32[1152,128]{1,0:T(8,128)}, f32[1152,128]{1,0:T(8,128)}, u32[]{:S(2)}, u32[]{:S(2)}) collective-permute-start(f32[1152,128]{1,0:T(8,128)} %param.3), channel_id=1, source_target_pairs={{12,64},{16,68},{20,72},{24,76},{28,80},{32,84},{36,88},{40,92},{4... | collective-permute-start | bytes 1769480 | tf_op jit(solution)/shard_map/cond/branch_3_fun/ppermute | solution.py:289
  43.4 37.4 %collective-permute-start.32 = (f32[1152,128]{1,0:T(8,128)}, f32[1152,128]{1,0:T(8,128)}, u32[]{:S(2)}, u32[]{:S(2)}) collective-permute-start(f32[1152,128]{1,0:T(8,128)} %get-tuple-element.94.x0_ref), channel_id=1, source_target_pairs={{68,64},{72,68},{76,72},{80,76},{84,80},{88,84},{92,88},{96,92},{1... | collective-permute-start | bytes 1769480 | tf_op jit(solution)/shard_map/ppermute | solution.py:298
  44.9 35.9 %collective-permute-start.34 = (f32[8,3,3,8,128]{4,3,2,1,0:T(8,128)}, f32[8,3,3,8,128]{4,3,2,1,0:T(8,128)S(1)}, u32[]{:S(2)}, u32[]{:S(2)}) collective-permute-start(f32[8,3,3,8,128]{4,3,2,1,0:T(8,128)} %copy-done.12), channel_id=1, source_target_pairs={{0,60},{4,0},{8,4},{12,8},{16,12},{20,16},{24,20},{28,24},{32,28},... | collective-permute-start | bytes 884744 | tf_op jit(solution)/shard_map/ppermute | solution.py:293
  45.3 35.5 %collective-permute-start.35 = (f32[8,3,3,8,128]{4,3,2,1,0:T(8,128)}, f32[8,3,3,8,128]{4,3,2,1,0:T(8,128)}, u32[]{:S(2)}, u32[]{:S(2)}) collective-permute-start(f32[8,3,3,8,128]{4,3,2,1,0:T(8,128)} %copy-done.11), channel_id=1, source_target_pairs={{0,4},{4,8},{8,12},{12,16},{16,20},{20,24},{24,28},{28,32},{32,36}... | collective-permute-start | bytes 884744 | tf_op jit(solution)/shard_map/ppermute | solution.py:294
  48.3 28.1 %collective-permute-start.36 = (f32[8,3,8,128]{3,2,1,0:T(8,128)}, f32[8,3,8,128]{3,2,1,0:T(8,128)S(1)}, u32[]{:S(2)}, u32[]{:S(2)}) collective-permute-start(f32[8,3,8,128]{3,2,1,0:T(8,128)} %copy-done.13), channel_id=1, source_target_pairs={{0,3},{1,0},{2,1},{3,2},{4,7},{5,4},{6,5},{7,6},{8,11},{9,8},{10,9... | collective-permute-start | bytes 294920 | tf_op jit(solution)/shard_map/ppermute | solution.py:295
  55.5 18.8 %collective-permute-start.16 = (f32[1152,128]{1,0:T(8,128)S(1)}, f32[1152,128]{1,0:T(8,128)}, u32[]{:S(2)}, u32[]{:S(2)}) collective-permute-start(f32[1152,128]{1,0:T(8,128)S(1)} %param.16), channel_id=1, source_target_pairs={{64,0},{68,4},{72,8},{76,12},{80,16},{84,20},{88,24},{92,28},{96,3... | collective-permute-start | bytes 1769480 | tf_op jit(solution)/shard_map/cond/branch_0_fun/ppermute | solution.py:289
  74.3 6.5 %collective-permute-start.37 = (f32[8,3,8,128]{3,2,1,0:T(8,128)}, f32[8,3,8,128]{3,2,1,0:T(8,128)}, u32[]{:S(2)}, u32[]{:S(2)}) collective-permute-start(f32[8,3,8,128]{3,2,1,0:T(8,128)} %copy-done.13), channel_id=1, source_target_pairs={{0,1},{1,2},{2,3},{3,0},{4,5},{5,6},{6,7},{7,4},{8,9},{9,10},{10,1... | collective-permute-start | bytes 294920 | tf_op jit(solution)/shard_map/ppermute | solution.py:296
  87.1 31.2 %all-to-all-start = ((f32[192,16,128]{2,1,0:T(8,128)}), f32[192,16,128]{2,1,0:T(8,128)S(1)}, u32[]{:S(2)}, u32[]{:S(2)}) async-start(f32[192,16,128]{2,1,0:T(8,128)} %bitcast.14), calls=%async_computation | async-start | bytes 3145728 | tf_op jit(solution)/shard_map/all_to_all | solution.py:315

commit v2 on v1

v2 whole, which is shorter than its diff:
```python
import functools
import math

import jax
import jax.numpy as jnp
import ml_dtypes
import numpy as np
from jax import lax
from jax.experimental import pallas as pl
from jax.experimental.pallas import tpu as pltpu
from jax.sharding import PartitionSpec as P

SHEAR_RATE = 1.5
TIME_STEP = 0.2
DIFFUSIVITY = 0.1
SECTION_WEIGHT = 1.0 / 3.0

D1 = [TIME_STEP * w / 60.0 for w in (45.0, -9.0, 1.0)]
D2 = [TIME_STEP * DIFFUSIVITY * w / 180.0 for w in (270.0, -27.0, 2.0)]
D2_CENTRE = -TIME_STEP * DIFFUSIVITY * 490.0 / 180.0
STRETCH = -TIME_STEP * SHEAR_RATE

BF16 = jnp.bfloat16
F32 = jnp.float32


def np_split(value):
    value = np.asarray(value, np.float64)
    high = value.astype(np.float32).astype(ml_dtypes.bfloat16)
    low = (value - high.astype(np.float64)).astype(np.float32).astype(ml_dtypes.bfloat16)
    return high, low


def stencil_1d(first_out, outs, size, centre):
    one = np.zeros((outs, size))
    two = np.zeros((outs, size))
    for row in range(outs):
        at = first_out + row
        for d in (1, 2, 3):
            if 0 <= at + d < size:
                one[row, at + d] += D1[d - 1]
                two[row, at + d] += D2[d - 1]
            if 0 <= at - d < size:
                one[row, at - d] -= D1[d - 1]
                two[row, at - d] += D2[d - 1]
        if 0 <= at < size:
            two[row, at] += centre
    return one, two


def left_weights(cx, cy):
    eye_x, eye_y = np.eye(cx), np.eye(cy)
    x1, x2 = stencil_1d(0, cx, cx, D2_CENTRE)
    y1, y2 = stencil_1d(0, cy, cy, D2_CENTRE)
    xl1, xl2 = stencil_1d(-3, 3, cx, 0.0)
    xh1, xh2 = stencil_1d(cx, 3, cx, 0.0)
    yl1, yl2 = stencil_1d(-3, 3, cy, 0.0)
    yh1, yh2 = stencil_1d(cy, 3, cy, 0.0)

    def face_y(rows):
        return np.einsum("iy,xz->ixzy", rows, eye_x).reshape(3 * cx, cx * cy)

    none_x = np.zeros((3 * cy, cx * cy))
    none_y = np.zeros((3 * cx, cx * cy))
    dx = np.concatenate([np.kron(x1, eye_y), np.kron(xl1, eye_y), np.kron(xh1, eye_y), none_y, none_y])
    dy = np.concatenate([np.kron(eye_x, y1), none_x, none_x, face_y(yl1), face_y(yh1)])
    lap = np.concatenate([
        np.kron(x2, eye_y) + np.kron(eye_x, y2),
        np.kron(xl2, eye_y), np.kron(xh2, eye_y), face_y(yl2), face_y(yh2),
    ])
    out_x = np.concatenate([dy, lap], 1)
    out_y = np.concatenate([-dx, lap], 1)
    out_z = np.concatenate([dx, -dy, lap], 1)
    result = []
    for value in (out_x, out_y, out_z):
        high, low = np_split(value)
        result.append(np.concatenate([high, high, low], 1))
    return result


def right_weights(cz):
    one, two = stencil_1d(0, cz, cz, D2_CENTRE)
    lo1, lo2 = stencil_1d(-3, 3, cz, 0.0)
    hi1, hi2 = stencil_1d(cz, 3, cz, 0.0)
    pad = np.zeros((2, cz))
    face1 = np.concatenate([lo1, hi1, pad])
    face2 = np.concatenate([lo2, hi2, pad])
    mains, faces = [], []
    for main, face in (
        (np.concatenate([-one.T, two.T]), np.concatenate([-face1, face2], 1)),
        (np.concatenate([one.T, two.T]), np.concatenate([face1, face2], 1)),
        (two.T, face2),
    ):
        high, low = np_split(main)
        mains.append(np.concatenate([high, high, low], 0))
        high, low = np_split(face)
        faces.append(np.concatenate([high, high, low], 1))
    return mains, faces


def shift_matrices(total_x, total_y):
    modes = np.arange(total_y // 2 + 1)
    sigma = -SHEAR_RATE * SECTION_WEIGHT * TIME_STEP * (np.arange(total_x) + 0.5 - total_x / 2.0)
    weight = np.full(modes.shape, 2.0)
    weight[0] = 1.0
    away = np.arange(total_y)
    rows = []
    for s in sigma:
        terms = weight[:-1, None] * np.cos(2.0 * np.pi / total_y * modes[:-1, None] * (away[None, :] - s))
        nyquist = np.cos(np.pi * s) * np.cos(np.pi * away)
        rows.append((terms.sum(0) + nyquist) / total_y)
    index = (away[:, None] - away[None, :]) % total_y
    full = np.stack(rows)[:, index]
    high, low = np_split(full)
    return np.concatenate([high, low], 2)


def split(value):
    high = value.astype(BF16)
    low = (value - high.astype(F32)).astype(BF16)
    return high, low


def rates_kernel(freq_ref, shift_ref, m_ref, v_ref, lx_ref, ly_ref, lz_ref, rx_ref, ry_ref, rz_ref, fx_ref, fy_ref, fz_ref,
                 rate_ref, x0_ref, x1_ref, y0_ref, y1_ref, z_ref, low_ref, high_ref, *, total_y, total_z):
    pair, comps, cx, cy, cz = m_ref.shape
    low_ref[0] = ((total_y - shift_ref[1]) & (total_y - 1)) // cy
    high_ref[0] = shift_ref[0] // cy
    cells = cx * cy
    planes = x0_ref.shape[0] // cy
    p = pl.program_id(0) * pair

    def wide(parts):
        return jnp.concatenate(parts, 1)

    def tall(value):
        return jnp.concatenate([value[:, i * cz:(i + 1) * cz] for i in range(pair)], 0)

    m = [wide([m_ref[i, c].reshape(cells, cz) for i in range(pair)]) for c in range(3)]
    v = [wide([v_ref[c].reshape(cells, cz)] * pair) for c in range(3)]
    step = pl.program_id(0)
    position = (lax.axis_index("gz") * cz + lax.broadcasted_iota(jnp.int32, (1, cz), 1)).astype(F32)
    phase = 2.0 * math.pi * freq_ref[step // 2].astype(F32) * position / total_z
    wave = wide([jnp.cos(phase), jnp.sin(phase)])
    along_x = step % 2 == 0
    tx = m[0] + jnp.where(along_x, wave, 0.0)
    ty = m[1] + jnp.where(along_x, 0.0, wave)
    tz = m[2]
    f = [
        v[1] * tz - v[2] * ty,
        v[2] * tx - v[0] * tz,
        v[0] * ty - v[1] * tx,
    ]
    fh, fl = zip(*[split(a) for a in f])
    mh, ml = zip(*[split(a) for a in m])
    lefts = (
        (lx_ref, [fh[2], mh[0], fl[2], ml[0], fh[2], mh[0]]),
        (ly_ref, [fh[2], mh[1], fl[2], ml[1], fh[2], mh[1]]),
        (lz_ref, [fh[1], fh[0], mh[2], fl[1], fl[0], ml[2], fh[1], fh[0], mh[2]]),
    )
    rights = (
        (rx_ref, fx_ref, [fh[1], mh[0], fl[1], ml[0], fh[1], mh[0]]),
        (ry_ref, fy_ref, [fh[0], mh[1], fl[0], ml[1], fh[0], mh[1]]),
        (rz_ref, fz_ref, [mh[2], ml[2], mh[2]]),
    )
    for c in range(3):
        weights, data = lefts[c]
        left = jnp.dot(weights[...], jnp.concatenate(data, 0), preferred_element_type=F32)
        if c == 1:
            main_left = left[:cells] + STRETCH * tx
        else:
            main_left = left[:cells]
        main, face, data = rights[c]
        data = jnp.concatenate([tall(d) for d in data], 1)
        right = jnp.dot(data, main[...], preferred_element_type=F32)
        ghost = lax.dot_general(face[...], data, (((1,), (1,)), ((), ())), preferred_element_type=F32)
        for i in range(pair):
            lanes = slice(i * cz, (i + 1) * cz)
            rate = main_left[:, lanes] + right[i * cells:(i + 1) * cells]
            rate_ref[i, c] = rate.reshape(cx, cy, cz)
            z_ref[i, c] = ghost[:, i * cells:(i + 1) * cells]
            at = cells
            for ref in (x0_ref, x1_ref):
                for j in range(3):
                    ref[pl.ds((p + i) * comps * 3 + c * 3 + j, cy, stride=planes), :] = left[at:at + cy, lanes]
                    at += cy
            for ref in (y0_ref, y1_ref):
                ref[i, c] = left[at:at + 3 * cx, lanes].reshape(3, cx, cz)
                at += 3 * cx


def three(value):
    high = value.astype(BF16)
    rest = value - high.astype(F32)
    middle = rest.astype(BF16)
    return [high, middle, (rest - middle.astype(F32)).astype(BF16)]


def place_weights(cx, cy, cz, comps):
    left = np.zeros((cx * cy, 6 * cx))
    for i in range(3):
        for x in range(cx):
            left[x * cy + i, i * cx + x] = 1.0
            left[x * cy + cy - 3 + i, 3 * cx + i * cx + x] = 1.0
    right = np.zeros((8 * comps, comps * cz))
    for c in range(comps):
        for i in range(3):
            right[8 * c + i, c * cz + cz - 3 + i] = 1.0
            right[8 * c + 3 + i, c * cz + i] = 1.0
    return (np.concatenate([left] * 3, 1).astype(ml_dtypes.bfloat16),
            np.concatenate([right] * 3, 0).astype(ml_dtypes.bfloat16))


def finish_kernel(shift_ref, m_ref, local_ref, x0_ref, follow_ref, x1_ref, y0_ref, y1_ref, zup_ref, zdown_ref,
                  left_ref, right_ref, rate_ref, section_ref, joined_ref):
    pair, comps, cx, cy, cz = m_ref.shape
    cells = cx * cy
    half = x0_ref.shape[0]
    planes = half // cy
    step = pl.program_id(0)

    @pl.when(step == 0)
    def _():
        joined_ref[0:half] = x0_ref[...]
        joined_ref[half:] = follow_ref[...]

    first = jnp.where(lax.axis_index("gx") == 1, (cy - (shift_ref[1] & (cy - 1))) & (cy - 1), 0) * planes
    zrow = lax.broadcasted_iota(jnp.int32, (8, cells), 0)
    for i in range(pair):
        ghosts = jnp.concatenate([jnp.where(zrow < 3, zup_ref[i, c], zdown_ref[i, c]) for c in range(comps)], 0)
        ghosts = jnp.concatenate(three(ghosts), 0)
        faces = jnp.concatenate([
            jnp.concatenate([y1_ref[i, c].reshape(3 * cx, cz), y0_ref[i, c].reshape(3 * cx, cz)], 0)
            for c in range(comps)], 1)
        placed = jnp.dot(left_ref[...], jnp.concatenate(three(faces), 0), preferred_element_type=F32)
        placed = placed + lax.dot_general(ghosts, right_ref[...], (((0,), (0,)), ((), ())), preferred_element_type=F32)
        for c in range(comps):
            k = (step * pair + i) * comps * 3 + c * 3
            spread = placed[:, c * cz:(c + 1) * cz].reshape(cx, cy, cz)
            for x in range(cx):
                value = local_ref[i, c, x] + spread[x]
                if x < 3:
                    value = value + x1_ref[pl.ds(k + x, cy, stride=planes), :]
                if x >= cx - 3:
                    value = value + joined_ref[pl.ds(first + k + x - (cx - 3), cy, stride=planes), :]
                rate_ref[i, c, x] = value
                section_ref[x, i * comps + c] = m_ref[i, c, x] + SECTION_WEIGHT * value


def shift_kernel(data_ref, table_ref, out_ref):
    blocks, rows, cy, cz = data_ref.shape
    total = blocks * cy
    high = table_ref[:, :total]
    low = table_ref[:, total:]
    for row in range(0, rows, 2):
        data = jnp.concatenate([data_ref[:, r].reshape(total, cz) for r in (row, row + 1)], 1)
        dh, dl = split(data)
        out = (jnp.dot(high, dh, preferred_element_type=F32) + jnp.dot(high, dl, preferred_element_type=F32)
               + jnp.dot(low, dh, preferred_element_type=F32))
        out_ref[:, row] = out[:, :cz].reshape(blocks, cy, cz)
        out_ref[:, row + 1] = out[:, cz:].reshape(blocks, cy, cz)


def reorder_kernel(in_ref, out_ref):
    cx, rows = in_ref.shape[:2]
    for x in range(cx):
        out_ref[:, x] = in_ref[x]


def struct(*shape):
    return jax.ShapeDtypeStruct(shape, F32)


VMEM = pl.BlockSpec(memory_space=pltpu.VMEM)
SMEM = pl.BlockSpec(memory_space=pltpu.SMEM)
PARAMS = pltpu.CompilerParams(vmem_limit_bytes=40 * 1024 * 1024)
STREAMED = pltpu.CompilerParams(vmem_limit_bytes=60 * 1024 * 1024)


def on_device(magnetic, velocity, shear_shift, freq_index):
    problems, comps, cx, cy, cz = magnetic.shape
    nx, ny, nz = lax.axis_size("gx"), lax.axis_size("gy"), lax.axis_size("gz")
    total_x, total_y, total_z = cx * nx, cy * ny, cz * nz
    gx, gy = lax.axis_index("gx"), lax.axis_index("gy")
    lefts = [jnp.asarray(w) for w in left_weights(cx, cy)]
    mains, faces = right_weights(cz)
    mains, faces = [jnp.asarray(w) for w in mains], [jnp.asarray(w) for w in faces]
    planes = problems * comps * 3
    pair = 2
    steps = problems // pair

    def whole(array):
        return pl.BlockSpec(array.shape, lambda i: (0,) * len(array.shape))

    def cut(*shape):
        return pl.BlockSpec((pair,) + shape, lambda i: (i,) + (0,) * len(shape))

    tile, edge, side = (comps, cx, cy, cz), (comps, 3, cx, cz), (comps, 8, cx * cy)
    faces_x = struct(cy * planes, cz)
    weights = [*lefts, *mains, *faces]
    index = jax.ShapeDtypeStruct((1,), jnp.int32)
    local, x0, x1, y0, y1, z, low_step, high_step = pl.pallas_call(
        functools.partial(rates_kernel, total_y=total_y, total_z=total_z),
        grid=(steps,),
        out_shape=(struct(problems, *tile), faces_x, faces_x, struct(problems, *edge), struct(problems, *edge),
                   struct(problems, *side), index, index),
        in_specs=[SMEM, SMEM, cut(*tile), whole(velocity)] + [whole(w) for w in weights],
        out_specs=(cut(*tile), whole(faces_x), whole(faces_x), cut(*edge), cut(*edge), cut(*side), SMEM, SMEM),
        compiler_params=STREAMED,
    )(freq_index, shear_shift, magnetic, velocity, *weights)

    def at(x, y):
        return (x % nx) * ny + y % ny

    down = [(j, (j - 1) % ny) for j in range(ny)]
    up = [(j, (j + 1) % ny) for j in range(ny)]
    zdown = [(j, (j - 1) % nz) for j in range(nz)]
    zup = [(j, (j + 1) % nz) for j in range(nz)]
    follow = [(at(1, j + 1), at(1, j)) for j in range(ny)]
    def towards_low(q):
        return [(at(0, j + q), at(1, j)) for j in range(ny)] + [(at(1, j), at(0, j)) for j in range(ny)]

    def towards_high(q):
        return [(at(1, j + q), at(0, j)) for j in range(ny)] + [(at(0, j), at(1, j)) for j in range(ny)]

    def routed(q, route, value):
        return lax.switch(q, [functools.partial(lax.ppermute, axis_name=("gx", "gy"), perm=route(i)) for i in range(ny)],
                          value)

    beside = (lax.ppermute(x1, ("gx", "gy"), follow), lax.ppermute(y0, "gy", down), lax.ppermute(y1, "gy", up),
              lax.ppermute(z, "gz", zdown), lax.ppermute(z, "gz", zup))
    x0_in = routed(low_step[0], towards_low, x0)
    x0_in, x1_next, y0_in, y1_in, z_up, z_down = lax.optimization_barrier((x0_in, *beside))
    x0_next = lax.ppermute(x0_in, ("gx", "gy"), follow)
    start = jnp.where(gx == 1, shear_shift[0] & (cy - 1), 0)
    x1_rows = lax.dynamic_slice_in_dim(
        jnp.concatenate([x1.reshape(cy, planes, cz), x1_next.reshape(cy, planes, cz)], 0), start, cy, 0)
    x1_in = routed(high_step[0], towards_high, x1_rows.reshape(cy * planes, cz))
    placing = [jnp.asarray(w) for w in place_weights(cx, cy, cz, comps)]
    rate, section = pl.pallas_call(
        finish_kernel,
        grid=(steps,),
        out_shape=(struct(problems, *tile), struct(cx, problems * comps, cy, cz)),
        in_specs=[SMEM, cut(*tile), cut(*tile)] + [whole(faces_x)] * 3
        + [cut(*edge)] * 2 + [cut(*side)] * 2 + [whole(w) for w in placing],
        out_specs=(cut(*tile), pl.BlockSpec((cx, pair * comps, cy, cz), lambda i: (0, i, 0, 0))),
        scratch_shapes=[pltpu.VMEM((2 * cy * planes, cz), F32)],
        compiler_params=STREAMED,
    )(shear_shift, magnetic, local, x0_in, x0_next, x1_in, y0_in, y1_in, z_up, z_down, *placing)

    rows = cx * problems * comps
    tables = jnp.asarray(shift_matrices(total_x, total_y))
    table = lax.dynamic_index_in_dim(tables, gx * cx + gy * (rows // ny) // (problems * comps), 0, keepdims=False)
    pencil = lax.all_to_all(section.reshape(rows, cy, cz), "gy", 0, 0, tiled=True)
    turned = pl.pallas_call(
        shift_kernel, out_shape=struct(ny, rows // ny, cy, cz), in_specs=[VMEM] * 2, out_specs=VMEM,
        compiler_params=PARAMS,
    )(pencil.reshape(ny, rows // ny, cy, cz), table)
    returned = lax.all_to_all(turned.reshape(rows, cy, cz), "gy", 0, 0, tiled=True)
    advanced = pl.pallas_call(
        reorder_kernel, out_shape=struct(problems * comps, cx, cy, cz), in_specs=[VMEM], out_specs=VMEM,
        compiler_params=PARAMS,
    )(returned.reshape(cx, problems * comps, cy, cz))
    return rate, advanced.reshape(magnetic.shape)


def solution(mesh):
    return jax.shard_map(
        on_device,
        mesh=mesh,
        in_specs=(P(None, None, "gx", "gy", "gz"), P(None, "gx", "gy", "gz"), P(), P()),
        out_specs=(P(None, None, "gx", "gy", "gz"), P(None, None, "gx", "gy", "gz")),
        check_vma=False,
    )
```

time: 146 us -> 129 us (0.88); the launches traced: 145 us -> 131 us
  local copies, waits for them, and re-layouts: 12.5 us -> 1.77 us
  waiting for transfers between devices: 48.9 us -> 55.8 us
  starting transfers between devices: 35.9 us -> 29.9 us
  Pallas kernels: 17.3 us -> 15 us
  between operations: 3.6 us -> 2.11 us
    unnamed x30 -> x12, local copies, waits for them, and re-layouts: 11 us -> 0.8 us
    ppermute x2, waiting for transfers between devices: 24 us -> 30 us  [routed(): lax.switch(q, [functools.partial(lax.ppermute, axis_name=('gx', 'gy'), pe...]
    ppermute x5, starting transfers between devices: 10.9 us -> 7.21 us  [the longest x1 3.76 us: on_device(): lax.ppermute(z, 'gz', zdown)]
    pallas_call x2, Pallas kernels: 15.2 us -> 13 us  [the longest x1 7.18 us: on_device(): pl.pallas_call(functools.partial(rates_kernel, total_y=total_y, total_z=t...]
    ppermute x2, starting transfers between devices: 13.9 us -> 11.9 us  [routed(): lax.switch(q, [functools.partial(lax.ppermute, axis_name=('gx', 'gy'), pe...]
where the time goes in v2:
time: 129 us; the launch traced here: 131 us
  waiting for transfers between devices  55.8 us (43%)
  starting transfers between devices  29.9 us (23%)
  blocking collectives  24.8 us (19%)
  Pallas kernels  15 us (12%)
  between operations  2.11 us (2%)
  local copies, waits for them, and re-layouts  1.77 us (1%)
    ppermute x2, waiting for transfers between devices, routed(): lax.switch(q, [functools.partial(lax.ppermute, axis_name=('gx', 'gy'), pe...  30 us
    all_to_all x1, blocking collectives, on_device(): lax.all_to_all(turned.reshape(rows, cy, cz), 'gy', 0, 0, tiled=True)  24.8 us
    all_to_all x1, waiting for transfers between devices, on_device(): lax.all_to_all(section.reshape(rows, cy, cz), 'gy', 0, 0, tiled=True)  20.5 us
    ppermute x2, starting transfers between devices, routed(): lax.switch(q, [functools.partial(lax.ppermute, axis_name=('gx', 'gy'), pe...  11.9 us
    all_to_all x1, starting transfers between devices, on_device(): lax.all_to_all(section.reshape(rows, cy, cz), 'gy', 0, 0, tiled=True)  10.1 us
    pallas_call x1, Pallas kernels, on_device(): pl.pallas_call(functools.partial(rates_kernel, total_y=total_y, total_z=t...  7.18 us
    pallas_call x1, Pallas kernels, on_device(): pl.pallas_call(finish_kernel, grid=(steps,), out_shape=(struct(problems,...  5.82 us
    ppermute x1, waiting for transfers between devices, on_device(): lax.ppermute(z, 'gz', zup)  5.28 us
  transfers between devices with their start and end apart: 9, of which 4 were waited for; matrix products, arithmetic and copies ran while one was open for 2% of the time, Pallas kernels for 0%

profile of v2, /device:TPU:1, one launch (start us, length us, event | category | flops | bytes accessed | tf_op | source)
XLA Modules:
  0.0 130.8 jit_solution(9229874038098532761)
XLA Ops:
  0.6 0.0 copy-start.5
  0.6 7.2 %shard_map.167 = (f32[8,3,8,16,128]{4,3,2,1,0:T(8,128)}, f32[1152,128]{1,0:T(8,128)S(1)}, f32[1152,128]{1,0:T(8,128)}, f32[8,3,3,8,128]{4,3,2,1,0:T(8,128)}, f32...) custom-call(s32[2]{0:T(128)} %freq_ref.1, s32[2]{0:T(128)} %shift_ref.3, ...), custom_call_target="tpu_custom_call" | custom-call | tf_op jit(solution)/shard_map/pallas_call | solution.py:302
  7.8 0.7 collective-permute-start.32
  8.5 1.5 %collective-permute-start.33 = (f32[8,3,3,8,128]{4,3,2,1,0:T(8,128)}, f32[8,3,3,8,128]{4,3,2,1,0:T(8,128)S(1)}, u32[]{:S(2)}, u32[]{:S(2)}) collective-permute-start(f32[8,3,3,8,128]{4,3,2,1,0:T(8,128)} %get-tuple-element.88), channel_id=1, source_target_pairs={{0,60},{4,0},{8,4},{12,8},{16,12},{20,16},{24,20},{28,24},{32,28},... | collective-permute-start | bytes 884744 | tf_op jit(solution)/shard_map/ppermute | solution.py:330
  10.0 1.3 collective-permute-start.34
  11.3 3.8 %collective-permute-start.35 = (f32[8,3,8,128]{3,2,1,0:T(8,128)}, f32[8,3,8,128]{3,2,1,0:T(8,128)S(1)}, u32[]{:S(2)}, u32[]{:S(2)}) collective-permute-start(f32[8,3,8,128]{3,2,1,0:T(8,128)} %get-tuple-element.90), channel_id=1, source_target_pairs={{0,3},{1,0},{2,1},{3,2},{4,7},{5,4},{6,5},{7,6},{8,11},{9,8},{10,9... | collective-permute-start | bytes 294920 | tf_op jit(solution)/shard_map/ppermute | solution.py:331
  15.7 21.8 %conditional.2 = (f32[1152,128]{1,0:T(8,128)}) conditional(s32[]{:T(128)} %bitcast, f32[1152,128]{1,0:T(8,128)S(1)} %get-tuple-element.86, f32[1152,128]{1,0:T(8,128)S(1)} %get-tuple-element.86, f32[1152,128]{1,0:T(8,128)S(1)} %get-tuple-element.86, f32[1152,128]{1,0:T(8,128)S(1)} %get-tuple-element.86, ...), branch_computations={%region_0.0_spmd, %region_1.0_spmd, %region_2.0_spmd, %region_3.0_... | conditional | bytes 2359344 | solution.py:327
  15.8 9.1 %collective-permute-start.10 = (f32[1152,128]{1,0:T(8,128)S(1)}, f32[1152,128]{1,0:T(8,128)}, u32[]{:S(2)}, u32[]{:S(2)}) collective-permute-start(f32[1152,128]{1,0:T(8,128)S(1)} %param.10), channel_id=1, source_target_pairs={{40,64},{44,68},{48,72},{52,76},{56,80},{60,84},{0,88},{4,92},{8,9... | collective-permute-start | bytes 1769480 | tf_op jit(solution)/shard_map/cond/branch_10_fun/ppermute | solution.py:327
  24.8 12.7 %collective-permute-done.10 = f32[1152,128]{1,0:T(8,128)} collective-permute-done((f32[1152,128]{1,0:T(8,128)S(1)}, f32[1152,128]{1,0:T(8,128)}, u32[]{:S(2)}, u32[]{:S(2)}) %collective-permute-start.10) | collective-permute-done | bytes 589856 | tf_op jit(solution)/shard_map/cond/branch_10_fun/ppermute | solution.py:327
  37.5 0.0 collective-permute-start.36
  37.5 0.0 collective-permute-done.35.zup_ref
  37.6 5.3 %collective-permute-done.36.zdown_ref = f32[8,3,8,128]{3,2,1,0:T(8,128)S(1)} collective-permute-done((f32[8,3,8,128]{3,2,1,0:T(8,128)}, f32[8,3,8,128]{3,2,1,0:T(8,128)S(1)}, u32[]{:S(2)}, u32[]{:S(2)}) %collective-permute-start.36) | collective-permute-done | bytes 98336 | tf_op jit(solution)/shard_map/ppermute | solution.py:331
  42.8 0.0 collective-permute-done.33.y0_ref
  42.8 0.0 collective-permute-done.34.y1_ref
  42.9 0.0 copy-start.2
  42.9 0.0 collective-permute-done.32
  42.9 0.7 collective-permute-start.37
  43.6 0.0 copy-done.5
  44.3 1.2 fusion
  45.4 20.3 %conditional.3 = (f32[1152,128]{1,0:T(8,128)}) conditional(s32[]{:T(128)} %bitcast.1, f32[1152,128]{1,0:T(8,128)S(1)} %bitcast.21, f32[1152,128]{1,0:T(8,128)S(1)} %bitcast.22, f32[1152,128]{1,0:T(8,128)S(1)} %bitcast.23, f32[1152,128]{1,0:T(8,128)S(1)} %bitcast.24, f32[1152,128]{1,0:T(8,128)S(1)} %bitcast.25, ...), branch_computations={%region_16.17_spmd, %region_17.18_spmd, %region_18.19_spmd, %regio... | conditional | bytes 2359344 | solution.py:327
  45.7 2.8 %collective-permute-start.29 = (f32[1152,128]{1,0:T(8,128)S(1)}, f32[1152,128]{1,0:T(8,128)}, u32[]{:S(2)}, u32[]{:S(2)}) collective-permute-start(f32[1152,128]{1,0:T(8,128)S(1)} %param.29), channel_id=1, source_target_pairs={{116,0},{120,4},{124,8},{64,12},{68,16},{72,20},{76,24},{80,28},{8... | collective-permute-start | bytes 1769480 | tf_op jit(solution)/shard_map/cond/branch_13_fun/ppermute | solution.py:327
  48.5 17.3 %collective-permute-done.29 = f32[1152,128]{1,0:T(8,128)} collective-permute-done((f32[1152,128]{1,0:T(8,128)S(1)}, f32[1152,128]{1,0:T(8,128)}, u32[]{:S(2)}, u32[]{:S(2)}) %collective-permute-start.29) | collective-permute-done | bytes 589856 | tf_op jit(solution)/shard_map/cond/branch_13_fun/ppermute | solution.py:327
  65.7 0.0 collective-permute-done.37.follow_ref
  65.7 0.0 copy-done.3
  65.8 0.8 copy-done
  66.5 5.8 %shard_map.168 = (f32[8,3,8,16,128]{4,3,2,1,0:T(8,128)}, f32[8,24,16,128]{3,2,1,0:T(8,128)}) custom-call(s32[2]{0:T(128)} %shift_ref.3, f32[8,3,8,16,128]{4,3,2,1,0:T(8,128)} %m_ref.3, f32[8,3,8,16,128]{4,3,2,1,0:T(8,128)} %get-tuple-element.84.local_ref, f32[1152,128]{1,0:T(8,128)} %get-tuple-element.100.x0_ref, f32[1152,128]{1,0:T(8,128)} %copy-done, ...), custom_call_target="tpu_custom_call" | custom-call | tf_op jit(solution)/shard_map/pallas_call | solution.py:340
  72.4 10.1 %all-to-all-start = ((f32[192,16,128]{2,1,0:T(8,128)}), f32[192,16,128]{2,1,0:T(8,128)S(1)}, u32[]{:S(2)}, u32[]{:S(2)}) async-start(f32[192,16,128]{2,1,0:T(8,128)} %bitcast.17), calls=%async_computation | async-start | bytes 3145728 | tf_op jit(solution)/shard_map/all_to_all | solution.py:354
  82.4 1.0 dynamic-slice_bitcast_fusion.table_ref
  83.4 20.5 %all-to-all-done = f32[192,16,128]{2,1,0:T(8,128)S(1)} async-done(((f32[192,16,128]{2,1,0:T(8,128)}), f32[192,16,128]{2,1,0:T(8,128)S(1)}, u32[]{:S(2)}, u32[]{:S(2)}) %all-to-all-start) | async-done | bytes 1572896 | tf_op jit(solution)/shard_map/all_to_all | solution.py:354
  103.9 0.8 shard_map.169
  104.7 24.8 %all_to_all.10 = f32[192,16,128]{2,1,0:T(8,128)S(1)} all-to-all(f32[192,16,128]{2,1,0:T(8,128)S(1)} %bitcast.16), channel_id=1, replica_groups=mesh['gx'=2,'gy'=16,'gz'=4] {'gy'}, dimensions={0} | all-to-all | bytes 3145728 | tf_op jit(solution)/shard_map/all_to_all | solution.py:359
  129.6 1.2 shard_map.170
  (7 shorter events, 0.0 us)
Async XLA Ops:
  0.6 43.0 %copy-start.5 = (s32[2]{0:T(128)S(1)}, s32[2]{0:T(128)}, u32[]{:S(2)}) copy-start(s32[2]{0:T(128)} %shift_ref.3) | copy-start | bytes 28
  7.8 35.0 %collective-permute-start.32 = (f32[1152,128]{1,0:T(8,128)}, f32[1152,128]{1,0:T(8,128)S(1)}, u32[]{:S(2)}, u32[]{:S(2)}) collective-permute-start(f32[1152,128]{1,0:T(8,128)} %get-tuple-element.87), channel_id=1, source_target_pairs={{68,64},{72,68},{76,72},{80,76},{84,80},{88,84},{92,88},{96,92},{1... | collective-permute-start | bytes 1769480 | tf_op jit(solution)/shard_map/ppermute | solution.py:330
  8.5 34.3 %collective-permute-start.33 = (f32[8,3,3,8,128]{4,3,2,1,0:T(8,128)}, f32[8,3,3,8,128]{4,3,2,1,0:T(8,128)S(1)}, u32[]{:S(2)}, u32[]{:S(2)}) collective-permute-start(f32[8,3,3,8,128]{4,3,2,1,0:T(8,128)} %get-tuple-element.88), channel_id=1, source_target_pairs={{0,60},{4,0},{8,4},{12,8},{16,12},{20,16},{24,20},{28,24},{32,28},... | collective-permute-start | bytes 884744 | tf_op jit(solution)/shard_map/ppermute | solution.py:330
  10.0 32.8 %collective-permute-start.34 = (f32[8,3,3,8,128]{4,3,2,1,0:T(8,128)}, f32[8,3,3,8,128]{4,3,2,1,0:T(8,128)S(1)}, u32[]{:S(2)}, u32[]{:S(2)}) collective-permute-start(f32[8,3,3,8,128]{4,3,2,1,0:T(8,128)} %get-tuple-element.89), channel_id=1, source_target_pairs={{0,4},{4,8},{8,12},{12,16},{16,20},{20,24},{24,28},{28,32},{32,36}... | collective-permute-start | bytes 884744 | tf_op jit(solution)/shard_map/ppermute | solution.py:330
  11.3 26.3 %collective-permute-start.35 = (f32[8,3,8,128]{3,2,1,0:T(8,128)}, f32[8,3,8,128]{3,2,1,0:T(8,128)S(1)}, u32[]{:S(2)}, u32[]{:S(2)}) collective-permute-start(f32[8,3,8,128]{3,2,1,0:T(8,128)} %get-tuple-element.90), channel_id=1, source_target_pairs={{0,3},{1,0},{2,1},{3,2},{4,7},{5,4},{6,5},{7,6},{8,11},{9,8},{10,9... | collective-permute-start | bytes 294920 | tf_op jit(solution)/shard_map/ppermute | solution.py:331
  15.8 21.8 %collective-permute-start.10 = (f32[1152,128]{1,0:T(8,128)S(1)}, f32[1152,128]{1,0:T(8,128)}, u32[]{:S(2)}, u32[]{:S(2)}) collective-permute-start(f32[1152,128]{1,0:T(8,128)S(1)} %param.10), channel_id=1, source_target_pairs={{40,64},{44,68},{48,72},{52,76},{56,80},{60,84},{0,88},{4,92},{8,9... | collective-permute-start | bytes 1769480 | tf_op jit(solution)/shard_map/cond/branch_10_fun/ppermute | solution.py:327
  37.5 5.3 %collective-permute-start.36 = (f32[8,3,8,128]{3,2,1,0:T(8,128)}, f32[8,3,8,128]{3,2,1,0:T(8,128)S(1)}, u32[]{:S(2)}, u32[]{:S(2)}) collective-permute-start(f32[8,3,8,128]{3,2,1,0:T(8,128)} %get-tuple-element.90), channel_id=1, source_target_pairs={{0,1},{1,2},{2,3},{3,0},{4,5},{5,6},{6,7},{7,4},{8,9},{9,10},{10,1... | collective-permute-start | bytes 294920 | tf_op jit(solution)/shard_map/ppermute | solution.py:331
  37.6 28.2 %copy-start.3 = (f32[8,3,8,128]{3,2,1,0:T(8,128)}, f32[8,3,8,128]{3,2,1,0:T(8,128)S(1)}, u32[]{:S(2)}) copy-start(f32[8,3,8,128]{3,2,1,0:T(8,128)S(1)} %collective-permute-done.35.zup_ref) | copy-start | bytes 294916
  42.8 22.9 %copy-start.4 = (f32[8,3,8,128]{3,2,1,0:T(8,128)}, f32[8,3,8,128]{3,2,1,0:T(8,128)S(1)}, u32[]{:S(2)}) copy-start(f32[8,3,8,128]{3,2,1,0:T(8,128)S(1)} %collective-permute-done.36.zdown_ref) | copy-start | bytes 294916
  42.8 22.9 %copy-start.1 = (f32[8,3,3,8,128]{4,3,2,1,0:T(8,128)}, f32[8,3,3,8,128]{4,3,2,1,0:T(8,128)S(1)}, u32[]{:S(2)}) copy-start(f32[8,3,3,8,128]{4,3,2,1,0:T(8,128)S(1)} %collective-permute-done.33.y0_ref) | copy-start | bytes 884740
  42.9 22.9 %copy-start.2 = (f32[8,3,3,8,128]{4,3,2,1,0:T(8,128)}, f32[8,3,3,8,128]{4,3,2,1,0:T(8,128)S(1)}, u32[]{:S(2)}) copy-start(f32[8,3,3,8,128]{4,3,2,1,0:T(8,128)S(1)} %collective-permute-done.34.y1_ref) | copy-start | bytes 884740
  42.9 22.9 %collective-permute-start.37 = (f32[1152,128]{1,0:T(8,128)}, f32[1152,128]{1,0:T(8,128)S(1)}, u32[]{:S(2)}, u32[]{:S(2)}) collective-permute-start(f32[1152,128]{1,0:T(8,128)} %get-tuple-element.100.x0_ref), channel_id=1, source_target_pairs={{68,64},{72,68},{76,72},{80,76},{84,80},{88,84},{92,88},{96,92},{1... | collective-permute-start | bytes 1769480 | tf_op jit(solution)/shard_map/ppermute | solution.py:334
  45.7 20.1 %collective-permute-start.29 = (f32[1152,128]{1,0:T(8,128)S(1)}, f32[1152,128]{1,0:T(8,128)}, u32[]{:S(2)}, u32[]{:S(2)}) collective-permute-start(f32[1152,128]{1,0:T(8,128)S(1)} %param.29), channel_id=1, source_target_pairs={{116,0},{120,4},{124,8},{64,12},{68,16},{72,20},{76,24},{80,28},{8... | collective-permute-start | bytes 1769480 | tf_op jit(solution)/shard_map/cond/branch_13_fun/ppermute | solution.py:327
  65.7 0.8 copy-start
  72.4 31.6 %all-to-all-start = ((f32[192,16,128]{2,1,0:T(8,128)}), f32[192,16,128]{2,1,0:T(8,128)S(1)}, u32[]{:S(2)}, u32[]{:S(2)}) async-start(f32[192,16,128]{2,1,0:T(8,128)} %bitcast.17), calls=%async_computation | async-start | bytes 3145728 | tf_op jit(solution)/shard_map/all_to_all | solution.py:354

commit v3 on v2

--- a/solution.py
+++ b/solution.py
@@ -121,14 +121,12 @@
     return high, low
 
 
-def rates_kernel(freq_ref, shift_ref, m_ref, v_ref, lx_ref, ly_ref, lz_ref, rx_ref, ry_ref, rz_ref, fx_ref, fy_ref, fz_ref,
-                 rate_ref, x0_ref, x1_ref, y0_ref, y1_ref, z_ref, low_ref, high_ref, *, total_y, total_z):
+def rates_kernel(freq_ref, m_ref, v_ref, lx_ref, ly_ref, lz_ref, rx_ref, ry_ref, rz_ref, fx_ref, fy_ref, fz_ref,
+                 rate_ref, facing_ref, outer_ref, y0_ref, y1_ref, z_ref, *, total_z):
     pair, comps, cx, cy, cz = m_ref.shape
-    low_ref[0] = ((total_y - shift_ref[1]) & (total_y - 1)) // cy
-    high_ref[0] = shift_ref[0] // cy
     cells = cx * cy
-    planes = x0_ref.shape[0] // cy
-    p = pl.program_id(0) * pair
+    side = 3 * cy
+    on_left = lax.axis_index("gx") == 0
 
     def wide(parts):
         return jnp.concatenate(parts, 1)
@@ -179,11 +177,11 @@
             rate = main_left[:, lanes] + right[i * cells:(i + 1) * cells]
             rate_ref[i, c] = rate.reshape(cx, cy, cz)
             z_ref[i, c] = ghost[:, i * cells:(i + 1) * cells]
-            at = cells
-            for ref in (x0_ref, x1_ref):
-                for j in range(3):
-                    ref[pl.ds((p + i) * comps * 3 + c * 3 + j, cy, stride=planes), :] = left[at:at + cy, lanes]
-                    at += cy
+            low = left[cells:cells + side, lanes].reshape(3, cy, cz)
+            high = left[cells + side:cells + 2 * side, lanes].reshape(3, cy, cz)
+            facing_ref[i, c] = jnp.where(on_left, high, low)
+            outer_ref[i, c] = jnp.where(on_left, low, high)
+            at = cells + 2 * side
             for ref in (y0_ref, y1_ref):
                 ref[i, c] = left[at:at + 3 * cx, lanes].reshape(3, cx, cz)
                 at += 3 * cx
@@ -211,20 +209,25 @@
             np.concatenate([right] * 3, 0).astype(ml_dtypes.bfloat16))
 
 
-def finish_kernel(shift_ref, m_ref, local_ref, x0_ref, follow_ref, x1_ref, y0_ref, y1_ref, zup_ref, zdown_ref,
-                  left_ref, right_ref, rate_ref, section_ref, joined_ref):
+FIRST = ((0, 1, 2, 6), (5, 6, 7, 3))
+SECOND = ((3, 4, 5, 7), (0, 1, 2, 4))
+
+
+def plane_slot(x, on_left):
+    where = []
+    for half in range(2):
+        if x in FIRST[half]:
+            where.append((FIRST[half].index(x), 0))
+        else:
+            where.append((SECOND[half].index(x), 3))
+    return tuple(jnp.where(on_left, a, b) for a, b in zip(*where))
+
+
+def finish_kernel(m_ref, local_ref, facing_ref, outer_ref, y0_ref, y1_ref, zup_ref, zdown_ref, left_ref, right_ref,
+                  rate_ref, lines_ref):
     pair, comps, cx, cy, cz = m_ref.shape
     cells = cx * cy
-    half = x0_ref.shape[0]
-    planes = half // cy
-    step = pl.program_id(0)
-
-    @pl.when(step == 0)
-    def _():
-        joined_ref[0:half] = x0_ref[...]
-        joined_ref[half:] = follow_ref[...]
-
-    first = jnp.where(lax.axis_index("gx") == 1, (cy - (shift_ref[1] & (cy - 1))) & (cy - 1), 0) * planes
+    on_left = lax.axis_index("gx") == 0
     zrow = lax.broadcasted_iota(jnp.int32, (8, cells), 0)
     for i in range(pair):
         ghosts = jnp.concatenate([jnp.where(zrow < 3, zup_ref[i, c], zdown_ref[i, c]) for c in range(comps)], 0)
@@ -235,36 +238,61 @@
         placed = jnp.dot(left_ref[...], jnp.concatenate(three(faces), 0), preferred_element_type=F32)
         placed = placed + lax.dot_general(ghosts, right_ref[...], (((0,), (0,)), ((), ())), preferred_element_type=F32)
         for c in range(comps):
-            k = (step * pair + i) * comps * 3 + c * 3
             spread = placed[:, c * cz:(c + 1) * cz].reshape(cx, cy, cz)
             for x in range(cx):
                 value = local_ref[i, c, x] + spread[x]
                 if x < 3:
-                    value = value + x1_ref[pl.ds(k + x, cy, stride=planes), :]
+                    value = value + jnp.where(on_left, 0.0, facing_ref[i, c, x])
                 if x >= cx - 3:
-                    value = value + joined_ref[pl.ds(first + k + x - (cx - 3), cy, stride=planes), :]
+                    value = value + jnp.where(on_left, facing_ref[i, c, x - (cx - 3)], 0.0)
                 rate_ref[i, c, x] = value
-                section_ref[x, i * comps + c] = m_ref[i, c, x] + SECTION_WEIGHT * value
-
-
-def shift_kernel(data_ref, table_ref, out_ref):
-    blocks, rows, cy, cz = data_ref.shape
+                k, row = plane_slot(x, on_left)
+                lines_ref[k, i, row + c] = m_ref[i, c, x] + SECTION_WEIGHT * value
+            for j in range(3):
+                lines_ref[j, i, 6 + c] = outer_ref[i, c, j]
+            lines_ref[3, i, 6 + c] = jnp.zeros((cy, cz), F32)
+
+
+def shift_kernel(shift_ref, data_ref, table_ref, out_ref, twice_ref):
+    halves, blocks, rows, cy, cz = data_ref.shape
     total = blocks * cy
-    high = table_ref[:, :total]
-    low = table_ref[:, total:]
-    for row in range(0, rows, 2):
-        data = jnp.concatenate([data_ref[:, r].reshape(total, cz) for r in (row, row + 1)], 1)
-        dh, dl = split(data)
-        out = (jnp.dot(high, dh, preferred_element_type=F32) + jnp.dot(high, dl, preferred_element_type=F32)
-               + jnp.dot(low, dh, preferred_element_type=F32))
-        out_ref[:, row] = out[:, :cz].reshape(blocks, cy, cz)
-        out_ref[:, row + 1] = out[:, cz:].reshape(blocks, cy, cz)
-
-
-def reorder_kernel(in_ref, out_ref):
-    cx, rows = in_ref.shape[:2]
+    for half in range(halves):
+        first = shift_ref[0] if half == 0 else (total - shift_ref[1]) & (total - 1)
+        rolled = []
+        for c in range(3):
+            sums = data_ref[1 - half, :, 6 + c].reshape(total, cz)
+            twice_ref[0:total] = sums
+            twice_ref[total:2 * total] = sums
+            moved = twice_ref[pl.ds(first, total), :]
+            out_ref[half, :, 6 + c] = moved.reshape(blocks, cy, cz)
+            rolled.append(moved)
+        for group in range(2):
+            data = [data_ref[half, :, 3 * group + c].reshape(total, cz) for c in range(3)]
+            if group == 0:
+                data = [d + SECTION_WEIGHT * r for d, r in zip(data, rolled)]
+            dh, dl = split(jnp.concatenate(data, 1))
+            table = table_ref.at[2 * half + group]
+            high = table[:, :total]
+            low = table[:, total:]
+            out = (jnp.dot(high, dh, preferred_element_type=F32) + jnp.dot(high, dl, preferred_element_type=F32)
+                   + jnp.dot(low, dh, preferred_element_type=F32))
+            for c in range(3):
+                out_ref[half, :, 3 * group + c] = out[:, c * cz:(c + 1) * cz].reshape(blocks, cy, cz)
+
+
+def reorder_kernel(lines_ref, local_ref, rate_ref, out_ref):
+    problems, comps, cx, cy, cz = local_ref.shape
+    on_left = lax.axis_index("gx") == 0
     for x in range(cx):
-        out_ref[:, x] = in_ref[x]
+        k, row = plane_slot(x, on_left)
+        for c in range(comps):
+            out_ref[:, c, x] = lines_ref[k, :, row + c]
+            value = local_ref[:, c, x]
+            if x < 3:
+                value = value + jnp.where(on_left, lines_ref[x, :, 6 + c], 0.0)
+            if x >= cx - 3:
+                value = value + jnp.where(on_left, 0.0, lines_ref[x - (cx - 3), :, 6 + c])
+            rate_ref[:, c, x] = value
 
 
 def struct(*shape):
@@ -285,7 +313,6 @@
     lefts = [jnp.asarray(w) for w in left_weights(cx, cy)]
     mains, faces = right_weights(cz)
     mains, faces = [jnp.asarray(w) for w in mains], [jnp.asarray(w) for w in faces]
-    planes = problems * comps * 3
     pair = 2
     steps = problems // pair
 
@@ -295,73 +322,54 @@
     def cut(*shape):
         return pl.BlockSpec((pair,) + shape, lambda i: (i,) + (0,) * len(shape))
 
-    tile, edge, side = (comps, cx, cy, cz), (comps, 3, cx, cz), (comps, 8, cx * cy)
-    faces_x = struct(cy * planes, cz)
+    tile, face, edge, side = (comps, cx, cy, cz), (comps, 3, cy, cz), (comps, 3, cx, cz), (comps, 8, cx * cy)
     weights = [*lefts, *mains, *faces]
-    index = jax.ShapeDtypeStruct((1,), jnp.int32)
-    local, x0, x1, y0, y1, z, low_step, high_step = pl.pallas_call(
-        functools.partial(rates_kernel, total_y=total_y, total_z=total_z),
+    outs = (tile, face, face, edge, edge, side)
+    local, facing, outer, y0, y1, z = pl.pallas_call(
+        functools.partial(rates_kernel, total_z=total_z),
         grid=(steps,),
-        out_shape=(struct(problems, *tile), faces_x, faces_x, struct(problems, *edge), struct(problems, *edge),
-                   struct(problems, *side), index, index),
-        in_specs=[SMEM, SMEM, cut(*tile), whole(velocity)] + [whole(w) for w in weights],
-        out_specs=(cut(*tile), whole(faces_x), whole(faces_x), cut(*edge), cut(*edge), cut(*side), SMEM, SMEM),
+        out_shape=tuple(struct(problems, *shape) for shape in outs),
+        in_specs=[SMEM, cut(*tile), whole(velocity)] + [whole(w) for w in weights],
+        out_specs=tuple(cut(*shape) for shape in outs),
         compiler_params=STREAMED,
-    )(freq_index, shear_shift, magnetic, velocity, *weights)
-
-    def at(x, y):
-        return (x % nx) * ny + y % ny
-
+    )(freq_index, magnetic, velocity, *weights)
+
+    swap = [(0, 1), (1, 0)]
     down = [(j, (j - 1) % ny) for j in range(ny)]
     up = [(j, (j + 1) % ny) for j in range(ny)]
     zdown = [(j, (j - 1) % nz) for j in range(nz)]
     zup = [(j, (j + 1) % nz) for j in range(nz)]
-    follow = [(at(1, j + 1), at(1, j)) for j in range(ny)]
-    def towards_low(q):
-        return [(at(0, j + q), at(1, j)) for j in range(ny)] + [(at(1, j), at(0, j)) for j in range(ny)]
-
-    def towards_high(q):
-        return [(at(1, j + q), at(0, j)) for j in range(ny)] + [(at(0, j), at(1, j)) for j in range(ny)]
-
-    def routed(q, route, value):
-        return lax.switch(q, [functools.partial(lax.ppermute, axis_name=("gx", "gy"), perm=route(i)) for i in range(ny)],
-                          value)
-
-    beside = (lax.ppermute(x1, ("gx", "gy"), follow), lax.ppermute(y0, "gy", down), lax.ppermute(y1, "gy", up),
-              lax.ppermute(z, "gz", zdown), lax.ppermute(z, "gz", zup))
-    x0_in = routed(low_step[0], towards_low, x0)
-    x0_in, x1_next, y0_in, y1_in, z_up, z_down = lax.optimization_barrier((x0_in, *beside))
-    x0_next = lax.ppermute(x0_in, ("gx", "gy"), follow)
-    start = jnp.where(gx == 1, shear_shift[0] & (cy - 1), 0)
-    x1_rows = lax.dynamic_slice_in_dim(
-        jnp.concatenate([x1.reshape(cy, planes, cz), x1_next.reshape(cy, planes, cz)], 0), start, cy, 0)
-    x1_in = routed(high_step[0], towards_high, x1_rows.reshape(cy * planes, cz))
+    facing_in = lax.ppermute(facing, "gx", swap)
+    y0_in = lax.ppermute(y0, "gy", down)
+    y1_in = lax.ppermute(y1, "gy", up)
+    z_up = lax.ppermute(z, "gz", zdown)
+    z_down = lax.ppermute(z, "gz", zup)
     placing = [jnp.asarray(w) for w in place_weights(cx, cy, cz, comps)]
-    rate, section = pl.pallas_call(
+    groups = nx * ny // problems
+    rate, lines = pl.pallas_call(
         finish_kernel,
         grid=(steps,),
-        out_shape=(struct(problems, *tile), struct(cx, problems * comps, cy, cz)),
-        in_specs=[SMEM, cut(*tile), cut(*tile)] + [whole(faces_x)] * 3
-        + [cut(*edge)] * 2 + [cut(*side)] * 2 + [whole(w) for w in placing],
-        out_specs=(cut(*tile), pl.BlockSpec((cx, pair * comps, cy, cz), lambda i: (0, i, 0, 0))),
-        scratch_shapes=[pltpu.VMEM((2 * cy * planes, cz), F32)],
+        out_shape=(struct(problems, *tile), struct(groups, problems, 9, cy, cz)),
+        in_specs=[cut(*tile), cut(*tile), cut(*face), cut(*face), cut(*edge), cut(*edge), cut(*side), cut(*side)]
+        + [whole(w) for w in placing],
+        out_specs=(cut(*tile), pl.BlockSpec((groups, pair, 9, cy, cz), lambda i: (0, i, 0, 0, 0))),
         compiler_params=STREAMED,
-    )(shear_shift, magnetic, local, x0_in, x0_next, x1_in, y0_in, y1_in, z_up, z_down, *placing)
-
-    rows = cx * problems * comps
-    tables = jnp.asarray(shift_matrices(total_x, total_y))
-    table = lax.dynamic_index_in_dim(tables, gx * cx + gy * (rows // ny) // (problems * comps), 0, keepdims=False)
-    pencil = lax.all_to_all(section.reshape(rows, cy, cz), "gy", 0, 0, tiled=True)
+    )(magnetic, local, facing_in, outer, y0_in, y1_in, z_up, z_down, *placing)
+
+    matrices = shift_matrices(total_x, total_y)
+    order = [[half * cx + planes[half][k] for half in range(2) for planes in (FIRST, SECOND)] for k in range(groups)]
+    tables = jnp.asarray(np.stack([matrices[picks] for picks in order]))
+    table = lax.dynamic_index_in_dim(tables, (gx * ny + gy) // problems, 0, keepdims=False)
+    received = lax.all_to_all(lines.reshape(nx * ny * 9, cy, cz), ("gx", "gy"), 0, 0, tiled=True)
     turned = pl.pallas_call(
-        shift_kernel, out_shape=struct(ny, rows // ny, cy, cz), in_specs=[VMEM] * 2, out_specs=VMEM,
+        shift_kernel, out_shape=struct(nx, ny, 9, cy, cz), in_specs=[SMEM, VMEM, VMEM], out_specs=VMEM,
+        scratch_shapes=[pltpu.VMEM((2 * total_y, cz), F32)], compiler_params=PARAMS,
+    )(shear_shift, received.reshape(nx, ny, 9, cy, cz), table)
+    returned = lax.all_to_all(turned.reshape(nx * ny * 9, cy, cz), ("gx", "gy"), 0, 0, tiled=True)
+    return pl.pallas_call(
+        reorder_kernel, out_shape=(struct(problems, *tile),) * 2, in_specs=[VMEM] * 2, out_specs=(VMEM,) * 2,
         compiler_params=PARAMS,
-    )(pencil.reshape(ny, rows // ny, cy, cz), table)
-    returned = lax.all_to_all(turned.reshape(rows, cy, cz), "gy", 0, 0, tiled=True)
-    advanced = pl.pallas_call(
-        reorder_kernel, out_shape=struct(problems * comps, cx, cy, cz), in_specs=[VMEM], out_specs=VMEM,
-        compiler_params=PARAMS,
-    )(returned.reshape(cx, problems * comps, cy, cz))
-    return rate, advanced.reshape(magnetic.shape)
+    )(returned.reshape(groups, problems, 9, cy, cz), rate)
 
 
 def solution(mesh):

time: 129 us -> 114 us (0.88); the launches traced: 131 us -> 114 us
  waiting for transfers between devices: 55.8 us -> 39.7 us
  blocking collectives: 24.8 us -> 36.9 us
  starting transfers between devices: 29.9 us -> 18 us
  Pallas kernels: 15 us -> 16.4 us
  between operations: 2.11 us -> 0.72 us
    ppermute x8 -> x5, waiting for transfers between devices: 35.3 us -> 10.3 us  [the longest x1 5.12 us: on_device(): facing_in = lax.ppermute(facing, 'gx', swap)]
    all_to_all x1, blocking collectives: 24.8 us -> 36.9 us  [on_device(): lax.all_to_all(turned.reshape(nx * ny * 9, cy, cz), ('gx', 'gy'), 0, 0, t...]
    ppermute x8 -> x5, starting transfers between devices: 19.8 us -> 9.64 us  [the longest x1 3.82 us: on_device(): facing_in = lax.ppermute(facing, 'gx', swap)]
    all_to_all x1, waiting for transfers between devices: 20.5 us -> 29.4 us  [on_device(): lax.all_to_all(lines.reshape(nx * ny * 9, cy, cz), ('gx', 'gy'), 0, 0, ti...]
    all_to_all x1, starting transfers between devices: 10.1 us -> 8.39 us  [on_device(): lax.all_to_all(lines.reshape(nx * ny * 9, cy, cz), ('gx', 'gy'), 0, 0, ti...]
    pallas_call x3, Pallas kernels: 9.22 us -> 10.8 us  [the longest x1 7.17 us: on_device(): pl.pallas_call(functools.partial(rates_kernel, total_z=total_z), grid=(st...]
  transfers between devices with their start and end apart: 9 -> 6, of which waited for: 4 -> 4; matrix products, arithmetic and copies ran while one was open for 2% -> 1% of each run, Pallas kernels for 0% -> 0%
where the time goes in v3:
time: 114 us
  waiting for transfers between devices  39.7 us (35%)
  blocking collectives  36.9 us (32%)
  starting transfers between devices  18 us (16%)
  Pallas kernels  16.4 us (14%)
  local copies, waits for them, and re-layouts  2.11 us (2%)
    all_to_all x1, blocking collectives, on_device(): lax.all_to_all(turned.reshape(nx * ny * 9, cy, cz), ('gx', 'gy'), 0, 0, t...  36.9 us
    all_to_all x1, waiting for transfers between devices, on_device(): lax.all_to_all(lines.reshape(nx * ny * 9, cy, cz), ('gx', 'gy'), 0, 0, ti...  29.4 us
    all_to_all x1, starting transfers between devices, on_device(): lax.all_to_all(lines.reshape(nx * ny * 9, cy, cz), ('gx', 'gy'), 0, 0, ti...  8.39 us
    pallas_call x1, Pallas kernels, on_device(): pl.pallas_call(functools.partial(rates_kernel, total_z=total_z), grid=(st...  7.17 us
    pallas_call x1, Pallas kernels, on_device(): pl.pallas_call(finish_kernel, grid=(steps,), out_shape=(struct(problems,...  5.56 us
    ppermute x1, waiting for transfers between devices, on_device(): facing_in = lax.ppermute(facing, 'gx', swap)  5.12 us
    ppermute x1, starting transfers between devices, on_device(): facing_in = lax.ppermute(facing, 'gx', swap)  3.82 us
    ppermute x1, starting transfers between devices, on_device(): z_up = lax.ppermute(z, 'gz', zdown)  3.76 us
  transfers between devices with their start and end apart: 6, of which 4 were waited for; matrix products, arithmetic and copies ran while one was open for 1% of the time, Pallas kernels for 0%

profile of v3, /device:TPU:1, one launch (start us, length us, event | category | flops | bytes accessed | tf_op | source)
XLA Modules:
  0.0 113.9 jit_solution(17924684557674192173)
XLA Ops:
  0.6 7.2 %shard_map.167 = (f32[8,3,8,16,128]{4,3,2,1,0:T(8,128)}, f32[8,3,3,16,128]{4,3,2,1,0:T(8,128)}, f32[8,3,3,16,128]{4,3,2,1,0:T(8,128)}, f32[8,3,3,8,128]{4,3,2,1,...) custom-call(s32[2]{0:T(128)} %freq_ref.1, f32[8,3,8,16,128]{4,3,2,1,0:T(8,128)} %m_ref.3, ...), custom_call_target="tpu_custom_call" | custom-call | tf_op jit(solution)/shard_map/pallas_call | solution.py:328
  7.8 3.8 %collective-permute-start = (f32[8,3,3,16,128]{4,3,2,1,0:T(8,128)}, f32[8,3,3,16,128]{4,3,2,1,0:T(8,128)S(1)}, u32[]{:S(2)}, u32[]{:S(2)}) collective-permute-start(f32[8,3,3,16,128]{4,3,2,1,0:T(8,128)} %get-tuple-element.11), channel_id=1, source_target_pairs={{0,64},{64,0},{1,65},{65,1},{2,66},{66,2},{3,67},{67,3},{4,68},{68... | collective-permute-start | bytes 1769480 | tf_op jit(solution)/shard_map/ppermute | solution.py:342
  11.6 1.0 collective-permute-start.1
  12.6 1.1 collective-permute-start.2
  13.7 3.8 %collective-permute-start.3 = (f32[8,3,8,128]{3,2,1,0:T(8,128)}, f32[8,3,8,128]{3,2,1,0:T(8,128)S(1)}, u32[]{:S(2)}, u32[]{:S(2)}) collective-permute-start(f32[8,3,8,128]{3,2,1,0:T(8,128)} %get-tuple-element.15), channel_id=1, source_target_pairs={{0,3},{1,0},{2,1},{3,2},{4,7},{5,4},{6,5},{7,6},{8,11},{9,8},{10,9... | collective-permute-start | bytes 294920 | tf_op jit(solution)/shard_map/ppermute | solution.py:345
  17.4 0.0 collective-permute-start.4
  17.4 2.0 %collective-permute-done.3.zup_ref = f32[8,3,8,128]{3,2,1,0:T(8,128)S(1)} collective-permute-done((f32[8,3,8,128]{3,2,1,0:T(8,128)}, f32[8,3,8,128]{3,2,1,0:T(8,128)S(1)}, u32[]{:S(2)}, u32[]{:S(2)}) %collective-permute-start.3) | collective-permute-done | bytes 98336 | tf_op jit(solution)/shard_map/ppermute | solution.py:345
  19.4 0.0 copy-start.5
  19.4 3.2 %collective-permute-done.4.zdown_ref = f32[8,3,8,128]{3,2,1,0:T(8,128)S(1)} collective-permute-done((f32[8,3,8,128]{3,2,1,0:T(8,128)}, f32[8,3,8,128]{3,2,1,0:T(8,128)S(1)}, u32[]{:S(2)}, u32[]{:S(2)}) %collective-permute-start.4) | collective-permute-done | bytes 98336 | tf_op jit(solution)/shard_map/ppermute | solution.py:346
  22.6 0.0 copy-start.6
  22.6 0.0 collective-permute-done.1.y0_ref
  22.6 0.0 copy-start.3
  22.6 0.0 collective-permute-done.2.y1_ref
  22.6 0.0 copy-start.4
  22.6 5.1 %collective-permute-done.facing_ref = f32[8,3,3,16,128]{4,3,2,1,0:T(8,128)S(1)} collective-permute-done((f32[8,3,3,16,128]{4,3,2,1,0:T(8,128)}, f32[8,3,3,16,128]{4,3,2,1,0:T(8,128)S(1)}, u32[]{:S(2)}, u32[]{:S(2)}) %collective-permute-start) | collective-permute-done | bytes 589856 | tf_op jit(solution)/shard_map/ppermute | solution.py:342
  27.8 0.0 copy-start.2
  27.8 0.0 copy-done.5
  27.8 0.0 copy-done.6
  27.8 0.0 copy-done.3
  27.8 0.0 copy-done.4
  27.8 0.8 copy-done.2
  28.6 5.6 %shard_map.168 = (f32[8,3,8,16,128]{4,3,2,1,0:T(8,128)}, f32[4,8,9,16,128]{4,3,2,1,0:T(8,128)}) custom-call(f32[8,3,8,16,128]{4,3,2,1,0:T(8,128)} %m_ref.3, f32[8,3,8,16,128]{4,3,2,1,0:T(8,128)} %get-tuple-element.10.local_ref, f32[8,3,3,16,128]{4,3,2,1,0:T(8,128)} %copy-done.2, f32[8,3,3,16,128]{4,3,2,1,0:T(8,128)} %get-tuple-element.12.outer_ref, ...), custom_call_target="tpu_custom_call" | custom-call | tf_op jit(solution)/shard_map/pallas_call | solution.py:349
  34.1 0.0 copy-start.1
  34.1 8.4 %all-to-all-start = ((f32[288,16,128]{2,1,0:T(8,128)}), f32[288,16,128]{2,1,0:T(8,128)S(1)}, u32[]{:S(2)}, u32[]{:S(2)}) async-start(f32[288,16,128]{2,1,0:T(8,128)} %bitcast.9), calls=%async_computation | async-start | bytes 4718592 | tf_op jit(solution)/shard_map/all_to_all | solution.py:363
  42.6 1.3 %dynamic-slice_bitcast_fusion.table_ref = bf16[4,256,512]{2,1,0:T(8,128)(2,1)S(1)} fusion(bf16[4,4,256,512]{3,2,1,0:T(8,128)(2,1)} %constant.70.clone, s32[]{:T(128)S(6)} %select_n.10), kind=kLoop, calls=%fused_computation | loop fusion | bytes 2097156 | tf_op jit(solution)/shard_map/jit(dynamic_index_in_dim)/squeeze | solution.py:362
  43.9 29.4 %all-to-all-done = f32[288,16,128]{2,1,0:T(8,128)S(1)} async-done(((f32[288,16,128]{2,1,0:T(8,128)}), f32[288,16,128]{2,1,0:T(8,128)S(1)}, u32[]{:S(2)}, u32[]{:S(2)}) %all-to-all-start) | async-done | bytes 2359328 | tf_op jit(solution)/shard_map/all_to_all | solution.py:363
  73.3 0.0 copy-done.1
  73.3 1.7 %shard_map.169 = f32[2,16,9,16,128]{4,3,2,1,0:T(8,128)S(1)} custom-call(s32[2]{0:T(128)S(1)} %copy-done.1, f32[2,16,9,16,128]{4,3,2,1,0:T(8,128)S(1)} %bitcast.6, bf16[4,256,512]{2,1,0:T(8,128)(2,1)S(1)} %dynamic-slice_bitcast_fusion.table_ref), custom_call_target="tpu_custom_call" | custom-call | tf_op jit(solution)/shard_map/pallas_call | solution.py:364
  75.0 0.0 copy-start
  75.0 36.9 %all_to_all.10 = f32[288,16,128]{2,1,0:T(8,128)S(1)} all-to-all(f32[288,16,128]{2,1,0:T(8,128)S(1)} %bitcast.8), channel_id=1, replica_groups=mesh['gx'=2,'gy'=16,'gz'=4] {'gx','gy'}, dimensions={0} | all-to-all | bytes 4718592 | tf_op jit(solution)/shard_map/all_to_all | solution.py:368
  111.9 0.0 copy-done
  111.9 2.0 %shard_map.170 = (f32[8,3,8,16,128]{4,3,2,1,0:T(8,128)}, f32[8,3,8,16,128]{4,3,2,1,0:T(8,128)}) custom-call(f32[4,8,9,16,128]{4,3,2,1,0:T(8,128)S(1)} %bitcast.7, f32[8,3,8,16,128]{4,3,2,1,0:T(8,128)S(1)} %copy-done), custom_call_target="tpu_custom_call" | custom-call | tf_op jit(solution)/shard_map/pallas_call | solution.py:369
Async XLA Ops:
  7.8 20.0 %collective-permute-start = (f32[8,3,3,16,128]{4,3,2,1,0:T(8,128)}, f32[8,3,3,16,128]{4,3,2,1,0:T(8,128)S(1)}, u32[]{:S(2)}, u32[]{:S(2)}) collective-permute-start(f32[8,3,3,16,128]{4,3,2,1,0:T(8,128)} %get-tuple-element.11), channel_id=1, source_target_pairs={{0,64},{64,0},{1,65},{65,1},{2,66},{66,2},{3,67},{67,3},{4,68},{68... | collective-permute-start | bytes 1769480 | tf_op jit(solution)/shard_map/ppermute | solution.py:342
  11.6 11.0 %collective-permute-start.1 = (f32[8,3,3,8,128]{4,3,2,1,0:T(8,128)}, f32[8,3,3,8,128]{4,3,2,1,0:T(8,128)S(1)}, u32[]{:S(2)}, u32[]{:S(2)}) collective-permute-start(f32[8,3,3,8,128]{4,3,2,1,0:T(8,128)} %get-tuple-element.13), channel_id=1, source_target_pairs={{0,60},{4,0},{8,4},{12,8},{16,12},{20,16},{24,20},{28,24},{32,28},... | collective-permute-start | bytes 884744 | tf_op jit(solution)/shard_map/ppermute | solution.py:343
  12.6 10.1 %collective-permute-start.2 = (f32[8,3,3,8,128]{4,3,2,1,0:T(8,128)}, f32[8,3,3,8,128]{4,3,2,1,0:T(8,128)S(1)}, u32[]{:S(2)}, u32[]{:S(2)}) collective-permute-start(f32[8,3,3,8,128]{4,3,2,1,0:T(8,128)} %get-tuple-element.14), channel_id=1, source_target_pairs={{0,4},{4,8},{8,12},{12,16},{16,20},{20,24},{24,28},{28,32},{32,36}... | collective-permute-start | bytes 884744 | tf_op jit(solution)/shard_map/ppermute | solution.py:344
  13.7 5.7 %collective-permute-start.3 = (f32[8,3,8,128]{3,2,1,0:T(8,128)}, f32[8,3,8,128]{3,2,1,0:T(8,128)S(1)}, u32[]{:S(2)}, u32[]{:S(2)}) collective-permute-start(f32[8,3,8,128]{3,2,1,0:T(8,128)} %get-tuple-element.15), channel_id=1, source_target_pairs={{0,3},{1,0},{2,1},{3,2},{4,7},{5,4},{6,5},{7,6},{8,11},{9,8},{10,9... | collective-permute-start | bytes 294920 | tf_op jit(solution)/shard_map/ppermute | solution.py:345
  17.4 5.2 %collective-permute-start.4 = (f32[8,3,8,128]{3,2,1,0:T(8,128)}, f32[8,3,8,128]{3,2,1,0:T(8,128)S(1)}, u32[]{:S(2)}, u32[]{:S(2)}) collective-permute-start(f32[8,3,8,128]{3,2,1,0:T(8,128)} %get-tuple-element.15), channel_id=1, source_target_pairs={{0,1},{1,2},{2,3},{3,0},{4,5},{5,6},{6,7},{7,4},{8,9},{9,10},{10,1... | collective-permute-start | bytes 294920 | tf_op jit(solution)/shard_map/ppermute | solution.py:346
  19.4 8.4 %copy-start.5 = (f32[8,3,8,128]{3,2,1,0:T(8,128)}, f32[8,3,8,128]{3,2,1,0:T(8,128)S(1)}, u32[]{:S(2)}) copy-start(f32[8,3,8,128]{3,2,1,0:T(8,128)S(1)} %collective-permute-done.3.zup_ref) | copy-start | bytes 294916
  22.6 5.2 %copy-start.6 = (f32[8,3,8,128]{3,2,1,0:T(8,128)}, f32[8,3,8,128]{3,2,1,0:T(8,128)S(1)}, u32[]{:S(2)}) copy-start(f32[8,3,8,128]{3,2,1,0:T(8,128)S(1)} %collective-permute-done.4.zdown_ref) | copy-start | bytes 294916
  22.6 5.2 %copy-start.3 = (f32[8,3,3,8,128]{4,3,2,1,0:T(8,128)}, f32[8,3,3,8,128]{4,3,2,1,0:T(8,128)S(1)}, u32[]{:S(2)}) copy-start(f32[8,3,3,8,128]{4,3,2,1,0:T(8,128)S(1)} %collective-permute-done.1.y0_ref) | copy-start | bytes 884740
  22.6 5.2 %copy-start.4 = (f32[8,3,3,8,128]{4,3,2,1,0:T(8,128)}, f32[8,3,3,8,128]{4,3,2,1,0:T(8,128)S(1)}, u32[]{:S(2)}) copy-start(f32[8,3,3,8,128]{4,3,2,1,0:T(8,128)S(1)} %collective-permute-done.2.y1_ref) | copy-start | bytes 884740
  27.8 0.8 copy-start.2
  34.1 39.2 %copy-start.1 = (s32[2]{0:T(128)S(1)}, s32[2]{0:T(128)}, u32[]{:S(2)}) copy-start(s32[2]{0:T(128)} %shift_ref.1) | copy-start | bytes 28
  34.1 39.2 %all-to-all-start = ((f32[288,16,128]{2,1,0:T(8,128)}), f32[288,16,128]{2,1,0:T(8,128)S(1)}, u32[]{:S(2)}, u32[]{:S(2)}) async-start(f32[288,16,128]{2,1,0:T(8,128)} %bitcast.9), calls=%async_computation | async-start | bytes 4718592 | tf_op jit(solution)/shard_map/all_to_all | solution.py:363
  75.0 36.9 %copy-start = (f32[8,3,8,16,128]{4,3,2,1,0:T(8,128)S(1)}, f32[8,3,8,16,128]{4,3,2,1,0:T(8,128)}, u32[]{:S(2)}) copy-start(f32[8,3,8,16,128]{4,3,2,1,0:T(8,128)} %get-tuple-element.17.local_ref) | copy-start | bytes 4718596

commit v4 on v3

--- a/solution.py
+++ b/solution.py
@@ -52,22 +52,16 @@
     eye_x, eye_y = np.eye(cx), np.eye(cy)
     x1, x2 = stencil_1d(0, cx, cx, D2_CENTRE)
     y1, y2 = stencil_1d(0, cy, cy, D2_CENTRE)
-    xl1, xl2 = stencil_1d(-3, 3, cx, 0.0)
-    xh1, xh2 = stencil_1d(cx, 3, cx, 0.0)
     yl1, yl2 = stencil_1d(-3, 3, cy, 0.0)
     yh1, yh2 = stencil_1d(cy, 3, cy, 0.0)
 
     def face_y(rows):
         return np.einsum("iy,xz->ixzy", rows, eye_x).reshape(3 * cx, cx * cy)
 
-    none_x = np.zeros((3 * cy, cx * cy))
-    none_y = np.zeros((3 * cx, cx * cy))
-    dx = np.concatenate([np.kron(x1, eye_y), np.kron(xl1, eye_y), np.kron(xh1, eye_y), none_y, none_y])
-    dy = np.concatenate([np.kron(eye_x, y1), none_x, none_x, face_y(yl1), face_y(yh1)])
-    lap = np.concatenate([
-        np.kron(x2, eye_y) + np.kron(eye_x, y2),
-        np.kron(xl2, eye_y), np.kron(xh2, eye_y), face_y(yl2), face_y(yh2),
-    ])
+    none = np.zeros((6 * cx, cx * cy))
+    dx = np.concatenate([np.kron(x1, eye_y), none])
+    dy = np.concatenate([np.kron(eye_x, y1), face_y(yl1), face_y(yh1)])
+    lap = np.concatenate([np.kron(x2, eye_y) + np.kron(eye_x, y2), face_y(yl2), face_y(yh2)])
     out_x = np.concatenate([dy, lap], 1)
     out_y = np.concatenate([-dx, lap], 1)
     out_z = np.concatenate([dx, -dy, lap], 1)
@@ -121,12 +115,87 @@
     return high, low
 
 
-def rates_kernel(freq_ref, m_ref, v_ref, lx_ref, ly_ref, lz_ref, rx_ref, ry_ref, rz_ref, fx_ref, fy_ref, fz_ref,
-                 rate_ref, facing_ref, outer_ref, y0_ref, y1_ref, z_ref, *, total_z):
+PAIR = 2
+
+
+def wave_pair(freq_ref, step, cz, total_z):
+    position = (lax.axis_index("gz") * cz + lax.broadcasted_iota(jnp.int32, (1, cz), 1)).astype(F32)
+    phase = 2.0 * math.pi * freq_ref[step // 2].astype(F32) * position / total_z
+    return (jnp.cos(phase), jnp.sin(phase)), step % 2 == 0
+
+
+def face_sums(m_ref, v_ref, waves, along_x, high, out_ref):
+    pair, comps, cx, cy, cz = m_ref.shape
+    sign = jnp.where(high, 1.0, -1.0)
+    near = [jnp.where(high, cx - 1 - j, j) for j in range(3)]
+    flow = [[v_ref[c, x] for c in range(3)] for x in near]
+    for i in range(pair):
+        add_x = jnp.where(along_x, waves[i], 0.0)
+        add_y = jnp.where(along_x, 0.0, waves[i])
+        field, turn_y, turn_z = [], [], []
+        for x, (vx, vy, vz) in zip(near, flow):
+            mx, my, mz = [m_ref[i, c, x] for c in range(3)]
+            tx, ty = mx + add_x, my + add_y
+            field.append((mx, my, mz))
+            turn_y.append(sign * (vz * tx - vx * mz))
+            turn_z.append(sign * (vx * ty - vy * tx))
+        for n in range(3):
+            out = [0.0, 0.0, 0.0]
+            for j in range(3 - n):
+                one, two = D1[n + j], D2[n + j]
+                out[0] += two * field[j][0]
+                out[1] += two * field[j][1] + one * turn_z[j]
+                out[2] += two * field[j][2] - one * turn_y[j]
+            at = jnp.where(high, n, 2 - n)
+            for c in range(3):
+                out_ref[i, c, at] = out[c]
+
+
+def block(ref, step):
+    return ref.at[pl.ds(step * PAIR, PAIR)]
+
+
+def facing_kernel(freq_ref, m_ref, v_ref, facing_ref, *, total_z):
+    @pl.loop(0, m_ref.shape[0] // PAIR)
+    def _(step):
+        waves, along_x = wave_pair(freq_ref, step, m_ref.shape[-1], total_z)
+        face_sums(block(m_ref, step), v_ref, waves, along_x, lax.axis_index("gx") == 0, block(facing_ref, step))
+
+
+def rates_kernel(freq_ref, m_ref, v_ref, left_ref, right_ref, face_ref, rate_ref, outer_ref, y0_ref, y1_ref, z_ref, *,
+                 total_z):
+    cells = m_ref.shape[2] * m_ref.shape[3]
+
+    def part(ref, dim, first, size):
+        at = [slice(None), slice(None)]
+        at[dim] = pl.ds(first, size)
+        return ref.at[tuple(at)]
+
+    first = 0
+    lefts = []
+    for size in (6 * cells, 6 * cells, 9 * cells):
+        lefts.append(part(left_ref, 1, first, size))
+        first += size
+    first = 0
+    cz = m_ref.shape[-1]
+    rights, faces = [], []
+    for size in (6 * cz, 6 * cz, 3 * cz):
+        rights.append(part(right_ref, 0, first, size))
+        faces.append(part(face_ref, 1, first, size))
+        first += size
+
+    @pl.loop(0, m_ref.shape[0] // PAIR)
+    def _(step):
+        pair_rates(step, freq_ref, block(m_ref, step), v_ref, *lefts, *rights, *faces,
+                   *[block(ref, step) for ref in (rate_ref, outer_ref, y0_ref, y1_ref, z_ref)], total_z=total_z)
+
+
+def pair_rates(step, freq_ref, m_ref, v_ref, lx_ref, ly_ref, lz_ref, rx_ref, ry_ref, rz_ref, fx_ref, fy_ref, fz_ref,
+               rate_ref, outer_ref, y0_ref, y1_ref, z_ref, *, total_z):
     pair, comps, cx, cy, cz = m_ref.shape
     cells = cx * cy
-    side = 3 * cy
-    on_left = lax.axis_index("gx") == 0
+    waves, along_x = wave_pair(freq_ref, step, cz, total_z)
+    face_sums(m_ref, v_ref, waves, along_x, lax.axis_index("gx") == 1, outer_ref)
 
     def wide(parts):
         return jnp.concatenate(parts, 1)
@@ -136,11 +205,7 @@
 
     m = [wide([m_ref[i, c].reshape(cells, cz) for i in range(pair)]) for c in range(3)]
     v = [wide([v_ref[c].reshape(cells, cz)] * pair) for c in range(3)]
-    step = pl.program_id(0)
-    position = (lax.axis_index("gz") * cz + lax.broadcasted_iota(jnp.int32, (1, cz), 1)).astype(F32)
-    phase = 2.0 * math.pi * freq_ref[step // 2].astype(F32) * position / total_z
-    wave = wide([jnp.cos(phase), jnp.sin(phase)])
-    along_x = step % 2 == 0
+    wave = wide(waves)
     tx = m[0] + jnp.where(along_x, wave, 0.0)
     ty = m[1] + jnp.where(along_x, 0.0, wave)
     tz = m[2]
@@ -177,11 +242,7 @@
             rate = main_left[:, lanes] + right[i * cells:(i + 1) * cells]
             rate_ref[i, c] = rate.reshape(cx, cy, cz)
             z_ref[i, c] = ghost[:, i * cells:(i + 1) * cells]
-            low = left[cells:cells + side, lanes].reshape(3, cy, cz)
-            high = left[cells + side:cells + 2 * side, lanes].reshape(3, cy, cz)
-            facing_ref[i, c] = jnp.where(on_left, high, low)
-            outer_ref[i, c] = jnp.where(on_left, low, high)
-            at = cells + 2 * side
+            at = cells
             for ref in (y0_ref, y1_ref):
                 ref[i, c] = left[at:at + 3 * cx, lanes].reshape(3, cx, cz)
                 at += 3 * cx
@@ -225,6 +286,15 @@
 
 def finish_kernel(m_ref, local_ref, facing_ref, outer_ref, y0_ref, y1_ref, zup_ref, zdown_ref, left_ref, right_ref,
                   rate_ref, lines_ref):
+    @pl.loop(0, m_ref.shape[0] // PAIR)
+    def _(step):
+        refs = (m_ref, local_ref, facing_ref, outer_ref, y0_ref, y1_ref, zup_ref, zdown_ref)
+        finish_pair(*[block(ref, step) for ref in refs], left_ref, right_ref, block(rate_ref, step),
+                    lines_ref.at[:, pl.ds(step * PAIR, PAIR)])
+
+
+def finish_pair(m_ref, local_ref, facing_ref, outer_ref, y0_ref, y1_ref, zup_ref, zdown_ref, left_ref, right_ref,
+                rate_ref, lines_ref):
     pair, comps, cx, cy, cz = m_ref.shape
     cells = cx * cy
     on_left = lax.axis_index("gx") == 0
@@ -301,8 +371,7 @@
 
 VMEM = pl.BlockSpec(memory_space=pltpu.VMEM)
 SMEM = pl.BlockSpec(memory_space=pltpu.SMEM)
-PARAMS = pltpu.CompilerParams(vmem_limit_bytes=40 * 1024 * 1024)
-STREAMED = pltpu.CompilerParams(vmem_limit_bytes=60 * 1024 * 1024)
+PARAMS = pltpu.CompilerParams(vmem_limit_bytes=32 * 1024 * 1024)
 
 
 def on_device(magnetic, velocity, shear_shift, freq_index):
@@ -310,28 +379,21 @@
     nx, ny, nz = lax.axis_size("gx"), lax.axis_size("gy"), lax.axis_size("gz")
     total_x, total_y, total_z = cx * nx, cy * ny, cz * nz
     gx, gy = lax.axis_index("gx"), lax.axis_index("gy")
-    lefts = [jnp.asarray(w) for w in left_weights(cx, cy)]
+    lefts = left_weights(cx, cy)
     mains, faces = right_weights(cz)
-    mains, faces = [jnp.asarray(w) for w in mains], [jnp.asarray(w) for w in faces]
-    pair = 2
-    steps = problems // pair
-
-    def whole(array):
-        return pl.BlockSpec(array.shape, lambda i: (0,) * len(array.shape))
-
-    def cut(*shape):
-        return pl.BlockSpec((pair,) + shape, lambda i: (i,) + (0,) * len(shape))
-
     tile, face, edge, side = (comps, cx, cy, cz), (comps, 3, cy, cz), (comps, 3, cx, cz), (comps, 8, cx * cy)
-    weights = [*lefts, *mains, *faces]
-    outs = (tile, face, face, edge, edge, side)
-    local, facing, outer, y0, y1, z = pl.pallas_call(
+    facing = pl.pallas_call(
+        functools.partial(facing_kernel, total_z=total_z),
+        out_shape=struct(problems, *face),
+        in_specs=[SMEM, VMEM, VMEM], out_specs=VMEM, compiler_params=PARAMS,
+    )(freq_index, magnetic, velocity)
+    weights = [jnp.asarray(np.concatenate(w, dim)) for w, dim in ((lefts, 1), (mains, 0), (faces, 1))]
+    outs = (tile, face, edge, edge, side)
+    local, outer, y0, y1, z = pl.pallas_call(
         functools.partial(rates_kernel, total_z=total_z),
-        grid=(steps,),
         out_shape=tuple(struct(problems, *shape) for shape in outs),
-        in_specs=[SMEM, cut(*tile), whole(velocity)] + [whole(w) for w in weights],
-        out_specs=tuple(cut(*shape) for shape in outs),
-        compiler_params=STREAMED,
+        in_specs=[SMEM] + [VMEM] * 5, out_specs=(VMEM,) * 5, compiler_params=PARAMS,
+        cost_estimate=pl.CostEstimate(flops=1 << 30, bytes_accessed=1 << 24, transcendentals=0),
     )(freq_index, magnetic, velocity, *weights)
 
     swap = [(0, 1), (1, 0)]
@@ -348,12 +410,8 @@
     groups = nx * ny // problems
     rate, lines = pl.pallas_call(
         finish_kernel,
-        grid=(steps,),
         out_shape=(struct(problems, *tile), struct(groups, problems, 9, cy, cz)),
-        in_specs=[cut(*tile), cut(*tile), cut(*face), cut(*face), cut(*edge), cut(*edge), cut(*side), cut(*side)]
-        + [whole(w) for w in placing],
-        out_specs=(cut(*tile), pl.BlockSpec((groups, pair, 9, cy, cz), lambda i: (0, i, 0, 0, 0))),
-        compiler_params=STREAMED,
+        in_specs=[VMEM] * 10, out_specs=(VMEM,) * 2, compiler_params=PARAMS,
     )(magnetic, local, facing_in, outer, y0_in, y1_in, z_up, z_down, *placing)
 
     matrices = shift_matrices(total_x, total_y)

time: 114 us -> 109 us (0.956)
  Pallas kernels: 16.4 us -> 10.6 us
  waiting for transfers between devices: 39.7 us -> 34.7 us
  local copies, waits for them, and re-layouts: 2.11 us -> 6.91 us
    pallas_call x2 -> x3, Pallas kernels: 12.7 us -> 6.97 us  [the longest x1 4.67 us: on_device(): pl.pallas_call(functools.partial(rates_kernel, total_z=total_z), out_shap...]
    ppermute x1, waiting for transfers between devices: 5.12 us -> 0.3 us  [on_device(): facing_in = lax.ppermute(facing, 'gx', swap)]
    unnamed x14 -> x30, local copies, waits for them, and re-layouts: 0.81 us -> 5.61 us
  transfers between devices with their start and end apart: 6 -> 6, of which waited for: 4 -> 4; matrix products, arithmetic and copies ran while one was open for 1% -> 1% of each run, Pallas kernels for 0% -> 4%
where the time goes in v4:
time: 109 us; the launch traced here: 108 us
  blocking collectives  36.9 us (34%)
  waiting for transfers between devices  34.7 us (32%)
  starting transfers between devices  18.3 us (17%)
  Pallas kernels  10.6 us (10%)
  local copies, waits for them, and re-layouts  6.91 us (6%)
    all_to_all x1, blocking collectives, on_device(): lax.all_to_all(turned.reshape(nx * ny * 9, cy, cz), ('gx', 'gy'), 0, 0, t...  36.9 us
    all_to_all x1, waiting for transfers between devices, on_device(): lax.all_to_all(lines.reshape(nx * ny * 9, cy, cz), ('gx', 'gy'), 0, 0, ti...  29.4 us
    all_to_all x1, starting transfers between devices, on_device(): lax.all_to_all(lines.reshape(nx * ny * 9, cy, cz), ('gx', 'gy'), 0, 0, ti...  8.51 us
    unnamed x30, local copies, waits for them, and re-layouts  5.61 us
    pallas_call x1, Pallas kernels, on_device(): pl.pallas_call(functools.partial(rates_kernel, total_z=total_z), out_shap...  4.67 us
    ppermute x1, starting transfers between devices, on_device(): facing_in = lax.ppermute(facing, 'gx', swap)  3.82 us
    ppermute x1, starting transfers between devices, on_device(): z_up = lax.ppermute(z, 'gz', zdown)  3.76 us
    ppermute x1, waiting for transfers between devices, on_device(): z_down = lax.ppermute(z, 'gz', zup)  3.33 us
  transfers between devices with their start and end apart: 6, of which 4 were waited for; matrix products, arithmetic and copies ran while one was open for 1% of the time, Pallas kernels for 4%

profile of v4, /device:TPU:1, one launch (start us, length us, event | category | flops | bytes accessed | tf_op | source)
XLA Modules:
  0.0 108.2 jit_solution(6749438307060129077)
XLA Ops:
  0.6 0.0 copy-start
  0.6 1.4 %copy-done = f32[8,3,8,16,128]{4,3,2,1,0:T(8,128)S(1)} copy-done((f32[8,3,8,16,128]{4,3,2,1,0:T(8,128)S(1)}, f32[8,3,8,16,128]{4,3,2,1,0:T(8,128)}, u32[]{:S(2)}) %copy-start) | copy-done | bytes 1572888
  2.0 0.9 copy-done.5
  3.0 0.7 copy-done.9
  3.6 0.0 copy-start.14
  3.6 1.0 shard_map.114
  4.6 0.0 copy-start.1
  4.6 0.0 copy-start.7
  4.6 0.0 copy-start.8
  4.6 3.8 %collective-permute-start = (f32[8,3,3,16,128]{4,3,2,1,0:T(8,128)S(1)}, f32[8,3,3,16,128]{4,3,2,1,0:T(8,128)S(1)}, u32[]{:S(2)}, u32[]{:S(2)}) collective-permute-start(f32[8,3,3,16,128]{4,3,2,1,0:T(8,128)S(1)} %shard_map.114), channel_id=1, source_target_pairs={{0,64},{64,0},{1,65},{65,1},{2,66},{66,2},{3,67},{67,3},{4,68},{68... | collective-permute-start | bytes 1769480 | tf_op jit(solution)/shard_map/ppermute | solution.py:404
  8.5 0.0 copy-done.13
  8.5 0.0 copy-done.14
  8.5 4.7 %shard_map.113 = (f32[8,3,8,16,128]{4,3,2,1,0:T(8,128)S(1)}, f32[8,3,3,16,128]{4,3,2,1,0:T(8,128)S(1)}, f32[8,3,3,8,128]{4,3,2,1,0:T(8,128)S(1)}, f32[8,3,3,8,128]{4,3,2,1,0:T(8,128)S(1)}, f32[8,3,8,128]{3,2,1,0:T(8,128)S(1)}) custom-call(s32[2]{0:T(128)S(1)} %copy-done.10, f32[8,3,8,16,128]{4,3,2,1,0:T(8,128)S(1)} %copy-done, ...), custom_call_target="tpu_custom_call" | custom-call | flops 1073741824 | bytes 16777216 | tf_op jit(solution)/shard_map/pallas_call | solution.py:392
  13.2 1.0 collective-permute-start.1
  14.2 1.2 %collective-permute-start.2 = (f32[8,3,3,8,128]{4,3,2,1,0:T(8,128)S(1)}, f32[8,3,3,8,128]{4,3,2,1,0:T(8,128)S(1)}, u32[]{:S(2)}, u32[]{:S(2)}) collective-permute-start(f32[8,3,3,8,128]{4,3,2,1,0:T(8,128)S(1)} %get-tuple-element.12), channel_id=1, source_target_pairs={{0,4},{4,8},{8,12},{12,16},{16,20},{20,24},{24,28},{28,32},{32,36}... | collective-permute-start | bytes 884744 | tf_op jit(solution)/shard_map/ppermute | solution.py:406
  15.4 3.8 %collective-permute-start.3 = (f32[8,3,8,128]{3,2,1,0:T(8,128)S(1)}, f32[8,3,8,128]{3,2,1,0:T(8,128)S(1)}, u32[]{:S(2)}, u32[]{:S(2)}) collective-permute-start(f32[8,3,8,128]{3,2,1,0:T(8,128)S(1)} %get-tuple-element.13), channel_id=1, source_target_pairs={{0,3},{1,0},{2,1},{3,2},{4,7},{5,4},{6,5},{7,6},{8,11},{9,8},{10,9... | collective-permute-start | bytes 294920 | tf_op jit(solution)/shard_map/ppermute | solution.py:407
  19.1 0.0 collective-permute-start.4
  19.1 1.6 %collective-permute-done.3.zup_ref = f32[8,3,8,128]{3,2,1,0:T(8,128)S(1)} collective-permute-done((f32[8,3,8,128]{3,2,1,0:T(8,128)S(1)}, f32[8,3,8,128]{3,2,1,0:T(8,128)S(1)}, u32[]{:S(2)}, u32[]{:S(2)}) %collective-permute-start.3) | collective-permute-done | bytes 98336 | tf_op jit(solution)/shard_map/ppermute | solution.py:407
  20.8 3.3 %collective-permute-done.4.zdown_ref = f32[8,3,8,128]{3,2,1,0:T(8,128)S(1)} collective-permute-done((f32[8,3,8,128]{3,2,1,0:T(8,128)S(1)}, f32[8,3,8,128]{3,2,1,0:T(8,128)S(1)}, u32[]{:S(2)}, u32[]{:S(2)}) %collective-permute-start.4) | collective-permute-done | bytes 98336 | tf_op jit(solution)/shard_map/ppermute | solution.py:408
  24.1 0.0 collective-permute-done.1.y0_ref
  24.1 0.0 collective-permute-done.2.y1_ref
  24.1 0.3 collective-permute-done.facing_ref
  24.4 1.4 %shard_map.115 = (f32[8,3,8,16,128]{4,3,2,1,0:T(8,128)S(1)}, f32[4,8,9,16,128]{4,3,2,1,0:T(8,128)S(1)}) custom-call(f32[8,3,8,16,128]{4,3,2,1,0:T(8,128)S(1)} %copy-done.1, f32[8,3,8,16,128]{4,3,2,1,0:T(8,128)S(1)} %get-tuple-element.9.local_ref, f32[8,3,3,16,128]{4,3,2,1,0:T(8,128)S(1)} %collective-permute-done.facing_ref, ...), custom_call_target="tpu_custom_call" | custom-call | tf_op jit(solution)/shard_map/pallas_call | solution.py:411
  25.8 1.4 %copy-done.2 = f32[4,8,9,16,128]{4,3,2,1,0:T(8,128)} copy-done((f32[4,8,9,16,128]{4,3,2,1,0:T(8,128)}, f32[4,8,9,16,128]{4,3,2,1,0:T(8,128)S(1)}, u32[]{:S(2)}) %copy-start.2) | copy-done | bytes 2359320
  27.2 1.1 %copy-done.3 = f32[8,3,8,16,128]{4,3,2,1,0:T(8,128)} copy-done((f32[8,3,8,16,128]{4,3,2,1,0:T(8,128)}, f32[8,3,8,16,128]{4,3,2,1,0:T(8,128)S(1)}, u32[]{:S(2)}) %copy-start.3) | copy-done | bytes 1572888
  28.4 8.5 %all-to-all-start = ((f32[288,16,128]{2,1,0:T(8,128)}), f32[288,16,128]{2,1,0:T(8,128)S(1)}, u32[]{:S(2)}, u32[]{:S(2)}) async-start(f32[288,16,128]{2,1,0:T(8,128)} %bitcast.9), calls=%async_computation | async-start | bytes 4718592 | tf_op jit(solution)/shard_map/all_to_all | solution.py:421
  36.9 1.3 %dynamic-slice_bitcast_fusion.table_ref = bf16[4,256,512]{2,1,0:T(8,128)(2,1)S(1)} fusion(bf16[4,4,256,512]{3,2,1,0:T(8,128)(2,1)} %constant.52.clone, s32[]{:T(128)S(6)} %select_n.10), kind=kLoop, calls=%fused_computation | loop fusion | bytes 2097156 | tf_op jit(solution)/shard_map/jit(dynamic_index_in_dim)/squeeze | solution.py:420
  38.2 29.4 %all-to-all-done = f32[288,16,128]{2,1,0:T(8,128)S(1)} async-done(((f32[288,16,128]{2,1,0:T(8,128)}), f32[288,16,128]{2,1,0:T(8,128)S(1)}, u32[]{:S(2)}, u32[]{:S(2)}) %all-to-all-start) | async-done | bytes 2359328 | tf_op jit(solution)/shard_map/all_to_all | solution.py:421
  67.6 1.7 %shard_map.116 = f32[2,16,9,16,128]{4,3,2,1,0:T(8,128)S(1)} custom-call(s32[2]{0:T(128)S(1)} %copy-done.11, f32[2,16,9,16,128]{4,3,2,1,0:T(8,128)S(1)} %bitcast.6, bf16[4,256,512]{2,1,0:T(8,128)(2,1)S(1)} %dynamic-slice_bitcast_fusion.table_ref), custom_call_target="tpu_custom_call" | custom-call | tf_op jit(solution)/shard_map/pallas_call | solution.py:422
  69.3 0.0 copy-start.4
  69.4 36.9 %all_to_all.10 = f32[288,16,128]{2,1,0:T(8,128)S(1)} all-to-all(f32[288,16,128]{2,1,0:T(8,128)S(1)} %bitcast.8), channel_id=1, replica_groups=mesh['gx'=2,'gy'=16,'gz'=4] {'gx','gy'}, dimensions={0} | all-to-all | bytes 4718592 | tf_op jit(solution)/shard_map/all_to_all | solution.py:426
  106.3 2.0 %shard_map.117 = (f32[8,3,8,16,128]{4,3,2,1,0:T(8,128)}, f32[8,3,8,16,128]{4,3,2,1,0:T(8,128)}) custom-call(f32[4,8,9,16,128]{4,3,2,1,0:T(8,128)S(1)} %bitcast.7, f32[8,3,8,16,128]{4,3,2,1,0:T(8,128)S(1)} %copy-done.4), custom_call_target="tpu_custom_call" | custom-call | tf_op jit(solution)/shard_map/pallas_call | solution.py:427
  (17 shorter events, 0.0 us)
Async XLA Ops:
  0.6 1.4 %copy-start = (f32[8,3,8,16,128]{4,3,2,1,0:T(8,128)S(1)}, f32[8,3,8,16,128]{4,3,2,1,0:T(8,128)}, u32[]{:S(2)}) copy-start(f32[8,3,8,16,128]{4,3,2,1,0:T(8,128)} %m_ref.5) | copy-start | bytes 4718596
  2.0 0.9 copy-start.5
  3.0 0.7 copy-start.9
  3.6 4.8 %copy-start.6 = (f32[3,8,16,128]{3,2,1,0:T(8,128)S(1)}, f32[3,8,16,128]{3,2,1,0:T(8,128)}, u32[]{:S(2)}) copy-start(f32[3,8,16,128]{3,2,1,0:T(8,128)} %v_ref.3) | copy-start | bytes 589828
  3.6 4.8 %copy-start.10 = (s32[2]{0:T(128)S(1)}, s32[2]{0:T(128)}, u32[]{:S(2)}) copy-start(s32[2]{0:T(128)} %freq_ref.3) | copy-start | bytes 28
  3.6 4.8 %copy-start.12 = (bf16[176,2688]{1,0:T(8,128)(2,1)S(1)}, bf16[176,2688]{1,0:T(8,128)(2,1)}, u32[]{:S(2)}) copy-start(bf16[176,2688]{1,0:T(8,128)(2,1)} %constant.47.clone.left_ref) | copy-start | bytes 2838532
  3.6 4.8 %copy-start.13 = (bf16[1920,128]{1,0:T(8,128)(2,1)S(1)}, bf16[1920,128]{1,0:T(8,128)(2,1)}, u32[]{:S(2)}) copy-start(bf16[1920,128]{1,0:T(8,128)(2,1)} %constant.48.clone.right_ref) | copy-start | bytes 1474564
  3.6 4.9 %copy-start.14 = (bf16[8,1920]{1,0:T(8,128)(2,1)S(1)}, bf16[8,1920]{1,0:T(8,128)(2,1)}, u32[]{:S(2)}) copy-start(bf16[8,1920]{1,0:T(8,128)(2,1)} %constant.49.clone.face_ref) | copy-start | bytes 92164
  4.6 19.8 %copy-start.1 = (f32[8,3,8,16,128]{4,3,2,1,0:T(8,128)S(1)}, f32[8,3,8,16,128]{4,3,2,1,0:T(8,128)}, u32[]{:S(2)}) copy-start(f32[8,3,8,16,128]{4,3,2,1,0:T(8,128)} %m_ref.5) | copy-start | bytes 4718596
  4.6 19.8 %copy-start.7 = (bf16[128,144]{1,0:T(8,128)(2,1)S(1)}, bf16[128,144]{1,0:T(8,128)(2,1)}, u32[]{:S(2)}) copy-start(bf16[128,144]{1,0:T(8,128)(2,1)} %constant.50.clone.left_ref) | copy-start | bytes 110596
  4.6 19.8 %copy-start.8 = (bf16[72,384]{1,0:T(8,128)(2,1)S(1)}, bf16[72,384]{1,0:T(8,128)(2,1)}, u32[]{:S(2)}) copy-start(bf16[72,384]{1,0:T(8,128)(2,1)} %constant.51.clone.right_ref) | copy-start | bytes 165892
  4.6 19.8 %collective-permute-start = (f32[8,3,3,16,128]{4,3,2,1,0:T(8,128)S(1)}, f32[8,3,3,16,128]{4,3,2,1,0:T(8,128)S(1)}, u32[]{:S(2)}, u32[]{:S(2)}) collective-permute-start(f32[8,3,3,16,128]{4,3,2,1,0:T(8,128)S(1)} %shard_map.114), channel_id=1, source_target_pairs={{0,64},{64,0},{1,65},{65,1},{2,66},{66,2},{3,67},{67,3},{4,68},{68... | collective-permute-start | bytes 1769480 | tf_op jit(solution)/shard_map/ppermute | solution.py:404
  13.2 10.9 %collective-permute-start.1 = (f32[8,3,3,8,128]{4,3,2,1,0:T(8,128)S(1)}, f32[8,3,3,8,128]{4,3,2,1,0:T(8,128)S(1)}, u32[]{:S(2)}, u32[]{:S(2)}) collective-permute-start(f32[8,3,3,8,128]{4,3,2,1,0:T(8,128)S(1)} %get-tuple-element.11), channel_id=1, source_target_pairs={{0,60},{4,0},{8,4},{12,8},{16,12},{20,16},{24,20},{28,24},{32,28},... | collective-permute-start | bytes 884744 | tf_op jit(solution)/shard_map/ppermute | solution.py:405
  14.2 9.9 %collective-permute-start.2 = (f32[8,3,3,8,128]{4,3,2,1,0:T(8,128)S(1)}, f32[8,3,3,8,128]{4,3,2,1,0:T(8,128)S(1)}, u32[]{:S(2)}, u32[]{:S(2)}) collective-permute-start(f32[8,3,3,8,128]{4,3,2,1,0:T(8,128)S(1)} %get-tuple-element.12), channel_id=1, source_target_pairs={{0,4},{4,8},{8,12},{12,16},{16,20},{20,24},{24,28},{28,32},{32,36}... | collective-permute-start | bytes 884744 | tf_op jit(solution)/shard_map/ppermute | solution.py:406
  15.4 5.4 %collective-permute-start.3 = (f32[8,3,8,128]{3,2,1,0:T(8,128)S(1)}, f32[8,3,8,128]{3,2,1,0:T(8,128)S(1)}, u32[]{:S(2)}, u32[]{:S(2)}) collective-permute-start(f32[8,3,8,128]{3,2,1,0:T(8,128)S(1)} %get-tuple-element.13), channel_id=1, source_target_pairs={{0,3},{1,0},{2,1},{3,2},{4,7},{5,4},{6,5},{7,6},{8,11},{9,8},{10,9... | collective-permute-start | bytes 294920 | tf_op jit(solution)/shard_map/ppermute | solution.py:407
  19.1 5.0 %collective-permute-start.4 = (f32[8,3,8,128]{3,2,1,0:T(8,128)S(1)}, f32[8,3,8,128]{3,2,1,0:T(8,128)S(1)}, u32[]{:S(2)}, u32[]{:S(2)}) collective-permute-start(f32[8,3,8,128]{3,2,1,0:T(8,128)S(1)} %get-tuple-element.13), channel_id=1, source_target_pairs={{0,1},{1,2},{2,3},{3,0},{4,5},{5,6},{6,7},{7,4},{8,9},{9,10},{10,1... | collective-permute-start | bytes 294920 | tf_op jit(solution)/shard_map/ppermute | solution.py:408
  25.8 1.4 %copy-start.2 = (f32[4,8,9,16,128]{4,3,2,1,0:T(8,128)}, f32[4,8,9,16,128]{4,3,2,1,0:T(8,128)S(1)}, u32[]{:S(2)}) copy-start(f32[4,8,9,16,128]{4,3,2,1,0:T(8,128)S(1)} %get-tuple-element.14) | copy-start | bytes 7077892
  27.2 1.1 %copy-start.3 = (f32[8,3,8,16,128]{4,3,2,1,0:T(8,128)}, f32[8,3,8,16,128]{4,3,2,1,0:T(8,128)S(1)}, u32[]{:S(2)}) copy-start(f32[8,3,8,16,128]{4,3,2,1,0:T(8,128)S(1)} %get-tuple-element.15.local_ref) | copy-start | bytes 4718596
  28.4 39.3 %copy-start.11 = (s32[2]{0:T(128)S(1)}, s32[2]{0:T(128)}, u32[]{:S(2)}) copy-start(s32[2]{0:T(128)} %shift_ref.1) | copy-start | bytes 28
  28.4 39.3 %all-to-all-start = ((f32[288,16,128]{2,1,0:T(8,128)}), f32[288,16,128]{2,1,0:T(8,128)S(1)}, u32[]{:S(2)}, u32[]{:S(2)}) async-start(f32[288,16,128]{2,1,0:T(8,128)} %bitcast.9), calls=%async_computation | async-start | bytes 4718592 | tf_op jit(solution)/shard_map/all_to_all | solution.py:421
  69.3 36.9 %copy-start.4 = (f32[8,3,8,16,128]{4,3,2,1,0:T(8,128)S(1)}, f32[8,3,8,16,128]{4,3,2,1,0:T(8,128)}, u32[]{:S(2)}) copy-start(f32[8,3,8,16,128]{4,3,2,1,0:T(8,128)} %copy-done.3) | copy-start | bytes 4718596

commit v5 on v4

--- a/solution.py
+++ b/solution.py
@@ -284,18 +284,25 @@
     return tuple(jnp.where(on_left, a, b) for a, b in zip(*where))
 
 
-def finish_kernel(m_ref, local_ref, facing_ref, outer_ref, y0_ref, y1_ref, zup_ref, zdown_ref, left_ref, right_ref,
-                  rate_ref, lines_ref):
+def lines_kernel(m_ref, local_ref, facing_ref, outer_ref, y0_ref, y1_ref, zup_ref, zdown_ref, left_ref, right_ref,
+                 lines_ref):
     @pl.loop(0, m_ref.shape[0] // PAIR)
     def _(step):
         refs = (m_ref, local_ref, facing_ref, outer_ref, y0_ref, y1_ref, zup_ref, zdown_ref)
-        finish_pair(*[block(ref, step) for ref in refs], left_ref, right_ref, block(rate_ref, step),
+        finish_pair(*[block(ref, step) for ref in refs], left_ref, right_ref, None,
                     lines_ref.at[:, pl.ds(step * PAIR, PAIR)])
+
+
+def section_rate_kernel(local_ref, facing_ref, y0_ref, y1_ref, zup_ref, zdown_ref, left_ref, right_ref, rate_ref):
+    @pl.loop(0, local_ref.shape[0] // PAIR)
+    def _(step):
+        local, facing, *edges = [block(ref, step) for ref in (local_ref, facing_ref, y0_ref, y1_ref, zup_ref, zdown_ref)]
+        finish_pair(None, local, facing, None, *edges, left_ref, right_ref, block(rate_ref, step), None)
 
 
 def finish_pair(m_ref, local_ref, facing_ref, outer_ref, y0_ref, y1_ref, zup_ref, zdown_ref, left_ref, right_ref,
                 rate_ref, lines_ref):
-    pair, comps, cx, cy, cz = m_ref.shape
+    pair, comps, cx, cy, cz = local_ref.shape
     cells = cx * cy
     on_left = lax.axis_index("gx") == 0
     zrow = lax.broadcasted_iota(jnp.int32, (8, cells), 0)
@@ -315,12 +322,15 @@
                     value = value + jnp.where(on_left, 0.0, facing_ref[i, c, x])
                 if x >= cx - 3:
                     value = value + jnp.where(on_left, facing_ref[i, c, x - (cx - 3)], 0.0)
-                rate_ref[i, c, x] = value
-                k, row = plane_slot(x, on_left)
-                lines_ref[k, i, row + c] = m_ref[i, c, x] + SECTION_WEIGHT * value
-            for j in range(3):
-                lines_ref[j, i, 6 + c] = outer_ref[i, c, j]
-            lines_ref[3, i, 6 + c] = jnp.zeros((cy, cz), F32)
+                if lines_ref is None:
+                    rate_ref[i, c, x] = value
+                else:
+                    k, row = plane_slot(x, on_left)
+                    lines_ref[k, i, row + c] = m_ref[i, c, x] + SECTION_WEIGHT * value
+            if lines_ref is not None:
+                for j in range(3):
+                    lines_ref[j, i, 6 + c] = outer_ref[i, c, j]
+                lines_ref[3, i, 6 + c] = jnp.zeros((cy, cz), F32)
 
 
 def shift_kernel(shift_ref, data_ref, table_ref, out_ref, twice_ref):
@@ -408,17 +418,22 @@
     z_down = lax.ppermute(z, "gz", zup)
     placing = [jnp.asarray(w) for w in place_weights(cx, cy, cz, comps)]
     groups = nx * ny // problems
-    rate, lines = pl.pallas_call(
-        finish_kernel,
-        out_shape=(struct(problems, *tile), struct(groups, problems, 9, cy, cz)),
-        in_specs=[VMEM] * 10, out_specs=(VMEM,) * 2, compiler_params=PARAMS,
+    lines = pl.pallas_call(
+        lines_kernel, out_shape=struct(groups, problems, 9, cy, cz),
+        in_specs=[VMEM] * 10, out_specs=VMEM, compiler_params=PARAMS,
     )(magnetic, local, facing_in, outer, y0_in, y1_in, z_up, z_down, *placing)
+    rate = pl.pallas_call(
+        section_rate_kernel, out_shape=struct(problems, *tile),
+        in_specs=[VMEM] * 8, out_specs=VMEM, compiler_params=PARAMS,
+        cost_estimate=pl.CostEstimate(flops=1 << 28, bytes_accessed=1 << 22, transcendentals=0),
+    )(local, facing_in, y0_in, y1_in, z_up, z_down, *placing)
 
     matrices = shift_matrices(total_x, total_y)
     order = [[half * cx + planes[half][k] for half in range(2) for planes in (FIRST, SECOND)] for k in range(groups)]
     tables = jnp.asarray(np.stack([matrices[picks] for picks in order]))
     table = lax.dynamic_index_in_dim(tables, (gx * ny + gy) // problems, 0, keepdims=False)
     received = lax.all_to_all(lines.reshape(nx * ny * 9, cy, cz), ("gx", "gy"), 0, 0, tiled=True)
+    received, rate = lax.optimization_barrier((received, rate))
     turned = pl.pallas_call(
         shift_kernel, out_shape=struct(nx, ny, 9, cy, cz), in_specs=[SMEM, VMEM, VMEM], out_specs=VMEM,
         scratch_shapes=[pltpu.VMEM((2 * total_y, cz), F32)], compiler_params=PARAMS,

time: 109 us -> 108 us (level)
  waiting for transfers between devices: 34.7 us -> 26.4 us
  local copies, waits for them, and re-layouts: 6.91 us -> 12.8 us
  Pallas kernels: 10.6 us -> 11.8 us
    all_to_all x1, waiting for transfers between devices: 29.4 us -> 21 us  [on_device(): lax.all_to_all(lines.reshape(nx * ny * 9, cy, cz), ('gx', 'gy'), 0, 0, ti...]
    unnamed x30 -> x50, local copies, waits for them, and re-layouts: 5.61 us -> 11.4 us
    pallas_call x1 -> x2, Pallas kernels: 1.35 us -> 2.66 us  [the longest x1 1.37 us: on_device(): pl.pallas_call(lines_kernel, out_shape=struct(groups, problems, 9, cy, cz...]
  transfers between devices with their start and end apart: 6 -> 6, of which waited for: 4 -> 4; matrix products, arithmetic and copies ran while one was open for 1% -> 1% of each run, Pallas kernels for 4% -> 5%
where the time goes in v5:
time: 108 us; the launch traced here: 107 us
  blocking collectives  36.9 us (34%)
  waiting for transfers between devices  26.4 us (24%)
  starting transfers between devices  18.2 us (17%)
  local copies, waits for them, and re-layouts  12.8 us (12%)
  Pallas kernels  11.8 us (11%)
    all_to_all x1, blocking collectives, on_device(): lax.all_to_all(turned.reshape(nx * ny * 9, cy, cz), ('gx', 'gy'), 0, 0, t...  36.9 us
    all_to_all x1, waiting for transfers between devices, on_device(): lax.all_to_all(lines.reshape(nx * ny * 9, cy, cz), ('gx', 'gy'), 0, 0, ti...  21 us
    unnamed x50, local copies, waits for them, and re-layouts  11.4 us
    all_to_all x1, starting transfers between devices, on_device(): lax.all_to_all(lines.reshape(nx * ny * 9, cy, cz), ('gx', 'gy'), 0, 0, ti...  8.38 us
    pallas_call x1, Pallas kernels, on_device(): pl.pallas_call(functools.partial(rates_kernel, total_z=total_z), out_shap...  4.56 us
    ppermute x1, starting transfers between devices, on_device(): facing_in = lax.ppermute(facing, 'gx', swap)  3.82 us
    ppermute x1, starting transfers between devices, on_device(): z_up = lax.ppermute(z, 'gz', zdown)  3.76 us
    ppermute x1, waiting for transfers between devices, on_device(): z_down = lax.ppermute(z, 'gz', zup)  3.33 us
  transfers between devices with their start and end apart: 6, of which 4 were waited for; matrix products, arithmetic and copies ran while one was open for 1% of the time, Pallas kernels for 5%

profile of v5, /device:TPU:1, one launch (start us, length us, event | category | flops | bytes accessed | tf_op | source)
XLA Modules:
  0.0 106.9 jit_solution(8986297942100009659)
XLA Ops:
  0.6 1.4 %copy-done.5 = f32[8,3,8,16,128]{4,3,2,1,0:T(8,128)S(1)} copy-done((f32[8,3,8,16,128]{4,3,2,1,0:T(8,128)S(1)}, f32[8,3,8,16,128]{4,3,2,1,0:T(8,128)}, u32[]{:S(2)}) %copy-start.5) | copy-done | bytes 1572888
  2.0 0.9 copy-done.19
  3.0 0.7 copy-done.20
  3.6 1.0 shard_map.114
  4.6 0.0 copy-start.6
  4.6 0.0 copy-start.15
  4.6 0.0 copy-start.17
  4.6 3.8 %collective-permute-start = (f32[8,3,3,16,128]{4,3,2,1,0:T(8,128)S(1)}, f32[8,3,3,16,128]{4,3,2,1,0:T(8,128)S(1)}, u32[]{:S(2)}, u32[]{:S(2)}) collective-permute-start(f32[8,3,3,16,128]{4,3,2,1,0:T(8,128)S(1)} %shard_map.114), channel_id=1, source_target_pairs={{0,64},{64,0},{1,65},{65,1},{2,66},{66,2},{3,67},{67,3},{4,68},{68... | collective-permute-start | bytes 1769480 | tf_op jit(solution)/shard_map/ppermute | solution.py:414
  8.5 4.6 %shard_map.113 = (f32[8,3,8,16,128]{4,3,2,1,0:T(8,128)S(1)}, f32[8,3,3,16,128]{4,3,2,1,0:T(8,128)S(1)}, f32[8,3,3,8,128]{4,3,2,1,0:T(8,128)S(1)}, f32[8,3,3,8,128]{4,3,2,1,0:T(8,128)S(1)}, f32[8,3,8,128]{3,2,1,0:T(8,128)S(1)}) custom-call(s32[2]{0:T(128)S(1)} %copy-done.20, f32[8,3,8,16,128]{4,3,2,1,0:T(8,128)S(1)} %copy-done.5, ...), custom_call_target="tpu_custom_call" | custom-call | flops 1073741824 | bytes 16777216 | tf_op jit(solution)/shard_map/pallas_call | solution.py:402
  13.0 1.0 collective-permute-start.1
  14.1 1.2 %collective-permute-start.2 = (f32[8,3,3,8,128]{4,3,2,1,0:T(8,128)S(1)}, f32[8,3,3,8,128]{4,3,2,1,0:T(8,128)S(1)}, u32[]{:S(2)}, u32[]{:S(2)}) collective-permute-start(f32[8,3,3,8,128]{4,3,2,1,0:T(8,128)S(1)} %get-tuple-element.12), channel_id=1, source_target_pairs={{0,4},{4,8},{8,12},{12,16},{16,20},{20,24},{24,28},{28,32},{32,36}... | collective-permute-start | bytes 884744 | tf_op jit(solution)/shard_map/ppermute | solution.py:416
  15.2 3.8 %collective-permute-start.3 = (f32[8,3,8,128]{3,2,1,0:T(8,128)S(1)}, f32[8,3,8,128]{3,2,1,0:T(8,128)S(1)}, u32[]{:S(2)}, u32[]{:S(2)}) collective-permute-start(f32[8,3,8,128]{3,2,1,0:T(8,128)S(1)} %get-tuple-element.13), channel_id=1, source_target_pairs={{0,3},{1,0},{2,1},{3,2},{4,7},{5,4},{6,5},{7,6},{8,11},{9,8},{10,9... | collective-permute-start | bytes 294920 | tf_op jit(solution)/shard_map/ppermute | solution.py:417
  19.0 1.6 %collective-permute-done.3.zup_ref = f32[8,3,8,128]{3,2,1,0:T(8,128)S(1)} collective-permute-done((f32[8,3,8,128]{3,2,1,0:T(8,128)S(1)}, f32[8,3,8,128]{3,2,1,0:T(8,128)S(1)}, u32[]{:S(2)}, u32[]{:S(2)}) %collective-permute-start.3) | collective-permute-done | bytes 98336 | tf_op jit(solution)/shard_map/ppermute | solution.py:417
  20.6 3.3 %collective-permute-done.4.zdown_ref = f32[8,3,8,128]{3,2,1,0:T(8,128)S(1)} collective-permute-done((f32[8,3,8,128]{3,2,1,0:T(8,128)S(1)}, f32[8,3,8,128]{3,2,1,0:T(8,128)S(1)}, u32[]{:S(2)}, u32[]{:S(2)}) %collective-permute-start.4) | collective-permute-done | bytes 98336 | tf_op jit(solution)/shard_map/ppermute | solution.py:418
  24.0 0.4 collective-permute-done.facing_ref
  24.4 1.4 %shard_map.115 = f32[4,8,9,16,128]{4,3,2,1,0:T(8,128)S(1)} custom-call(f32[8,3,8,16,128]{4,3,2,1,0:T(8,128)S(1)} %copy-done.6, f32[8,3,8,16,128]{4,3,2,1,0:T(8,128)S(1)} %get-tuple-element.9.local_ref, f32[8,3,3,16,128]{4,3,2,1,0:T(8,128)S(1)} %collective-permute-done.facing_ref, f32[8,3,3,16,128]{4,3,2,1,0:T(8,128)S(1)} %get-tuple-element.10.outer_ref, ...), custom_call_target="tpu_custom_call" | custom-call | tf_op jit(solution)/shard_map/pallas_call | solution.py:421
  25.8 1.4 %copy-done = f32[4,8,9,16,128]{4,3,2,1,0:T(8,128)} copy-done((f32[4,8,9,16,128]{4,3,2,1,0:T(8,128)}, f32[4,8,9,16,128]{4,3,2,1,0:T(8,128)S(1)}, u32[]{:S(2)}) %copy-start) | copy-done | bytes 2359320
  27.2 8.4 %all-to-all-start = ((f32[288,16,128]{2,1,0:T(8,128)}), f32[288,16,128]{2,1,0:T(8,128)S(1)}, u32[]{:S(2)}, u32[]{:S(2)}) async-start(f32[288,16,128]{2,1,0:T(8,128)} %bitcast.9), calls=%async_computation | async-start | bytes 4718592 | tf_op jit(solution)/shard_map/all_to_all | solution.py:435
  35.7 1.4 %dynamic-slice_bitcast_fusion.table_ref = bf16[4,256,512]{2,1,0:T(8,128)(2,1)S(1)} fusion(bf16[4,4,256,512]{3,2,1,0:T(8,128)(2,1)} %constant.52.clone, s32[]{:T(128)S(6)} %select_n.10), kind=kLoop, calls=%fused_computation | loop fusion | bytes 2097156 | tf_op jit(solution)/shard_map/jit(dynamic_index_in_dim)/squeeze | solution.py:434
  37.1 0.3 copy-done.4
  37.4 1.1 copy-done.8
  38.4 1.0 copy-done.10
  39.4 1.0 copy-done.12
  40.4 0.9 copy-done.14
  41.3 0.8 copy-done.16
  42.1 0.8 copy-done.18
  42.9 1.3 %shard_map.116.local_ref = f32[8,3,8,16,128]{4,3,2,1,0:T(8,128)S(1)} custom-call(f32[8,3,8,16,128]{4,3,2,1,0:T(8,128)S(1)} %copy-done.4, f32[8,3,3,16,128]{4,3,2,1,0:T(8,128)S(1)} %copy-done.8, f32[8,3,3,8,128]{4,3,2,1,0:T(8,128)S(1)} %copy-done.10, f32[8,3,3,8,128]{4,3,2,1,0:T(8,128)S(1)} %copy-done.12, ...), custom_call_target="tpu_custom_call" | custom-call | flops 268435456 | bytes 4194304 | tf_op jit(solution)/shard_map/pallas_call | solution.py:425
  44.2 1.1 %copy-done.1 = f32[8,3,8,16,128]{4,3,2,1,0:T(8,128)} copy-done((f32[8,3,8,16,128]{4,3,2,1,0:T(8,128)}, f32[8,3,8,16,128]{4,3,2,1,0:T(8,128)S(1)}, u32[]{:S(2)}) %copy-start.1) | copy-done | bytes 1572888
  45.4 21.0 %all-to-all-done = f32[288,16,128]{2,1,0:T(8,128)S(1)} async-done(((f32[288,16,128]{2,1,0:T(8,128)}), f32[288,16,128]{2,1,0:T(8,128)S(1)}, u32[]{:S(2)}, u32[]{:S(2)}) %all-to-all-start) | async-done | bytes 2359328 | tf_op jit(solution)/shard_map/all_to_all | solution.py:435
  66.4 1.7 %shard_map.117 = f32[2,16,9,16,128]{4,3,2,1,0:T(8,128)S(1)} custom-call(s32[2]{0:T(128)S(1)} %copy-done.21, f32[2,16,9,16,128]{4,3,2,1,0:T(8,128)S(1)} %bitcast.6, bf16[4,256,512]{2,1,0:T(8,128)(2,1)S(1)} %dynamic-slice_bitcast_fusion.table_ref), custom_call_target="tpu_custom_call" | custom-call | tf_op jit(solution)/shard_map/pallas_call | solution.py:437
  68.1 36.9 %all_to_all.10 = f32[288,16,128]{2,1,0:T(8,128)S(1)} all-to-all(f32[288,16,128]{2,1,0:T(8,128)S(1)} %bitcast.8), channel_id=1, replica_groups=mesh['gx'=2,'gy'=16,'gz'=4] {'gx','gy'}, dimensions={0} | all-to-all | bytes 4718592 | tf_op jit(solution)/shard_map/all_to_all | solution.py:441
  105.0 1.9 %shard_map.118 = (f32[8,3,8,16,128]{4,3,2,1,0:T(8,128)}, f32[8,3,8,16,128]{4,3,2,1,0:T(8,128)}) custom-call(f32[4,8,9,16,128]{4,3,2,1,0:T(8,128)S(1)} %bitcast.7, f32[8,3,8,16,128]{4,3,2,1,0:T(8,128)S(1)} %copy-done.2), custom_call_target="tpu_custom_call" | custom-call | tf_op jit(solution)/shard_map/pallas_call | solution.py:442
  (38 shorter events, 0.1 us)
Async XLA Ops:
  0.6 1.4 %copy-start.5 = (f32[8,3,8,16,128]{4,3,2,1,0:T(8,128)S(1)}, f32[8,3,8,16,128]{4,3,2,1,0:T(8,128)}, u32[]{:S(2)}) copy-start(f32[8,3,8,16,128]{4,3,2,1,0:T(8,128)} %m_ref.5) | copy-start | bytes 4718596
  2.0 0.9 copy-start.19
  3.0 0.7 copy-start.20
  3.6 4.8 %copy-start.22 = (bf16[176,2688]{1,0:T(8,128)(2,1)S(1)}, bf16[176,2688]{1,0:T(8,128)(2,1)}, u32[]{:S(2)}) copy-start(bf16[176,2688]{1,0:T(8,128)(2,1)} %constant.47.clone.left_ref) | copy-start | bytes 2838532
  3.6 4.8 %copy-start.23 = (bf16[1920,128]{1,0:T(8,128)(2,1)S(1)}, bf16[1920,128]{1,0:T(8,128)(2,1)}, u32[]{:S(2)}) copy-start(bf16[1920,128]{1,0:T(8,128)(2,1)} %constant.48.clone.right_ref) | copy-start | bytes 1474564
  3.6 4.8 %copy-start.24 = (bf16[8,1920]{1,0:T(8,128)(2,1)S(1)}, bf16[8,1920]{1,0:T(8,128)(2,1)}, u32[]{:S(2)}) copy-start(bf16[8,1920]{1,0:T(8,128)(2,1)} %constant.49.clone.face_ref) | copy-start | bytes 92164
  4.6 19.8 %copy-start.6 = (f32[8,3,8,16,128]{4,3,2,1,0:T(8,128)S(1)}, f32[8,3,8,16,128]{4,3,2,1,0:T(8,128)}, u32[]{:S(2)}) copy-start(f32[8,3,8,16,128]{4,3,2,1,0:T(8,128)} %m_ref.5) | copy-start | bytes 4718596
  4.6 19.8 %copy-start.15 = (bf16[128,144]{1,0:T(8,128)(2,1)S(1)}, bf16[128,144]{1,0:T(8,128)(2,1)}, u32[]{:S(2)}) copy-start(bf16[128,144]{1,0:T(8,128)(2,1)} %constant.50.clone.left_ref) | copy-start | bytes 110596
  4.6 19.8 %copy-start.17 = (bf16[72,384]{1,0:T(8,128)(2,1)S(1)}, bf16[72,384]{1,0:T(8,128)(2,1)}, u32[]{:S(2)}) copy-start(bf16[72,384]{1,0:T(8,128)(2,1)} %constant.51.clone.right_ref) | copy-start | bytes 165892
  4.6 19.8 %collective-permute-start = (f32[8,3,3,16,128]{4,3,2,1,0:T(8,128)S(1)}, f32[8,3,3,16,128]{4,3,2,1,0:T(8,128)S(1)}, u32[]{:S(2)}, u32[]{:S(2)}) collective-permute-start(f32[8,3,3,16,128]{4,3,2,1,0:T(8,128)S(1)} %shard_map.114), channel_id=1, source_target_pairs={{0,64},{64,0},{1,65},{65,1},{2,66},{66,2},{3,67},{67,3},{4,68},{68... | collective-permute-start | bytes 1769480 | tf_op jit(solution)/shard_map/ppermute | solution.py:414
  13.0 12.8 %copy-start.3 = (f32[8,3,8,16,128]{4,3,2,1,0:T(8,128)}, f32[8,3,8,16,128]{4,3,2,1,0:T(8,128)S(1)}, u32[]{:S(2)}) copy-start(f32[8,3,8,16,128]{4,3,2,1,0:T(8,128)S(1)} %get-tuple-element.9.local_ref) | copy-start | bytes 4718596
  13.0 10.9 %collective-permute-start.1 = (f32[8,3,3,8,128]{4,3,2,1,0:T(8,128)S(1)}, f32[8,3,3,8,128]{4,3,2,1,0:T(8,128)S(1)}, u32[]{:S(2)}, u32[]{:S(2)}) collective-permute-start(f32[8,3,3,8,128]{4,3,2,1,0:T(8,128)S(1)} %get-tuple-element.11), channel_id=1, source_target_pairs={{0,60},{4,0},{8,4},{12,8},{16,12},{20,16},{24,20},{28,24},{32,28},... | collective-permute-start | bytes 884744 | tf_op jit(solution)/shard_map/ppermute | solution.py:415
  14.1 9.9 %collective-permute-start.2 = (f32[8,3,3,8,128]{4,3,2,1,0:T(8,128)S(1)}, f32[8,3,3,8,128]{4,3,2,1,0:T(8,128)S(1)}, u32[]{:S(2)}, u32[]{:S(2)}) collective-permute-start(f32[8,3,3,8,128]{4,3,2,1,0:T(8,128)S(1)} %get-tuple-element.12), channel_id=1, source_target_pairs={{0,4},{4,8},{8,12},{12,16},{16,20},{20,24},{24,28},{28,32},{32,36}... | collective-permute-start | bytes 884744 | tf_op jit(solution)/shard_map/ppermute | solution.py:416
  15.2 5.4 %collective-permute-start.3 = (f32[8,3,8,128]{3,2,1,0:T(8,128)S(1)}, f32[8,3,8,128]{3,2,1,0:T(8,128)S(1)}, u32[]{:S(2)}, u32[]{:S(2)}) collective-permute-start(f32[8,3,8,128]{3,2,1,0:T(8,128)S(1)} %get-tuple-element.13), channel_id=1, source_target_pairs={{0,3},{1,0},{2,1},{3,2},{4,7},{5,4},{6,5},{7,6},{8,11},{9,8},{10,9... | collective-permute-start | bytes 294920 | tf_op jit(solution)/shard_map/ppermute | solution.py:417
  19.0 5.0 %collective-permute-start.4 = (f32[8,3,8,128]{3,2,1,0:T(8,128)S(1)}, f32[8,3,8,128]{3,2,1,0:T(8,128)S(1)}, u32[]{:S(2)}, u32[]{:S(2)}) collective-permute-start(f32[8,3,8,128]{3,2,1,0:T(8,128)S(1)} %get-tuple-element.13), channel_id=1, source_target_pairs={{0,1},{1,2},{2,3},{3,0},{4,5},{5,6},{6,7},{7,4},{8,9},{9,10},{10,1... | collective-permute-start | bytes 294920 | tf_op jit(solution)/shard_map/ppermute | solution.py:418
  24.0 1.8 %copy-start.13 = (f32[8,3,8,128]{3,2,1,0:T(8,128)}, f32[8,3,8,128]{3,2,1,0:T(8,128)S(1)}, u32[]{:S(2)}) copy-start(f32[8,3,8,128]{3,2,1,0:T(8,128)S(1)} %collective-permute-done.4.zdown_ref) | copy-start | bytes 294916
  24.0 1.8 %copy-start.9 = (f32[8,3,3,8,128]{4,3,2,1,0:T(8,128)}, f32[8,3,3,8,128]{4,3,2,1,0:T(8,128)S(1)}, u32[]{:S(2)}) copy-start(f32[8,3,3,8,128]{4,3,2,1,0:T(8,128)S(1)} %collective-permute-done.1.y0_ref) | copy-start | bytes 884740
  24.0 1.8 %copy-start.11 = (f32[8,3,3,8,128]{4,3,2,1,0:T(8,128)}, f32[8,3,3,8,128]{4,3,2,1,0:T(8,128)S(1)}, u32[]{:S(2)}) copy-start(f32[8,3,3,8,128]{4,3,2,1,0:T(8,128)S(1)} %collective-permute-done.2.y1_ref) | copy-start | bytes 884740
  24.4 1.4 %copy-start.7 = (f32[8,3,3,16,128]{4,3,2,1,0:T(8,128)}, f32[8,3,3,16,128]{4,3,2,1,0:T(8,128)S(1)}, u32[]{:S(2)}) copy-start(f32[8,3,3,16,128]{4,3,2,1,0:T(8,128)S(1)} %collective-permute-done.facing_ref) | copy-start | bytes 1769476
  25.8 1.4 %copy-start = (f32[4,8,9,16,128]{4,3,2,1,0:T(8,128)}, f32[4,8,9,16,128]{4,3,2,1,0:T(8,128)S(1)}, u32[]{:S(2)}) copy-start(f32[4,8,9,16,128]{4,3,2,1,0:T(8,128)S(1)} %shard_map.115) | copy-start | bytes 7077892
  27.2 39.1 %all-to-all-start = ((f32[288,16,128]{2,1,0:T(8,128)}), f32[288,16,128]{2,1,0:T(8,128)S(1)}, u32[]{:S(2)}, u32[]{:S(2)}) async-start(f32[288,16,128]{2,1,0:T(8,128)} %bitcast.9), calls=%async_computation | async-start | bytes 4718592 | tf_op jit(solution)/shard_map/all_to_all | solution.py:435
  35.7 1.7 %copy-start.4 = (f32[8,3,8,16,128]{4,3,2,1,0:T(8,128)S(1)}, f32[8,3,8,16,128]{4,3,2,1,0:T(8,128)}, u32[]{:S(2)}) copy-start(f32[8,3,8,16,128]{4,3,2,1,0:T(8,128)} %copy-done.3) | copy-start | bytes 4718596
  37.4 1.1 copy-start.8
  38.4 1.0 copy-start.10
  39.4 1.0 copy-start.12
  40.4 0.9 copy-start.14
  41.3 0.8 copy-start.16
  42.1 0.8 copy-start.18
  42.9 23.5 %copy-start.21 = (s32[2]{0:T(128)S(1)}, s32[2]{0:T(128)}, u32[]{:S(2)}) copy-start(s32[2]{0:T(128)} %shift_ref.1) | copy-start | bytes 28
  44.2 1.1 %copy-start.1 = (f32[8,3,8,16,128]{4,3,2,1,0:T(8,128)}, f32[8,3,8,16,128]{4,3,2,1,0:T(8,128)S(1)}, u32[]{:S(2)}) copy-start(f32[8,3,8,16,128]{4,3,2,1,0:T(8,128)S(1)} %shard_map.116.local_ref) | copy-start | bytes 4718596
  68.1 36.9 %copy-start.2 = (f32[8,3,8,16,128]{4,3,2,1,0:T(8,128)S(1)}, f32[8,3,8,16,128]{4,3,2,1,0:T(8,128)}, u32[]{:S(2)}) copy-start(f32[8,3,8,16,128]{4,3,2,1,0:T(8,128)} %copy-done.1) | copy-start | bytes 4718596

commit v6 on v5

--- a/solution.py
+++ b/solution.py
@@ -124,17 +124,19 @@
     return (jnp.cos(phase), jnp.sin(phase)), step % 2 == 0
 
 
-def face_sums(m_ref, v_ref, waves, along_x, high, out_ref):
-    pair, comps, cx, cy, cz = m_ref.shape
+def near_plane(high, j, cx):
+    return jnp.where(high, cx - 1 - j, j)
+
+
+def face_sums(field_of, flow, waves, along_x, high, out_ref):
+    pair = out_ref.shape[0]
     sign = jnp.where(high, 1.0, -1.0)
-    near = [jnp.where(high, cx - 1 - j, j) for j in range(3)]
-    flow = [[v_ref[c, x] for c in range(3)] for x in near]
     for i in range(pair):
         add_x = jnp.where(along_x, waves[i], 0.0)
         add_y = jnp.where(along_x, 0.0, waves[i])
         field, turn_y, turn_z = [], [], []
-        for x, (vx, vy, vz) in zip(near, flow):
-            mx, my, mz = [m_ref[i, c, x] for c in range(3)]
+        for j, (vx, vy, vz) in enumerate(flow):
+            mx, my, mz = [field_of(i, c, j) for c in range(3)]
             tx, ty = mx + add_x, my + add_y
             field.append((mx, my, mz))
             turn_y.append(sign * (vz * tx - vx * mz))
@@ -155,11 +157,27 @@
     return ref.at[pl.ds(step * PAIR, PAIR)]
 
 
-def facing_kernel(freq_ref, m_ref, v_ref, facing_ref, *, total_z):
-    @pl.loop(0, m_ref.shape[0] // PAIR)
-    def _(step):
-        waves, along_x = wave_pair(freq_ref, step, m_ref.shape[-1], total_z)
-        face_sums(block(m_ref, step), v_ref, waves, along_x, lax.axis_index("gx") == 0, block(facing_ref, step))
+def facing_kernel(freq_ref, m_ref, v_ref, facing_ref, field_ref, flow_ref, sems, *, total_z):
+    cx = m_ref.shape[2]
+    high = lax.axis_index("gx") == 0
+    first = jnp.where(high, cx - 3, 0)
+    steps = m_ref.shape[0] // PAIR
+    flow_copy = pltpu.make_async_copy(v_ref.at[:, pl.ds(first, 3)], flow_ref, sems.at[steps])
+    flow_copy.start()
+    copies = []
+    for step in range(steps):
+        at = pl.ds(step * PAIR, PAIR)
+        copies.append(pltpu.make_async_copy(m_ref.at[at, :, pl.ds(first, 3)], field_ref.at[at], sems.at[step]))
+        copies[-1].start()
+    near = [near_plane(high, j, 3) for j in range(3)]
+    waves = [wave_pair(freq_ref, step, m_ref.shape[-1], total_z) for step in range(steps)]
+    flow_copy.wait()
+    flow = [[flow_ref[c, x] for c in range(3)] for x in near]
+    for step in range(steps):
+        copies[step].wait()
+        mine = block(field_ref, step)
+        face_sums(lambda i, c, j: mine[i, c, near[j]], flow, waves[step][0], waves[step][1], high,
+                  block(facing_ref, step))
 
 
 def rates_kernel(freq_ref, m_ref, v_ref, left_ref, right_ref, face_ref, rate_ref, outer_ref, y0_ref, y1_ref, z_ref, *,
@@ -195,7 +213,10 @@
     pair, comps, cx, cy, cz = m_ref.shape
     cells = cx * cy
     waves, along_x = wave_pair(freq_ref, step, cz, total_z)
-    face_sums(m_ref, v_ref, waves, along_x, lax.axis_index("gx") == 1, outer_ref)
+    high = lax.axis_index("gx") == 1
+    near = [near_plane(high, j, cx) for j in range(3)]
+    flow = [[v_ref[c, x] for c in range(3)] for x in near]
+    face_sums(lambda i, c, j: m_ref[i, c, near[j]], flow, waves, along_x, high, outer_ref)
 
     def wide(parts):
         return jnp.concatenate(parts, 1)
@@ -380,6 +401,7 @@
 
 
 VMEM = pl.BlockSpec(memory_space=pltpu.VMEM)
+ANY = pl.BlockSpec(memory_space=pl.ANY)
 SMEM = pl.BlockSpec(memory_space=pltpu.SMEM)
 PARAMS = pltpu.CompilerParams(vmem_limit_bytes=32 * 1024 * 1024)
 
@@ -395,7 +417,10 @@
     facing = pl.pallas_call(
         functools.partial(facing_kernel, total_z=total_z),
         out_shape=struct(problems, *face),
-        in_specs=[SMEM, VMEM, VMEM], out_specs=VMEM, compiler_params=PARAMS,
+        in_specs=[SMEM, ANY, ANY], out_specs=VMEM,
+        compiler_params=pltpu.CompilerParams(vmem_limit_bytes=60 * 1024 * 1024),
+        scratch_shapes=[pltpu.VMEM((problems, comps, 3, cy, cz), F32), pltpu.VMEM((comps, 3, cy, cz), F32),
+                        pltpu.SemaphoreType.DMA((problems // PAIR + 1,))],
     )(freq_index, magnetic, velocity)
     weights = [jnp.asarray(np.concatenate(w, dim)) for w, dim in ((lefts, 1), (mains, 0), (faces, 1))]
     outs = (tile, face, edge, edge, side)

time: 108 us -> 107 us (level)
  Pallas kernels: 11.8 us -> 13.6 us
  local copies, waits for them, and re-layouts: 12.8 us -> 11.1 us
    pallas_call x1, Pallas kernels: 0.95 us -> 2.87 us  [on_device(): pl.pallas_call(functools.partial(facing_kernel, total_z=total_z), out_sha...]
    unnamed x50 -> x48, local copies, waits for them, and re-layouts: 11.4 us -> 9.64 us
  transfers between devices with their start and end apart: 6 -> 6, of which waited for: 4 -> 3; matrix products, arithmetic and copies ran while one was open for 1% -> 1% of each run, Pallas kernels for 5% -> 5%
where the time goes in v6:
time: 107 us; the launch traced here: 106 us
  blocking collectives  36.9 us (34%)
  waiting for transfers between devices  26 us (24%)
  starting transfers between devices  17.6 us (16%)
  Pallas kernels  13.6 us (13%)
  local copies, waits for them, and re-layouts  11.1 us (10%)
    all_to_all x1, blocking collectives, on_device(): lax.all_to_all(turned.reshape(nx * ny * 9, cy, cz), ('gx', 'gy'), 0, 0, t...  36.9 us
    all_to_all x1, waiting for transfers between devices, on_device(): lax.all_to_all(lines.reshape(nx * ny * 9, cy, cz), ('gx', 'gy'), 0, 0, ti...  21 us
    unnamed x48, local copies, waits for them, and re-layouts  9.64 us
    all_to_all x1, starting transfers between devices, on_device(): lax.all_to_all(lines.reshape(nx * ny * 9, cy, cz), ('gx', 'gy'), 0, 0, ti...  7.85 us
    pallas_call x1, Pallas kernels, on_device(): pl.pallas_call(functools.partial(rates_kernel, total_z=total_z), out_shap...  4.45 us
    ppermute x1, starting transfers between devices, on_device(): facing_in = lax.ppermute(facing, 'gx', swap)  3.82 us
    ppermute x1, starting transfers between devices, on_device(): z_up = lax.ppermute(z, 'gz', zdown)  3.76 us
    ppermute x1, waiting for transfers between devices, on_device(): z_down = lax.ppermute(z, 'gz', zup)  3.33 us
  transfers between devices with their start and end apart: 6, of which 3 were waited for; matrix products, arithmetic and copies ran while one was open for 1% of the time, Pallas kernels for 5%

profile of v6, /device:TPU:1, one launch (start us, length us, event | category | flops | bytes accessed | tf_op | source)
XLA Modules:
  0.0 106.1 jit_solution(9919904916986282832)
XLA Ops:
  0.6 0.0 copy-start.22
  0.6 0.0 copy-start.23
  0.7 2.9 %shard_map.114 = f32[8,3,3,16,128]{4,3,2,1,0:T(8,128)} custom-call(s32[2]{0:T(128)} %freq_ref.3, f32[8,3,8,16,128]{4,3,2,1,0:T(8,128)} %m_ref.5, f32[3,8,16,128]{3,2,1,0:T(8,128)} %v_ref.3), custom_call_target="tpu_custom_call" | custom-call | tf_op jit(solution)/shard_map/pallas_call | solution.py:417
  3.6 0.0 copy-start.14
  3.6 0.0 copy-start.16
  3.6 3.8 %collective-permute-start = (f32[8,3,3,16,128]{4,3,2,1,0:T(8,128)}, f32[8,3,3,16,128]{4,3,2,1,0:T(8,128)S(1)}, u32[]{:S(2)}, u32[]{:S(2)}) collective-permute-start(f32[8,3,3,16,128]{4,3,2,1,0:T(8,128)} %shard_map.114), channel_id=1, source_target_pairs={{0,64},{64,0},{1,65},{65,1},{2,66},{66,2},{3,67},{67,3},{4,68},{68... | collective-permute-start | bytes 1769480 | tf_op jit(solution)/shard_map/ppermute | solution.py:439
  7.4 0.0 copy-start.21
  7.4 1.2 %copy-done.21 = bf16[176,2688]{1,0:T(8,128)(2,1)S(1)} copy-done((bf16[176,2688]{1,0:T(8,128)(2,1)S(1)}, bf16[176,2688]{1,0:T(8,128)(2,1)}, u32[]{:S(2)}) %copy-start.21) | copy-done | bytes 946200
  8.6 4.4 %shard_map.113 = (f32[8,3,8,16,128]{4,3,2,1,0:T(8,128)S(1)}, f32[8,3,3,16,128]{4,3,2,1,0:T(8,128)S(1)}, f32[8,3,3,8,128]{4,3,2,1,0:T(8,128)S(1)}, f32[8,3,3,8,128]{4,3,2,1,0:T(8,128)S(1)}, f32[8,3,8,128]{3,2,1,0:T(8,128)S(1)}) custom-call(s32[2]{0:T(128)S(1)} %copy-done.19, f32[8,3,8,16,128]{4,3,2,1,0:T(8,128)S(1)} %copy-done.5, ...), custom_call_target="tpu_custom_call" | custom-call | flops 1073741824 | bytes 16777216 | tf_op jit(solution)/shard_map/pallas_call | solution.py:427
  13.1 1.0 collective-permute-start.1
  14.1 1.2 %collective-permute-start.2 = (f32[8,3,3,8,128]{4,3,2,1,0:T(8,128)S(1)}, f32[8,3,3,8,128]{4,3,2,1,0:T(8,128)S(1)}, u32[]{:S(2)}, u32[]{:S(2)}) collective-permute-start(f32[8,3,3,8,128]{4,3,2,1,0:T(8,128)S(1)} %get-tuple-element.12), channel_id=1, source_target_pairs={{0,4},{4,8},{8,12},{12,16},{16,20},{20,24},{24,28},{28,32},{32,36}... | collective-permute-start | bytes 884744 | tf_op jit(solution)/shard_map/ppermute | solution.py:441
  15.3 3.8 %collective-permute-start.3 = (f32[8,3,8,128]{3,2,1,0:T(8,128)S(1)}, f32[8,3,8,128]{3,2,1,0:T(8,128)S(1)}, u32[]{:S(2)}, u32[]{:S(2)}) collective-permute-start(f32[8,3,8,128]{3,2,1,0:T(8,128)S(1)} %get-tuple-element.13), channel_id=1, source_target_pairs={{0,3},{1,0},{2,1},{3,2},{4,7},{5,4},{6,5},{7,6},{8,11},{9,8},{10,9... | collective-permute-start | bytes 294920 | tf_op jit(solution)/shard_map/ppermute | solution.py:442
  19.1 1.6 %collective-permute-done.3.zup_ref = f32[8,3,8,128]{3,2,1,0:T(8,128)S(1)} collective-permute-done((f32[8,3,8,128]{3,2,1,0:T(8,128)S(1)}, f32[8,3,8,128]{3,2,1,0:T(8,128)S(1)}, u32[]{:S(2)}, u32[]{:S(2)}) %collective-permute-start.3) | collective-permute-done | bytes 98336 | tf_op jit(solution)/shard_map/ppermute | solution.py:442
  20.7 3.3 %collective-permute-done.4.zdown_ref = f32[8,3,8,128]{3,2,1,0:T(8,128)S(1)} collective-permute-done((f32[8,3,8,128]{3,2,1,0:T(8,128)S(1)}, f32[8,3,8,128]{3,2,1,0:T(8,128)S(1)}, u32[]{:S(2)}, u32[]{:S(2)}) %collective-permute-start.4) | collective-permute-done | bytes 98336 | tf_op jit(solution)/shard_map/ppermute | solution.py:443
  24.1 1.4 %shard_map.115 = f32[4,8,9,16,128]{4,3,2,1,0:T(8,128)S(1)} custom-call(f32[8,3,8,16,128]{4,3,2,1,0:T(8,128)S(1)} %copy-done.5, f32[8,3,8,16,128]{4,3,2,1,0:T(8,128)S(1)} %get-tuple-element.9.local_ref, f32[8,3,3,16,128]{4,3,2,1,0:T(8,128)S(1)} %collective-permute-done.facing_ref, f32[8,3,3,16,128]{4,3,2,1,0:T(8,128)S(1)} %get-tuple-element.10.outer_ref, ...), custom_call_target="tpu_custom_call" | custom-call | tf_op jit(solution)/shard_map/pallas_call | solution.py:446
  25.5 1.4 %copy-done = f32[4,8,9,16,128]{4,3,2,1,0:T(8,128)} copy-done((f32[4,8,9,16,128]{4,3,2,1,0:T(8,128)}, f32[4,8,9,16,128]{4,3,2,1,0:T(8,128)S(1)}, u32[]{:S(2)}) %copy-start) | copy-done | bytes 2359320
  26.9 7.8 %all-to-all-start = ((f32[288,16,128]{2,1,0:T(8,128)}), f32[288,16,128]{2,1,0:T(8,128)S(1)}, u32[]{:S(2)}, u32[]{:S(2)}) async-start(f32[288,16,128]{2,1,0:T(8,128)} %bitcast.9), calls=%async_computation | async-start | bytes 4718592 | tf_op jit(solution)/shard_map/all_to_all | solution.py:460
  34.8 1.4 %dynamic-slice_bitcast_fusion.table_ref = bf16[4,256,512]{2,1,0:T(8,128)(2,1)S(1)} fusion(bf16[4,4,256,512]{3,2,1,0:T(8,128)(2,1)} %constant.52.clone, s32[]{:T(128)S(6)} %select_n.10), kind=kLoop, calls=%fused_computation | loop fusion | bytes 2097156 | tf_op jit(solution)/shard_map/jit(dynamic_index_in_dim)/squeeze | solution.py:459
  36.3 0.3 copy-done.4
  36.5 1.1 %copy-done.7 = f32[8,3,3,16,128]{4,3,2,1,0:T(8,128)S(1)} copy-done((f32[8,3,3,16,128]{4,3,2,1,0:T(8,128)S(1)}, f32[8,3,3,16,128]{4,3,2,1,0:T(8,128)}, u32[]{:S(2)}) %copy-start.7) | copy-done | bytes 589848
  37.6 1.0 copy-done.9
  38.6 1.0 copy-done.11
  39.5 0.9 copy-done.13
  40.4 0.8 copy-done.15
  41.3 0.8 copy-done.17
  42.1 1.3 %shard_map.116.local_ref = f32[8,3,8,16,128]{4,3,2,1,0:T(8,128)S(1)} custom-call(f32[8,3,8,16,128]{4,3,2,1,0:T(8,128)S(1)} %copy-done.4, f32[8,3,3,16,128]{4,3,2,1,0:T(8,128)S(1)} %copy-done.7, f32[8,3,3,8,128]{4,3,2,1,0:T(8,128)S(1)} %copy-done.9, f32[8,3,3,8,128]{4,3,2,1,0:T(8,128)S(1)} %copy-done.11, f32[8,3,8,128]{3,2,1,0:T(8,128)S(1)} %collective-permute-done.3.zup_ref, ...), custom_call_target="tpu_custom_call" | custom-call | flops 268435456 | bytes 4194304 | tf_op jit(solution)/shard_map/pallas_call | solution.py:450
  43.4 0.0 copy-start.1
  43.4 1.1 %copy-done.1 = f32[8,3,8,16,128]{4,3,2,1,0:T(8,128)} copy-done((f32[8,3,8,16,128]{4,3,2,1,0:T(8,128)}, f32[8,3,8,16,128]{4,3,2,1,0:T(8,128)S(1)}, u32[]{:S(2)}) %copy-start.1) | copy-done | bytes 1572888
  44.5 21.0 %all-to-all-done = f32[288,16,128]{2,1,0:T(8,128)S(1)} async-done(((f32[288,16,128]{2,1,0:T(8,128)}), f32[288,16,128]{2,1,0:T(8,128)S(1)}, u32[]{:S(2)}, u32[]{:S(2)}) %all-to-all-start) | async-done | bytes 2359328 | tf_op jit(solution)/shard_map/all_to_all | solution.py:460
  65.6 1.7 %shard_map.117 = f32[2,16,9,16,128]{4,3,2,1,0:T(8,128)S(1)} custom-call(s32[2]{0:T(128)S(1)} %copy-done.20, f32[2,16,9,16,128]{4,3,2,1,0:T(8,128)S(1)} %bitcast.6, bf16[4,256,512]{2,1,0:T(8,128)(2,1)S(1)} %dynamic-slice_bitcast_fusion.table_ref), custom_call_target="tpu_custom_call" | custom-call | tf_op jit(solution)/shard_map/pallas_call | solution.py:462
  67.3 36.9 %all_to_all.10 = f32[288,16,128]{2,1,0:T(8,128)S(1)} all-to-all(f32[288,16,128]{2,1,0:T(8,128)S(1)} %bitcast.8), channel_id=1, replica_groups=mesh['gx'=2,'gy'=16,'gz'=4] {'gx','gy'}, dimensions={0} | all-to-all | bytes 4718592 | tf_op jit(solution)/shard_map/all_to_all | solution.py:466
  104.2 1.9 %shard_map.118 = (f32[8,3,8,16,128]{4,3,2,1,0:T(8,128)}, f32[8,3,8,16,128]{4,3,2,1,0:T(8,128)}) custom-call(f32[4,8,9,16,128]{4,3,2,1,0:T(8,128)S(1)} %bitcast.7, f32[8,3,8,16,128]{4,3,2,1,0:T(8,128)S(1)} %copy-done.2), custom_call_target="tpu_custom_call" | custom-call | tf_op jit(solution)/shard_map/pallas_call | solution.py:467
  (36 shorter events, 0.1 us)
Async XLA Ops:
  0.6 6.8 %copy-start.22 = (bf16[1920,128]{1,0:T(8,128)(2,1)S(1)}, bf16[1920,128]{1,0:T(8,128)(2,1)}, u32[]{:S(2)}) copy-start(bf16[1920,128]{1,0:T(8,128)(2,1)} %constant.48.clone.right_ref) | copy-start | bytes 1474564
  0.6 6.8 %copy-start.23 = (bf16[8,1920]{1,0:T(8,128)(2,1)S(1)}, bf16[8,1920]{1,0:T(8,128)(2,1)}, u32[]{:S(2)}) copy-start(bf16[8,1920]{1,0:T(8,128)(2,1)} %constant.49.clone.face_ref) | copy-start | bytes 92164
  0.7 6.8 %copy-start.5 = (f32[8,3,8,16,128]{4,3,2,1,0:T(8,128)S(1)}, f32[8,3,8,16,128]{4,3,2,1,0:T(8,128)}, u32[]{:S(2)}) copy-start(f32[8,3,8,16,128]{4,3,2,1,0:T(8,128)} %m_ref.5) | copy-start | bytes 4718596
  0.7 6.8 %copy-start.19 = (s32[2]{0:T(128)S(1)}, s32[2]{0:T(128)}, u32[]{:S(2)}) copy-start(s32[2]{0:T(128)} %freq_ref.3) | copy-start | bytes 28
  0.7 6.8 %copy-start.18 = (f32[3,8,16,128]{3,2,1,0:T(8,128)S(1)}, f32[3,8,16,128]{3,2,1,0:T(8,128)}, u32[]{:S(2)}) copy-start(f32[3,8,16,128]{3,2,1,0:T(8,128)} %v_ref.3) | copy-start | bytes 589828
  3.6 20.5 %copy-start.14 = (bf16[128,144]{1,0:T(8,128)(2,1)S(1)}, bf16[128,144]{1,0:T(8,128)(2,1)}, u32[]{:S(2)}) copy-start(bf16[128,144]{1,0:T(8,128)(2,1)} %constant.50.clone.left_ref) | copy-start | bytes 110596
  3.6 20.5 %copy-start.16 = (bf16[72,384]{1,0:T(8,128)(2,1)S(1)}, bf16[72,384]{1,0:T(8,128)(2,1)}, u32[]{:S(2)}) copy-start(bf16[72,384]{1,0:T(8,128)(2,1)} %constant.51.clone.right_ref) | copy-start | bytes 165892
  3.6 20.5 %collective-permute-start = (f32[8,3,3,16,128]{4,3,2,1,0:T(8,128)}, f32[8,3,3,16,128]{4,3,2,1,0:T(8,128)S(1)}, u32[]{:S(2)}, u32[]{:S(2)}) collective-permute-start(f32[8,3,3,16,128]{4,3,2,1,0:T(8,128)} %shard_map.114), channel_id=1, source_target_pairs={{0,64},{64,0},{1,65},{65,1},{2,66},{66,2},{3,67},{67,3},{4,68},{68... | collective-permute-start | bytes 1769480 | tf_op jit(solution)/shard_map/ppermute | solution.py:439
  7.4 1.2 %copy-start.21 = (bf16[176,2688]{1,0:T(8,128)(2,1)S(1)}, bf16[176,2688]{1,0:T(8,128)(2,1)}, u32[]{:S(2)}) copy-start(bf16[176,2688]{1,0:T(8,128)(2,1)} %constant.47.clone.left_ref) | copy-start | bytes 2838532
  13.1 12.4 %copy-start.3 = (f32[8,3,8,16,128]{4,3,2,1,0:T(8,128)}, f32[8,3,8,16,128]{4,3,2,1,0:T(8,128)S(1)}, u32[]{:S(2)}) copy-start(f32[8,3,8,16,128]{4,3,2,1,0:T(8,128)S(1)} %get-tuple-element.9.local_ref) | copy-start | bytes 4718596
  13.1 10.9 %collective-permute-start.1 = (f32[8,3,3,8,128]{4,3,2,1,0:T(8,128)S(1)}, f32[8,3,3,8,128]{4,3,2,1,0:T(8,128)S(1)}, u32[]{:S(2)}, u32[]{:S(2)}) collective-permute-start(f32[8,3,3,8,128]{4,3,2,1,0:T(8,128)S(1)} %get-tuple-element.11), channel_id=1, source_target_pairs={{0,60},{4,0},{8,4},{12,8},{16,12},{20,16},{24,20},{28,24},{32,28},... | collective-permute-start | bytes 884744 | tf_op jit(solution)/shard_map/ppermute | solution.py:440
  14.1 9.9 %collective-permute-start.2 = (f32[8,3,3,8,128]{4,3,2,1,0:T(8,128)S(1)}, f32[8,3,3,8,128]{4,3,2,1,0:T(8,128)S(1)}, u32[]{:S(2)}, u32[]{:S(2)}) collective-permute-start(f32[8,3,3,8,128]{4,3,2,1,0:T(8,128)S(1)} %get-tuple-element.12), channel_id=1, source_target_pairs={{0,4},{4,8},{8,12},{12,16},{16,20},{20,24},{24,28},{28,32},{32,36}... | collective-permute-start | bytes 884744 | tf_op jit(solution)/shard_map/ppermute | solution.py:441
  15.3 5.4 %collective-permute-start.3 = (f32[8,3,8,128]{3,2,1,0:T(8,128)S(1)}, f32[8,3,8,128]{3,2,1,0:T(8,128)S(1)}, u32[]{:S(2)}, u32[]{:S(2)}) collective-permute-start(f32[8,3,8,128]{3,2,1,0:T(8,128)S(1)} %get-tuple-element.13), channel_id=1, source_target_pairs={{0,3},{1,0},{2,1},{3,2},{4,7},{5,4},{6,5},{7,6},{8,11},{9,8},{10,9... | collective-permute-start | bytes 294920 | tf_op jit(solution)/shard_map/ppermute | solution.py:442
  19.1 5.0 %collective-permute-start.4 = (f32[8,3,8,128]{3,2,1,0:T(8,128)S(1)}, f32[8,3,8,128]{3,2,1,0:T(8,128)S(1)}, u32[]{:S(2)}, u32[]{:S(2)}) collective-permute-start(f32[8,3,8,128]{3,2,1,0:T(8,128)S(1)} %get-tuple-element.13), channel_id=1, source_target_pairs={{0,1},{1,2},{2,3},{3,0},{4,5},{5,6},{6,7},{7,4},{8,9},{9,10},{10,1... | collective-permute-start | bytes 294920 | tf_op jit(solution)/shard_map/ppermute | solution.py:443
  24.0 1.5 %copy-start.12 = (f32[8,3,8,128]{3,2,1,0:T(8,128)}, f32[8,3,8,128]{3,2,1,0:T(8,128)S(1)}, u32[]{:S(2)}) copy-start(f32[8,3,8,128]{3,2,1,0:T(8,128)S(1)} %collective-permute-done.4.zdown_ref) | copy-start | bytes 294916
  24.0 1.5 %copy-start.8 = (f32[8,3,3,8,128]{4,3,2,1,0:T(8,128)}, f32[8,3,3,8,128]{4,3,2,1,0:T(8,128)S(1)}, u32[]{:S(2)}) copy-start(f32[8,3,3,8,128]{4,3,2,1,0:T(8,128)S(1)} %collective-permute-done.1.y0_ref) | copy-start | bytes 884740
  24.0 1.5 %copy-start.10 = (f32[8,3,3,8,128]{4,3,2,1,0:T(8,128)}, f32[8,3,3,8,128]{4,3,2,1,0:T(8,128)S(1)}, u32[]{:S(2)}) copy-start(f32[8,3,3,8,128]{4,3,2,1,0:T(8,128)S(1)} %collective-permute-done.2.y1_ref) | copy-start | bytes 884740
  24.1 1.5 %copy-start.6 = (f32[8,3,3,16,128]{4,3,2,1,0:T(8,128)}, f32[8,3,3,16,128]{4,3,2,1,0:T(8,128)S(1)}, u32[]{:S(2)}) copy-start(f32[8,3,3,16,128]{4,3,2,1,0:T(8,128)S(1)} %collective-permute-done.facing_ref) | copy-start | bytes 1769476
  25.5 1.4 %copy-start = (f32[4,8,9,16,128]{4,3,2,1,0:T(8,128)}, f32[4,8,9,16,128]{4,3,2,1,0:T(8,128)S(1)}, u32[]{:S(2)}) copy-start(f32[4,8,9,16,128]{4,3,2,1,0:T(8,128)S(1)} %shard_map.115) | copy-start | bytes 7077892
  26.9 38.6 %all-to-all-start = ((f32[288,16,128]{2,1,0:T(8,128)}), f32[288,16,128]{2,1,0:T(8,128)S(1)}, u32[]{:S(2)}, u32[]{:S(2)}) async-start(f32[288,16,128]{2,1,0:T(8,128)} %bitcast.9), calls=%async_computation | async-start | bytes 4718592 | tf_op jit(solution)/shard_map/all_to_all | solution.py:460
  34.8 1.7 %copy-start.4 = (f32[8,3,8,16,128]{4,3,2,1,0:T(8,128)S(1)}, f32[8,3,8,16,128]{4,3,2,1,0:T(8,128)}, u32[]{:S(2)}) copy-start(f32[8,3,8,16,128]{4,3,2,1,0:T(8,128)} %copy-done.3) | copy-start | bytes 4718596
  36.5 1.1 %copy-start.7 = (f32[8,3,3,16,128]{4,3,2,1,0:T(8,128)S(1)}, f32[8,3,3,16,128]{4,3,2,1,0:T(8,128)}, u32[]{:S(2)}) copy-start(f32[8,3,3,16,128]{4,3,2,1,0:T(8,128)} %copy-done.6) | copy-start | bytes 1769476
  37.6 1.0 copy-start.9
  38.6 1.0 copy-start.11
  39.5 0.9 copy-start.13
  40.4 0.8 copy-start.15
  41.3 0.8 copy-start.17
  42.1 23.5 %copy-start.20 = (s32[2]{0:T(128)S(1)}, s32[2]{0:T(128)}, u32[]{:S(2)}) copy-start(s32[2]{0:T(128)} %shift_ref.1) | copy-start | bytes 28
  43.4 1.1 %copy-start.1 = (f32[8,3,8,16,128]{4,3,2,1,0:T(8,128)}, f32[8,3,8,16,128]{4,3,2,1,0:T(8,128)S(1)}, u32[]{:S(2)}) copy-start(f32[8,3,8,16,128]{4,3,2,1,0:T(8,128)S(1)} %shard_map.116.local_ref) | copy-start | bytes 4718596
  67.2 36.9 %copy-start.2 = (f32[8,3,8,16,128]{4,3,2,1,0:T(8,128)S(1)}, f32[8,3,8,16,128]{4,3,2,1,0:T(8,128)}, u32[]{:S(2)}) copy-start(f32[8,3,8,16,128]{4,3,2,1,0:T(8,128)} %copy-done.1) | copy-start | bytes 4718596
